TPU v7x, 32 devices: a whole 2x2x4 slice. The times are simulated.
32 devices in a mesh: dom: 16 (over z, x, core), feat: 2 (over y).
Axes of the slice: x: 2, y: 2, z: 4, core: 2. Of those that a mesh axis runs over, the one named last changes fastest.
Arguments:
- fine_latent: bfloat16 [256, 262144], P('feat', 'dom'), may hold values from -6 to 6
- coarse_latent: bfloat16 [256, 131072], P('feat', 'dom'), may hold values from -6 to 6
- parents: int32 [4, 262144], P(None, 'dom'), may hold values from 0 to 24575, as said below
- interp_weights: float32 [4, 262144], P(None, 'dom'), may hold values from 0.1 to 1
- live_rows: int32 [16], P('dom'), may hold values from 8192 to 16384, as said below
- w_fine: bfloat16 [256, 256], replicated, may hold values from -0.25 to 0.25
- w_parent: bfloat16 [256, 256], replicated, may hold values from -0.25 to 0.25
- w_edge_out: bfloat16 [256, 256], replicated, may hold values from -0.375 to 0.375
- w_node_fine: bfloat16 [256, 256], replicated, may hold values from -0.25 to 0.25
- w_node_agg: bfloat16 [256, 256], replicated, may hold values from -0.25 to 0.25
- w_node_out: bfloat16 [256, 256], replicated, may hold values from -0.375 to 0.375
- edge_bias: float32 [256], replicated, may hold values from -3 to 3
- node_bias: float32 [256], replicated, may hold values from -3 to 3
- norm_gain: float32 [256], replicated, may hold values from 0.1 to 1.9
- norm_bias: float32 [256], replicated, may hold values from -2 to 2
Outputs:
- fine_out: bfloat16 [256, 262144], P('feat', 'dom')
Inputs may be any that keep to these rules, and one draw needn't show every extreme that they name: `parents`: a parent slot s of a fine node of block b names coarse node (b - 1) * 8192 + s, block b holding coarse nodes b * 8192 to (b + 1) * 8192 - 1; slots of block 0 are at least 8192, slots of the last block under 2 * 8192. `live_rows`: fine node slots of a block at or beyond its count are padding; at least one block is full.
All inputs are finite; a program needn't handle non-finite values.
Results may differ from a plain program's by a relative error of at most 0.0042.
Values may be sent and summed in bfloat16 or wider, within the bound.
No kernel may reach another device: no remote copies, remote signals or barrier semaphores. Data moves between devices by JAX's collectives and lax.ppermute only.
A program may use at most 128 MiB of HBM per device.

v0:
```python
import functools

import jax
import jax.numpy as jnp
from jax import lax
from jax.experimental import pallas as pl
from jax.experimental.pallas import tpu as pltpu
from jax.sharding import PartitionSpec as P

F32 = jnp.float32
BF16 = jnp.bfloat16
PAD = 8
SHARE = 4
PARTS = 1
STEP = 256
GROUPS = 13


def dot(a, b, ca, cb):
    return lax.dot_general(a, b, (((ca,), (cb,)), ((), ())), preferred_element_type=F32)


def fill_table(segments, step, places, refs, weight, table, landed, sems):
    rows = (table.shape[0] - 2 * PAD) // 6
    features = landed.shape[2] // sems.shape[2]
    table[pl.ds(0, PAD), :] = jnp.zeros((PAD, 128), F32)
    table[pl.ds(PAD + 6 * rows, PAD), :] = jnp.zeros((PAD, 128), F32)

    def copies(segment, i, slot, which):
        found = []
        for p, (sources, first) in enumerate(segments[segment][3]):
            at = pl.multiple_of(first + i * step, 128)
            found.append(
                pltpu.make_async_copy(
                    refs[sources[min(which, len(sources) - 1)]].at[:, pl.ds(at, step)],
                    landed.at[segment % 2, slot, pl.ds(p * features, features), :],
                    sems.at[segment % 2, slot, p],
                )
            )
        return found

    def start(segment, i, slot):
        if all(len(sources) == 1 for sources, _ in segments[segment][3]):
            for copy in copies(segment, i, slot, 0):
                copy.start()
            return
        for which in range(2):

            @pl.when(places[3] == which)
            def _(which=which):
                for copy in copies(segment, i, slot, which):
                    copy.start()

    start(0, 0, 0)
    for segment, (window, row, length, _) in enumerate(segments):
        steps = length // step
        if segment + 1 < len(segments):
            start(segment + 1, 0, 0)

        def one(i, carry, segment=segment, window=window, row=row, steps=steps):
            slot = lax.rem(i, 2)

            @pl.when(i + 1 < steps)
            def _():
                start(segment, i + 1, 1 - slot)

            for copy in copies(segment, i, slot, 0):
                copy.wait()
            projected = dot(landed[segment % 2, slot], weight[...], 0, 0)
            base = pl.multiple_of(PAD + 2 * (places[window] * rows + row + i * step), 8)
            table[pl.ds(base, step, stride=2), :] = projected[:, :128]
            table[pl.ds(base + 1, step, stride=2), :] = projected[:, 128:]
            return carry

        lax.fori_loop(0, steps, one, 0)


def update_kernel(sources, step, start, segments, table_step, places, aux, *refs):
    count = len(sources)
    given = 1 + max(at for source in sources for at, _ in source)
    arrays, refs = refs[:given], refs[given:]
    given, refs = refs[:8], refs[8:]
    held_here, refs = refs[-8:], refs[:-8]
    scales, w_latent, w_edge, w_agg, w_out_t, bias, gain, shift = held_here
    table, latents, fine, total, earlier, later, scale_rows, slots, live, sems, given_sems = refs[-11:]
    refs = refs[:-11]
    fetches = [
        pltpu.make_async_copy(far if at else far.at[:, pl.ds(start, near.shape[1])], near, given_sems.at[at])
        for at, (far, near) in enumerate(zip(given, held_here))
    ]
    features, nodes = latents.shape[0] // count, latents.shape[1]
    parents = slots.shape[0] // nodes
    if segments is None:
        kept, outs = refs[0], refs[1:]
        move = pltpu.make_async_copy(kept, table, sems.at[parents + 1 + count])
        move.start()
    else:
        w_parent, *coarse = refs[: -count - 3]
        *outs, kept, landed, landed_sems = refs[-count - 3 :]
        move = pltpu.make_async_copy(table, kept, sems.at[parents + 1 + count])
    held = aux.shape[0] // (parents + 1)
    fetches.append(pltpu.make_async_copy(aux.at[pl.ds(parents * start, parents * nodes)], slots, sems.at[0]))
    fetches.append(pltpu.make_async_copy(aux.at[pl.ds(parents * held, 1024)], live, sems.at[parents]))
    for fetch in fetches:
        fetch.start()

    def bring(p, which):
        at, shifted = sources[p][min(which, len(sources[p]) - 1)]
        column = arrays[at].shape[1] - nodes if shifted is None else pl.multiple_of(places[4] + start, 128)
        return pltpu.make_async_copy(
            arrays[at].at[:, pl.ds(column, nodes)],
            latents.at[pl.ds(p * features, features), :],
            sems.at[parents + 1 + p],
        )

    for p, source in enumerate(sources):
        for which in range(len(source)):

            @pl.when((places[3] == which) | (len(source) == 1))
            def _(p=p, which=which):
                bring(p, which).start()

    if segments is not None:
        fill_table(segments, table_step, places, coarse, w_parent, table, landed, landed_sems)
        move.start()
    for fetch in fetches:
        fetch.wait()
    for p in range(count):
        bring(p, 0).wait()
    if segments is None:
        move.wait()
    sublane = lax.broadcasted_iota(jnp.int32, (8, 128), 0)
    owns = [sublane >= 2 * j for j in range(4)]

    def begin(i):
        columns = pl.ds(pl.multiple_of(i * step, step), step)
        first = dot(latents[:, columns], w_latent[...], 0, 0) + bias[...]
        return first, scales[:, pl.ds(pl.multiple_of(i * step, step), step)].T

    def keep(first, scale_columns):
        width = first.shape[1] // 2
        fine[pl.ds(0, step, stride=2), :] = first[:, :128]
        fine[pl.ds(1, step, stride=2), :] = first[:, 128:width]
        later[...] = first[:, width:]
        scale_rows[pl.ds(0, step, stride=2), :] = scale_columns
        scale_rows[pl.ds(1, step, stride=2), :] = scale_columns

    def group(at, g):
        part = fine[pl.ds(g * 8, 8), :]
        scale = scale_rows[pl.ds(g * 8, 8), :]
        acc = None
        for k in range(parents):
            rows = None
            for j in range(4):
                loaded = table[pl.ds(slots[at + (k * step + g * 4 + j)], 8), :]
                rows = loaded if rows is None else jnp.where(owns[j], loaded, rows)
            hidden = jnp.maximum(part + rows, 0.0) * scale[:, k : k + 1]
            acc = hidden if acc is None else acc + hidden
        return acc

    def widened(ref):
        return jnp.concatenate([ref[...]] * (step // 128), axis=1)

    def finish(i, summed, own_part):
        at = pl.multiple_of(i * step, step)
        aggregate = dot(summed.astype(BF16), w_edge[...], 1, 0).astype(BF16)
        yield
        node_hidden = jnp.maximum(own_part + dot(aggregate, w_agg[...], 1, 0), 0.0).astype(BF16)
        yield
        output = dot(w_out_t[...], node_hidden, 1, 1)
        yield
        centered = output - jnp.mean(output, axis=0, keepdims=True)
        spread = jnp.mean(centered * centered, axis=0, keepdims=True)
        yield
        normed = centered * lax.rsqrt(spread + 1e-05) * widened(gain) + widened(shift)
        column = start + at + lax.broadcasted_iota(jnp.int32, (1, step), 1)
        moved = jnp.where(column < live[0], normed, 0.0)
        yield (latents[:, pl.ds(at, step)].astype(F32) + moved).astype(BF16)

    def last(parts):
        for value in parts:
            pass
        return value

    def write(i, result):
        for r in range(count):
            outs[r][:, pl.ds(pl.multiple_of(i * step, step), step)] = result[r * features : (r + 1) * features]

    def gathered():
        return jnp.concatenate([total[pl.ds(0, step, stride=2), :], total[pl.ds(1, step, stride=2), :]], axis=1)

    steps = nodes // step
    keep(*begin(0))

    def one_step(i, carry):
        before, after = jnp.maximum(i - 1, 0), jnp.minimum(i + 1, steps - 1)
        summed, own_part, current = gathered(), earlier[...], later[...]
        parts = finish(before, summed, own_part)
        base = pl.multiple_of(i * (parents * step), parents * step)
        begun = begin(after)
        for first in range(0, step // 4, GROUPS):
            result = next(parts, None) if first < 4 * GROUPS else last(parts)
            sums = [group(base, g) for g in range(first, min(first + GROUPS, step // 4))]
            total[pl.ds(first * 8, len(sums) * 8), :] = jnp.concatenate(sums, axis=0)
        write(before, result)
        earlier[...] = current
        keep(*begun)
        return carry

    lax.fori_loop(0, steps, one_step, 0)
    write(steps - 1, last(finish(steps - 1, gathered(), earlier[...])))
    if segments is not None:
        move.wait()


def by_step(aux, step):
    slots = aux[:-1].reshape(aux.shape[0] - 1, -1, step).transpose(1, 0, 2)
    return jnp.concatenate([slots.reshape(-1), aux[-1]])


def update(
    start, nodes, aux, arrays, sources, scales, params, places, table=None, segments=None, w_parent=None, coarse=()
):
    count, features = len(sources), arrays[0].shape[0]
    parents = aux.shape[0] - 1
    step = min(STEP, nodes)
    vmem = pl.BlockSpec(memory_space=pltpu.VMEM)
    smem = pl.BlockSpec(memory_space=pltpu.SMEM)
    far = pl.BlockSpec(memory_space=pltpu.HBM)
    out_shape = [jax.ShapeDtypeStruct((features, nodes), BF16)] * count
    operands = [places, by_step(aux, step), *arrays, scales, *params]
    specs = [smem, far] + [far] * (len(arrays) + 1 + len(params))
    scratch, table_step = [], 0
    if segments is None:
        operands, specs = operands + [table], specs + [far]
    else:
        operands, specs = operands + [w_parent, *coarse], specs + [vmem] + [far] * len(coarse)
        table_step = min(2048, segments[0][2])
        table = jax.ShapeDtypeStruct((2 * sum(segment[2] for segment in segments) + 2 * PAD, 128), F32)
        out_shape.append(table)
        scratch = [
            pltpu.VMEM((2, 2, w_parent.shape[0], table_step), BF16),
            pltpu.SemaphoreType.DMA((2, 2, len(segments[0][3]))),
        ]
    return pl.pallas_call(
        functools.partial(update_kernel, sources, step, start, segments, table_step),
        out_shape=out_shape,
        in_specs=specs,
        out_specs=[vmem] * count + [far] * (len(out_shape) - count),
        scratch_shapes=scratch
        + [
            pltpu.VMEM(table.shape, F32),
            pltpu.VMEM((count * features, nodes), BF16),
            pltpu.VMEM((2 * step, 128), F32),
            pltpu.VMEM((2 * step, 128), F32),
            pltpu.VMEM((step, 256), F32),
            pltpu.VMEM((step, 256), F32),
            pltpu.VMEM((2 * step, 8), F32),
            pltpu.SMEM((parents * nodes,), jnp.int32),
            pltpu.SMEM((1024,), jnp.int32),
            pltpu.SemaphoreType.DMA((parents + 2 + count,)),
            pltpu.SemaphoreType.DMA((1 + len(params),)),
            pltpu.VMEM((scales.shape[0], nodes), F32),
        ]
        + [pltpu.VMEM(param.shape, param.dtype) for param in params],
        compiler_params=pltpu.CompilerParams(vmem_limit_bytes=40 << 20),
        cost_estimate=pl.CostEstimate(flops=nodes * 700000, bytes_accessed=nodes * 2048, transcendentals=nodes),
    )(*operands)


def after(value, *others):
    return lax.optimization_barrier((value, *others))[0]


def shares(nodes):
    first = nodes * SHARE // 8 // STEP * STEP
    return [(0, first), (first, nodes - first)]


def cut(array, at, size):
    return lax.dynamic_slice_in_dim(array, at, size, 1)


def plain(fine_latent, coarse_latent, aux, weights, w_parent, run):
    groups, domains = lax.axis_size("feat"), lax.axis_size("dom")
    rank = lax.axis_index("feat")
    per_device = fine_latent.shape[1] // groups
    forward = [(i, i + 1) for i in range(domains - 1)]
    backward = [(i + 1, i) for i in range(domains - 1)]

    def turn(value, r):
        return lax.ppermute(value, "feat", [(i, (i + r) % groups) for i in range(groups)])

    own = [coarse_latent] + [turn(coarse_latent, r) for r in range(1, groups)]
    low = [lax.ppermute(piece, "dom", forward) for piece in own]
    high = [lax.ppermute(piece, "dom", backward) for piece in own]
    first_row = rank * per_device
    rows = coarse_latent.shape[1]
    segments = [
        (w, 0, rows, [((w * groups + p,), 0) for p in range(groups)]) for w in range(3)
    ]
    making = dict(segments=segments, w_parent=w_parent, coarse=low + own + high)
    places = jnp.stack([0, 1, 2, 0, first_row]).astype(jnp.int32)
    sources = [((0, 0),)] + [((r, None),) for r in range(1, groups)]
    aux = cut(aux, first_row, per_device)
    aux = jnp.concatenate([aux[:-1], aux[-1:] - first_row])
    weights = cut(weights, first_row, per_device)
    result = fine_latent
    arrived = []
    for c, (start, length) in enumerate(shares(per_device)):
        pieces = [fine_latent]
        for r in range(1, groups):
            part = cut(fine_latent, ((rank + r) % groups) * per_device + start, length)
            pieces.append(turn(after(part, own[-1]), r))
        outs = run(start, length, aux, pieces, sources, weights, places, **(making if c == 0 else dict(table=table)))
        table = outs[-1] if c == 0 else table
        result = lax.dynamic_update_slice_in_dim(result, outs[0], first_row + start, 1)
        for r in range(1, groups):
            arrived.append((turn(outs[r], -r), ((rank + r) % groups) * per_device + start))
    for part, at in arrived:
        result = lax.dynamic_update_slice_in_dim(result, part, at, 1)
    return result


def paired(fine_latent, coarse_latent, aux, weights, w_parent, run):
    domains = lax.axis_size("dom")
    side, rank = lax.axis_index("dom") % 2, lax.axis_index("feat")
    matched = side == rank
    pairs = range(domains // 2)

    def send(value, moves):
        perm = [((2 * c + a) * 2 + b, (2 * c + x) * 2 + y) for c in pairs for (a, b), (x, y) in moves]
        return lax.ppermute(value, ("dom", "feat"), perm)

    def swap_rank(value):
        return send(value, [((k, f), (k, 1 - f)) for k in range(2) for f in range(2)])

    def swap_side(value):
        return send(value, [((k, f), (1 - k, f)) for k in range(2) for f in range(2)])

    def halo(value):
        perm = [((2 * c - 1) * 2, (2 * c) * 2) for c in pairs if c > 0]
        perm += [((2 * c + 2) * 2 + 1, (2 * c + 1) * 2 + 1) for c in pairs if c + 1 < len(pairs)]
        return lax.ppermute(value, ("dom", "feat"), perm)

    def hand_over(value):
        return send(value, [((0, 0), (1, 0)), ((1, 1), (0, 1))])

    to_first = [((0, 0), (1, 0)), ((1, 1), (0, 1)), ((0, 1), (0, 0)), ((1, 0), (1, 1))]
    from_first = [(b, a) for a, b in to_first]
    to_second = [((0, 1), (1, 0)), ((1, 0), (0, 1))]

    half = fine_latent.shape[1] // 2
    mine = side * half
    rows = coarse_latent.shape[1]
    part = rows // PARTS
    mate = []
    for i in range(PARTS):
        piece = lax.slice_in_dim(coarse_latent, i * part, (i + 1) * part, axis=1)
        mate.append(swap_rank(after(piece, mate[-1]) if mate else piece))
    halo_own, other = halo(coarse_latent), swap_side(after(coarse_latent, mate[-1]))
    halo_mate, other_mate = [halo(piece) for piece in mate], [swap_side(piece) for piece in mate]
    passed_own, passed_mate = hand_over(halo_own), [hand_over(piece) for piece in halo_mate]
    coarse = [coarse_latent, other, halo_own, passed_own, *mate, *other_mate, *halo_mate, *passed_mate]
    segments = []
    for window, own in enumerate([(0,), (1,), (2, 3)]):
        for i in range(PARTS):
            came = tuple(4 + (w + window) * PARTS + i for w in range(len(own)))
            segments.append((window, i * part, part, [(own, i * part), (came, 0)]))
    places = jnp.stack([side + 1 - rank, 2 - side - rank, 2 * rank, jnp.where(matched, 0, 1), mine])
    places = places.astype(jnp.int32)

    chunks = []
    for start, length in shares(half):
        extra = max(half // 2 - length, 0)
        first = cut(fine_latent, jnp.where(matched, half - mine, mine) + start - extra, length + extra)
        second = cut(fine_latent, half - mine + start - extra, length + extra)
        first, second = send(after(first, mate[-1]), to_first), send(after(second, mate[-1]), to_second)
        chunks.append([first, fine_latent, second])

    both = jnp.concatenate([aux.astype(F32), weights])
    both = jnp.where(matched, cut(both, mine, half), hand_over(cut(both, half - mine, half)))
    aux, weights = both[: aux.shape[0]].astype(jnp.int32), both[aux.shape[0] :]
    aux = jnp.concatenate([aux[:-1], aux[-1:] - mine])

    making = dict(segments=segments, w_parent=w_parent, coarse=coarse)
    sources = [((0, None),), ((1, 0), (2, None))]
    result = jnp.zeros_like(fine_latent)
    moved = []
    for c, (start, length) in enumerate(shares(half)):
        out, kept, *made = run(
            start, length, aux, chunks[c], sources, weights, places, **(making if c == 0 else dict(table=table))
        )
        table = made[0] if made else table
        moved.append((start, kept, send(out, from_first), send(kept, to_second)))
    for start, kept, first, second in moved:
        result = lax.dynamic_update_slice_in_dim(result, jnp.where(matched, kept, first), mine + start, 1)
        result = lax.dynamic_update_slice_in_dim(
            result, jnp.where(matched, first, second), half - mine + start, 1
        )
    return result


def shards(
    fine_latent,
    coarse_latent,
    parents,
    interp_weights,
    live_rows,
    w_fine,
    w_parent,
    w_edge_out,
    w_node_fine,
    w_node_agg,
    w_node_out,
    edge_bias,
    node_bias,
    norm_gain,
    norm_bias,
):
    groups, domains = lax.axis_size("feat"), lax.axis_size("dom")
    rank = lax.axis_index("feat")
    own_features = fine_latent.shape[0]
    owners = [(rank - r) % groups for r in range(groups)]
    pairing = groups == 2 and domains % 2 == 0
    flip = jnp.where(lax.axis_index("dom") % 2 == rank, 1, 0) if pairing else 0

    def ordered(weight, axis, flip=flip):
        parts = [lax.dynamic_slice_in_dim(weight, o * own_features, own_features, axis) for o in owners]
        if pairing:
            parts = [jnp.where(flip == 1, parts[1], parts[0]), jnp.where(flip == 1, parts[0], parts[1])]
        return jnp.concatenate(parts, axis=axis)

    params = (
        jnp.concatenate([ordered(w_fine, 0), ordered(w_node_fine, 0)], axis=1),
        w_edge_out,
        w_node_agg,
        ordered(w_node_out, 1).T,
        jnp.concatenate([edge_bias, node_bias])[None],
        jnp.broadcast_to(ordered(norm_gain, 0)[:, None], (norm_gain.shape[0], 128)),
        jnp.broadcast_to(ordered(norm_bias, 0)[:, None], (norm_bias.shape[0], 128)),
    )

    def run(start, nodes, aux, arrays, sources, weights, places, **table):
        scales = jnp.pad(weights, ((0, 8 - weights.shape[0]), (0, 0)))
        return update(start, nodes, aux, arrays, sources, scales, params, places, **table)

    count = parents.shape[1]
    slots = 2 * parents + (PAD - 2 * (jnp.arange(count, dtype=jnp.int32) % 4))
    aux = jnp.concatenate([slots, jnp.broadcast_to(live_rows[:, None], (1, count))])
    plan = paired if pairing else plain
    return plan(fine_latent, coarse_latent, aux, interp_weights, ordered(w_parent, 0, 0), run)


def solution(mesh):
    in_specs = (P("feat", "dom"), P("feat", "dom"), P(None, "dom"), P(None, "dom"), P("dom")) + (P(),) * 10
    return jax.shard_map(shards, mesh=mesh, in_specs=in_specs, out_specs=P("feat", "dom"), check_vma=False)
```

profile of v0, /device:TPU:1, one launch (start us, length us, event | category | flops | bytes accessed | tf_op | source)
XLA Modules:
  0.0 180.7 jit_solution(900975014300583571)
XLA Ops:
  0.0 2.1 %collective-permute-start.1 = (bf16[128,8192]{1,0:T(8,128)(2,1)}, bf16[128,8192]{1,0:T(8,128)(2,1)}, u32[]{:S(2)}, u32[]{:S(2)}) collective-permute-start(bf16[128,8192]{1,0:T(8,128)(2,1)} %refs_12_.1), channel_id=1, source_target_pairs={{0,1},{1,0},{2,3},{3,2},{4,5},{5,4},{6,7},{7,6},{8,9},{9,8},{10,11... | collective-permute-start | bytes 6291464 | tf_op jit(solution)/shard_map/ppermute | solution.py:333
  2.1 4.1 %collective-permute-start.5 = (bf16[128,8192]{1,0:T(8,128)(2,1)}, bf16[128,8192]{1,0:T(8,128)(2,1)S(1)}, u32[]{:S(2)}, u32[]{:S(2)}) collective-permute-start(bf16[128,8192]{1,0:T(8,128)(2,1)} %refs_12_.1), channel_id=1, source_target_pairs={{2,4},{6,8},{10,12},{14,16},{18,20},{22,24},{26,28},{5,3},{9,7},{1... | collective-permute-start | bytes 6291464 | tf_op jit(solution)/shard_map/ppermute | solution.py:344
  6.9 1.0 multiply_add_fusion
  8.0 0.8 copy-done.6
  8.7 1.9 %fusion = f32[9,8192]{1,0:T(8,128)} fusion(s32[]{:T(128)S(6)} %select_n.168, f32[5,16384]{1,0:T(8,128)S(1)} %pad_convert_fusion, f32[4,16384]{1,0:T(4,128)} %param.18), kind=kLoop, calls=%fused_computation.8 | loop fusion | flops 73728 | bytes 884740 | tf_op jit(solution)/shard_map/concatenate | solution.py:381
  10.6 1.3 collective-permute-start
  12.0 0.9 constant_dynamic-slice_fusion.5
  12.9 0.1 copy.21
  13.0 0.1 copy.22
  13.1 0.1 stack.23.places
  13.2 0.8 broadcast_select_fusion.7
  14.1 0.7 pad_maximum_fusion.1
  14.8 0.9 constant_dynamic-slice_fusion.3
  15.7 0.0 copy-start.14
  15.8 4.2 %constant_dynamic-slice_fusion = (bf16[128,4096]{1,0:T(8,128)(2,1)}, bf16[128,4096]{1,0:T(8,128)(2,1)}, bf16[128,4096]{1,0:T(8,128)(2,1)S(1)}, bf16[128,4096]{1,0:T(8,128)(2,1)S(1)}) fusion(bf16[128,16384]{1,0:T(8,128)(2,1)} %refs_1_.3, s32[]{:T(128)S(6)} %select_n.193, s32[]{:T(128)S(6)} %select_n.192, s32[]{:T(128)S(6)} %select_n.168, s32[]{:T(128)S(6)} %select_n.171), kind=kLoop, calls=%fused_computation.32 | loop fusion | bytes 8388624 | tf_op jit(solution)/shard_map/dynamic_slice | solution.py:281
  20.0 0.1 broadcast_select_fusion.3
  20.1 27.7 %collective-permute-done.1.refs_16_ = bf16[128,8192]{1,0:T(8,128)(2,1)} collective-permute-done((bf16[128,8192]{1,0:T(8,128)(2,1)}, bf16[128,8192]{1,0:T(8,128)(2,1)}, u32[]{:S(2)}, u32[]{:S(2)}) %collective-permute-start.1) | collective-permute-done | bytes 2097184 | tf_op jit(solution)/shard_map/ppermute | solution.py:333
  47.7 4.6 %collective-permute-start.8 = (bf16[128,8192]{1,0:T(8,128)(2,1)}, bf16[128,8192]{1,0:T(8,128)(2,1)S(1)}, u32[]{:S(2)}, u32[]{:S(2)}) collective-permute-start(bf16[128,8192]{1,0:T(8,128)(2,1)} %collective-permute-done.1.refs_16_), channel_id=1, source_target_pairs={{2,4},{6,8},{10,12},{14,16},{18,20},{22,24},{26,28},{5,3},{9,7},{1... | collective-permute-start | bytes 6291464 | tf_op jit(solution)/shard_map/ppermute | solution.py:344
  52.4 1.3 fusion.2
  53.6 0.0 collective-permute-start.2
  53.7 1.9 %collective-permute-start.3 = (bf16[128,4096]{1,0:T(8,128)(2,1)S(1)}, bf16[128,4096]{1,0:T(8,128)(2,1)S(1)}, u32[]{:S(2)}, u32[]{:S(2)}) collective-permute-start(bf16[128,4096]{1,0:T(8,128)(2,1)S(1)} %get-tuple-element.16), channel_id=1, source_target_pairs={{1,2},{2,1},{5,6},{6,5},{9,10},{10,9},{13,14},{14,13},{17,18},{18,... | collective-permute-start | bytes 3145736 | tf_op jit(solution)/shard_map/ppermute | solution.py:333
  55.6 0.1 collective-permute-start.4
  55.7 0.5 collective-permute-start.7
  56.2 9.2 %collective-permute-done.2.refs_0_ = bf16[128,4096]{1,0:T(8,128)(2,1)S(1)} collective-permute-done((bf16[128,4096]{1,0:T(8,128)(2,1)S(1)}, bf16[128,4096]{1,0:T(8,128)(2,1)S(1)}, u32[]{:S(2)}, u32[]{:S(2)}) %collective-permute-start.2) | collective-permute-done | bytes 1048608 | tf_op jit(solution)/shard_map/ppermute | solution.py:333
  65.4 1.3 collective-permute-start.6
  66.7 8.8 %collective-permute-done.8.refs_18_ = bf16[128,8192]{1,0:T(8,128)(2,1)S(1)} collective-permute-done((bf16[128,8192]{1,0:T(8,128)(2,1)}, bf16[128,8192]{1,0:T(8,128)(2,1)S(1)}, u32[]{:S(2)}, u32[]{:S(2)}) %collective-permute-start.8) | collective-permute-done | bytes 2097184 | tf_op jit(solution)/shard_map/ppermute | solution.py:344
  75.5 1.3 collective-permute-start.9
  76.9 0.1 copy.23
  77.0 1.7 collective-permute-start.12
  78.7 3.1 %collective-permute-start.13 = (bf16[128,4096]{1,0:T(8,128)(2,1)}, bf16[128,4096]{1,0:T(8,128)(2,1)}, u32[]{:S(2)}, u32[]{:S(2)}) collective-permute-start(bf16[128,4096]{1,0:T(8,128)(2,1)} %get-tuple-element.21), channel_id=1, source_target_pairs={{1,2},{2,1},{5,6},{6,5},{9,10},{10,9},{13,14},{14,13},{17,18},{18,... | collective-permute-start | bytes 3145736 | tf_op jit(solution)/shard_map/ppermute | solution.py:333
  81.9 0.1 broadcast_in_dim.13.refs_9_
  82.0 0.1 broadcast_in_dim.14.refs_10_
  82.1 1.1 copy-done.10
  83.2 0.7 copy-done.11
  83.8 34.4 %shard_map.145 = (bf16[128,4096]{1,0:T(8,128)(2,1)}, bf16[128,4096]{1,0:T(8,128)(2,1)S(1)}, f32[49168,128]{1,0:T(8,128)}) custom-call(s32[5]{0:T(128)S(1)} %stack.23.places, s32[40960]{0:T(1024)S(1)} %pad_add_fusion.aux, bf16[128,4096]{1,0:T(8,128)(2,1)S(1)} %collective-permute-done.2.refs_0_, bf16[128,16384]{1,0:T(8,128)(2,1)} %refs_1_.3, ...), custom_call_target="tpu_custom_call" | custom-call | flops 2867200000 | bytes 8388608 | tf_op jit(solution)/shard_map/pallas_call | solution.py:245
  118.3 1.0 copy-done.2
  119.2 2.4 %collective-permute-start.11 = (bf16[128,4096]{1,0:T(8,128)(2,1)}, bf16[128,4096]{1,0:T(8,128)(2,1)S(1)}, u32[]{:S(2)}, u32[]{:S(2)}) collective-permute-start(bf16[128,4096]{1,0:T(8,128)(2,1)} %copy-done.2), channel_id=1, source_target_pairs={{1,2},{2,1},{5,6},{6,5},{9,10},{10,9},{13,14},{14,13},{17,18},{18,... | collective-permute-start | bytes 3145736 | tf_op jit(solution)/shard_map/ppermute | solution.py:333
  121.7 2.2 %copy-done = bf16[128,16384]{1,0:T(8,128)(2,1)S(1)} copy-done((bf16[128,16384]{1,0:T(8,128)(2,1)S(1)}, bf16[128,16384]{1,0:T(8,128)(2,1)}, u32[]{:S(2)}) %copy-start) | copy-done | bytes 4194328
  123.9 30.7 %shard_map.146 = (bf16[128,4096]{1,0:T(8,128)(2,1)S(1)}, bf16[128,4096]{1,0:T(8,128)(2,1)S(1)}) custom-call(s32[5]{0:T(128)S(1)} %stack.23.places, s32[40960]{0:T(1024)S(1)} %pad_add_fusion.aux, bf16[128,4096]{1,0:T(8,128)(2,1)} %collective-permute-done.12.refs_0_, bf16[128,16384]{1,0:T(8,128)(2,1)S(1)} %copy-done, ...), custom_call_target="tpu_custom_call" | custom-call | flops 2867200000 | bytes 8388608 | tf_op jit(solution)/shard_map/pallas_call | solution.py:245
  154.6 0.0 collective-permute-start.14
  154.6 3.3 %collective-permute-start.15 = (bf16[128,4096]{1,0:T(8,128)(2,1)S(1)}, bf16[128,4096]{1,0:T(8,128)(2,1)S(1)}, u32[]{:S(2)}, u32[]{:S(2)}) collective-permute-start(bf16[128,4096]{1,0:T(8,128)(2,1)S(1)} %get-tuple-element.23), channel_id=1, source_target_pairs={{1,2},{2,1},{5,6},{6,5},{9,10},{10,9},{13,14},{14,13},{17,18},{18,... | collective-permute-start | bytes 3145736 | tf_op jit(solution)/shard_map/ppermute | solution.py:333
  157.9 0.4 broadcast_in_dim.10
  158.3 0.3 select_dynamic-update-slice_fusion.3
  158.6 0.3 select_dynamic-update-slice_fusion.2
  158.9 17.9 %collective-permute-done.14 = bf16[128,4096]{1,0:T(8,128)(2,1)S(1)} collective-permute-done((bf16[128,4096]{1,0:T(8,128)(2,1)S(1)}, bf16[128,4096]{1,0:T(8,128)(2,1)S(1)}, u32[]{:S(2)}, u32[]{:S(2)}) %collective-permute-start.14) | collective-permute-done | bytes 1048608 | tf_op jit(solution)/shard_map/ppermute | solution.py:333
  176.8 0.3 select_dynamic-update-slice_fusion.1
  177.1 2.4 %collective-permute-done.15 = bf16[128,4096]{1,0:T(8,128)(2,1)S(1)} collective-permute-done((bf16[128,4096]{1,0:T(8,128)(2,1)S(1)}, bf16[128,4096]{1,0:T(8,128)(2,1)S(1)}, u32[]{:S(2)}, u32[]{:S(2)}) %collective-permute-start.15) | collective-permute-done | bytes 1048608 | tf_op jit(solution)/shard_map/ppermute | solution.py:333
  179.5 1.2 select_dynamic-update-slice_fusion
  (50 shorter events, 0.4 us)
Async XLA Ops:
  0.0 47.7 %collective-permute-start.1 = (bf16[128,8192]{1,0:T(8,128)(2,1)}, bf16[128,8192]{1,0:T(8,128)(2,1)}, u32[]{:S(2)}, u32[]{:S(2)}) collective-permute-start(bf16[128,8192]{1,0:T(8,128)(2,1)} %refs_12_.1), channel_id=1, source_target_pairs={{0,1},{1,0},{2,3},{3,2},{4,5},{5,4},{6,7},{7,6},{8,9},{9,8},{10,11... | collective-permute-start | bytes 6291464 | tf_op jit(solution)/shard_map/ppermute | solution.py:333
  2.1 53.6 %collective-permute-start.5 = (bf16[128,8192]{1,0:T(8,128)(2,1)}, bf16[128,8192]{1,0:T(8,128)(2,1)S(1)}, u32[]{:S(2)}, u32[]{:S(2)}) collective-permute-start(bf16[128,8192]{1,0:T(8,128)(2,1)} %refs_12_.1), channel_id=1, source_target_pairs={{2,4},{6,8},{10,12},{14,16},{18,20},{22,24},{26,28},{5,3},{9,7},{1... | collective-permute-start | bytes 6291464 | tf_op jit(solution)/shard_map/ppermute | solution.py:344
  7.9 0.8 copy-start.6
  10.6 41.7 %collective-permute-start = (f32[9,8192]{1,0:T(8,128)}, f32[9,8192]{1,0:T(8,128)}, u32[]{:S(2)}, u32[]{:S(2)}) collective-permute-start(f32[9,8192]{1,0:T(8,128)} %fusion), channel_id=1, source_target_pairs={{0,2},{3,1},{4,6},{7,5},{8,10},{11,9},{12,14},{15,13},{16,18},{19,... | collective-permute-start | bytes 884744 | tf_op jit(solution)/shard_map/ppermute | solution.py:333
  15.7 4.2 %copy-start.13 = (bf16[256,256]{1,0:T(8,128)(2,1)S(1)}, bf16[256,256]{1,0:T(8,128)(2,1)}, u32[]{:S(2)}) copy-start(bf16[256,256]{1,0:T(8,128)(2,1)} %param.23) | copy-start | bytes 393220
  15.7 4.2 %copy-start.14 = (bf16[256,256]{1,0:T(8,128)(2,1)S(1)}, bf16[256,256]{1,0:T(8,128)(2,1)}, u32[]{:S(2)}) copy-start(bf16[256,256]{1,0:T(8,128)(2,1)} %param.20) | copy-start | bytes 393220
  15.8 36.6 %copy-start.7 = (f32[5,16384]{1,0:T(8,128)S(1)}, f32[5,16384]{1,0:T(8,128)}, u32[]{:S(2)}) copy-start(f32[5,16384]{1,0:T(8,128)} %copy-done.6) | copy-start | bytes 983044
  15.8 36.6 %copy-start.12 = (f32[4,16384]{1,0:T(4,128)S(1)}, f32[4,16384]{1,0:T(4,128)}, u32[]{:S(2)}) copy-start(f32[4,16384]{1,0:T(4,128)} %param.18) | copy-start | bytes 786436
  15.8 39.8 %copy-start.1 = (bf16[128,8192]{1,0:T(8,128)(2,1)S(1)}, bf16[128,8192]{1,0:T(8,128)(2,1)}, u32[]{:S(2)}) copy-start(bf16[128,8192]{1,0:T(8,128)(2,1)} %refs_12_.1) | copy-start | bytes 6291460
  19.9 63.9 %copy-start.4 = (bf16[256,256]{1,0:T(8,128)(2,1)S(1)}, bf16[256,256]{1,0:T(8,128)(2,1)}, u32[]{:S(2)}) copy-start(bf16[256,256]{1,0:T(8,128)(2,1)} %refs_5_.3) | copy-start | bytes 393220
  19.9 63.9 %copy-start.5 = (bf16[256,256]{1,0:T(8,128)(2,1)S(1)}, bf16[256,256]{1,0:T(8,128)(2,1)}, u32[]{:S(2)}) copy-start(bf16[256,256]{1,0:T(8,128)(2,1)} %refs_6_.3) | copy-start | bytes 393220
  47.7 27.7 %collective-permute-start.8 = (bf16[128,8192]{1,0:T(8,128)(2,1)}, bf16[128,8192]{1,0:T(8,128)(2,1)S(1)}, u32[]{:S(2)}, u32[]{:S(2)}) collective-permute-start(bf16[128,8192]{1,0:T(8,128)(2,1)} %collective-permute-done.1.refs_16_), channel_id=1, source_target_pairs={{2,4},{6,8},{10,12},{14,16},{18,20},{22,24},{26,28},{5,3},{9,7},{1... | collective-permute-start | bytes 6291464 | tf_op jit(solution)/shard_map/ppermute | solution.py:344
  53.6 11.8 %collective-permute-start.2 = (bf16[128,4096]{1,0:T(8,128)(2,1)S(1)}, bf16[128,4096]{1,0:T(8,128)(2,1)S(1)}, u32[]{:S(2)}, u32[]{:S(2)}) collective-permute-start(bf16[128,4096]{1,0:T(8,128)(2,1)S(1)} %get-tuple-element.15), channel_id=1, source_target_pairs={{0,2},{3,1},{1,0},{2,3},{4,6},{7,5},{5,4},{6,7},{8,10},{11,9},{9,8... | collective-permute-start | bytes 3145736 | tf_op jit(solution)/shard_map/ppermute | solution.py:333
  53.7 23.3 %collective-permute-start.3 = (bf16[128,4096]{1,0:T(8,128)(2,1)S(1)}, bf16[128,4096]{1,0:T(8,128)(2,1)S(1)}, u32[]{:S(2)}, u32[]{:S(2)}) collective-permute-start(bf16[128,4096]{1,0:T(8,128)(2,1)S(1)} %get-tuple-element.16), channel_id=1, source_target_pairs={{1,2},{2,1},{5,6},{6,5},{9,10},{10,9},{13,14},{14,13},{17,18},{18,... | collective-permute-start | bytes 3145736 | tf_op jit(solution)/shard_map/ppermute | solution.py:333
  55.6 23.1 %collective-permute-start.4 = (bf16[128,8192]{1,0:T(8,128)(2,1)S(1)}, bf16[128,8192]{1,0:T(8,128)(2,1)S(1)}, u32[]{:S(2)}, u32[]{:S(2)}) collective-permute-start(bf16[128,8192]{1,0:T(8,128)(2,1)S(1)} %copy-done.1), channel_id=1, source_target_pairs={{0,2},{1,3},{2,0},{3,1},{4,6},{5,7},{6,4},{7,5},{8,10},{9,11},{10,... | collective-permute-start | bytes 6291464 | tf_op jit(solution)/shard_map/ppermute | solution.py:333
  55.7 26.1 %collective-permute-start.7 = (bf16[128,8192]{1,0:T(8,128)(2,1)}, bf16[128,8192]{1,0:T(8,128)(2,1)S(1)}, u32[]{:S(2)}, u32[]{:S(2)}) collective-permute-start(bf16[128,8192]{1,0:T(8,128)(2,1)} %collective-permute-done.1.refs_16_), channel_id=1, source_target_pairs={{0,2},{1,3},{2,0},{3,1},{4,6},{5,7},{6,4},{7,5},{8,10},{9,11},{10,... | collective-permute-start | bytes 6291464 | tf_op jit(solution)/shard_map/ppermute | solution.py:333
  65.4 16.5 %collective-permute-start.6 = (bf16[128,8192]{1,0:T(8,128)(2,1)S(1)}, bf16[128,8192]{1,0:T(8,128)(2,1)S(1)}, u32[]{:S(2)}, u32[]{:S(2)}) collective-permute-start(bf16[128,8192]{1,0:T(8,128)(2,1)S(1)} %collective-permute-done.5.refs_14_), channel_id=1, source_target_pairs={{0,2},{3,1},{4,6},{7,5},{8,10},{11,9},{12,14},{15,13},{16,18},{19,... | collective-permute-start | bytes 6291464 | tf_op jit(solution)/shard_map/ppermute | solution.py:333
  75.5 6.6 %copy-start.9 = (bf16[128,8192]{1,0:T(8,128)(2,1)}, bf16[128,8192]{1,0:T(8,128)(2,1)S(1)}, u32[]{:S(2)}) copy-start(bf16[128,8192]{1,0:T(8,128)(2,1)S(1)} %collective-permute-done.8.refs_18_) | copy-start | bytes 6291460
  75.5 6.4 %collective-permute-start.9 = (bf16[128,8192]{1,0:T(8,128)(2,1)S(1)}, bf16[128,8192]{1,0:T(8,128)(2,1)S(1)}, u32[]{:S(2)}, u32[]{:S(2)}) collective-permute-start(bf16[128,8192]{1,0:T(8,128)(2,1)S(1)} %collective-permute-done.8.refs_18_), channel_id=1, source_target_pairs={{0,2},{3,1},{4,6},{7,5},{8,10},{11,9},{12,14},{15,13},{16,18},{19,... | collective-permute-start | bytes 6291464 | tf_op jit(solution)/shard_map/ppermute | solution.py:333
  77.0 44.7 %collective-permute-start.12 = (bf16[128,4096]{1,0:T(8,128)(2,1)}, bf16[128,4096]{1,0:T(8,128)(2,1)}, u32[]{:S(2)}, u32[]{:S(2)}) collective-permute-start(bf16[128,4096]{1,0:T(8,128)(2,1)} %get-tuple-element.20), channel_id=1, source_target_pairs={{0,2},{3,1},{1,0},{2,3},{4,6},{7,5},{5,4},{6,7},{8,10},{11,9},{9,8... | collective-permute-start | bytes 3145736 | tf_op jit(solution)/shard_map/ppermute | solution.py:333
  78.7 43.0 %collective-permute-start.13 = (bf16[128,4096]{1,0:T(8,128)(2,1)}, bf16[128,4096]{1,0:T(8,128)(2,1)}, u32[]{:S(2)}, u32[]{:S(2)}) collective-permute-start(bf16[128,4096]{1,0:T(8,128)(2,1)} %get-tuple-element.21), channel_id=1, source_target_pairs={{1,2},{2,1},{5,6},{6,5},{9,10},{10,9},{13,14},{14,13},{17,18},{18,... | collective-permute-start | bytes 3145736 | tf_op jit(solution)/shard_map/ppermute | solution.py:333
  81.8 1.3 copy-start.10
  81.9 2.0 %copy-start.11 = (bf16[128,8192]{1,0:T(8,128)(2,1)}, bf16[128,8192]{1,0:T(8,128)(2,1)S(1)}, u32[]{:S(2)}) copy-start(bf16[128,8192]{1,0:T(8,128)(2,1)S(1)} %collective-permute-done.9.refs_19_) | copy-start | bytes 6291460
  118.3 1.0 copy-start.2
  119.2 38.7 %collective-permute-start.10 = (bf16[128,4096]{1,0:T(8,128)(2,1)}, bf16[128,4096]{1,0:T(8,128)(2,1)S(1)}, u32[]{:S(2)}, u32[]{:S(2)}) collective-permute-start(bf16[128,4096]{1,0:T(8,128)(2,1)} %get-tuple-element.19), channel_id=1, source_target_pairs={{2,0},{1,3},{0,1},{3,2},{6,4},{5,7},{4,5},{7,6},{10,8},{9,11},{8,9... | collective-permute-start | bytes 3145736 | tf_op jit(solution)/shard_map/ppermute | solution.py:333
  119.2 39.4 %collective-permute-start.11 = (bf16[128,4096]{1,0:T(8,128)(2,1)}, bf16[128,4096]{1,0:T(8,128)(2,1)S(1)}, u32[]{:S(2)}, u32[]{:S(2)}) collective-permute-start(bf16[128,4096]{1,0:T(8,128)(2,1)} %copy-done.2), channel_id=1, source_target_pairs={{1,2},{2,1},{5,6},{6,5},{9,10},{10,9},{13,14},{14,13},{17,18},{18,... | collective-permute-start | bytes 3145736 | tf_op jit(solution)/shard_map/ppermute | solution.py:333
  121.7 2.2 %copy-start = (bf16[128,16384]{1,0:T(8,128)(2,1)S(1)}, bf16[128,16384]{1,0:T(8,128)(2,1)}, u32[]{:S(2)}) copy-start(bf16[128,16384]{1,0:T(8,128)(2,1)} %refs_1_.3) | copy-start | bytes 12582916
  154.6 3.7 %copy-start.3 = (bf16[128,4096]{1,0:T(8,128)(2,1)S(1)}, bf16[128,4096]{1,0:T(8,128)(2,1)}, u32[]{:S(2)}) copy-start(bf16[128,4096]{1,0:T(8,128)(2,1)} %copy-done.2) | copy-start | bytes 3145732
  154.6 22.2 %collective-permute-start.14 = (bf16[128,4096]{1,0:T(8,128)(2,1)S(1)}, bf16[128,4096]{1,0:T(8,128)(2,1)S(1)}, u32[]{:S(2)}, u32[]{:S(2)}) collective-permute-start(bf16[128,4096]{1,0:T(8,128)(2,1)S(1)} %get-tuple-element.24), channel_id=1, source_target_pairs={{2,0},{1,3},{0,1},{3,2},{6,4},{5,7},{4,5},{7,6},{10,8},{9,11},{8,9... | collective-permute-start | bytes 3145736 | tf_op jit(solution)/shard_map/ppermute | solution.py:333
  154.6 24.9 %collective-permute-start.15 = (bf16[128,4096]{1,0:T(8,128)(2,1)S(1)}, bf16[128,4096]{1,0:T(8,128)(2,1)S(1)}, u32[]{:S(2)}, u32[]{:S(2)}) collective-permute-start(bf16[128,4096]{1,0:T(8,128)(2,1)S(1)} %get-tuple-element.23), channel_id=1, source_target_pairs={{1,2},{2,1},{5,6},{6,5},{9,10},{10,9},{13,14},{14,13},{17,18},{18,... | collective-permute-start | bytes 3145736 | tf_op jit(solution)/shard_map/ppermute | solution.py:333
  177.1 2.4 %copy-start.8 = (bf16[128,16384]{1,0:T(8,128)(2,1)}, bf16[128,16384]{1,0:T(8,128)(2,1)S(1)}, u32[]{:S(2)}) copy-start(bf16[128,16384]{1,0:T(8,128)(2,1)S(1)} %select_dynamic-update-slice_fusion.1) | copy-start | bytes 12582916
where the time goes:
time: 183 us; the launch traced here: 181 us
  waiting for transfers between devices  65.9 us (36%)
  Pallas kernels  65.1 us (36%)
  starting transfers between devices  27.6 us (15%)
  local copies, waits for them, and re-layouts  12.7 us (7%)
  other arithmetic  8.1 us (4%)
    pallas_call x2, Pallas kernels, update(): pl.pallas_call(functools.partial(update_kernel, sources, step, start, seg...  65.1 us
    ppermute x14, waiting for transfers between devices, send(): return lax.ppermute(value, ('dom', 'feat'), perm)  57.1 us
    ppermute x14, starting transfers between devices, send(): return lax.ppermute(value, ('dom', 'feat'), perm)  18.9 us
    ppermute x2, waiting for transfers between devices, halo(): return lax.ppermute(value, ('dom', 'feat'), perm)  8.8 us
    ppermute x2, starting transfers between devices, halo(): return lax.ppermute(value, ('dom', 'feat'), perm)  8.65 us
    unnamed x33, local copies, waits for them, and re-layouts  6.01 us
    dynamic_slice x1, local copies, waits for them, and re-layouts, cut(): return lax.dynamic_slice_in_dim(array, at, size, 1)  4.16 us
  transfers between devices with their start and end apart: 16, of which 5 were waited for; matrix products, arithmetic and copies ran while one was open for 8% of the time, Pallas kernels for 36%

commit v1 on v0

--- a/solution.py
+++ b/solution.py
@@ -12,7 +12,7 @@
 PAD = 8
 SHARE = 4
 PARTS = 1
-STEP = 256
+STEP = 512
 GROUPS = 13
 
 
@@ -197,11 +197,13 @@
         summed, own_part, current = gathered(), earlier[...], later[...]
         parts = finish(before, summed, own_part)
         base = pl.multiple_of(i * (parents * step), parents * step)
-        begun = begin(after)
+        begun, result = begin(after), None
         for first in range(0, step // 4, GROUPS):
-            result = next(parts, None) if first < 4 * GROUPS else last(parts)
+            result = next(parts, result)
             sums = [group(base, g) for g in range(first, min(first + GROUPS, step // 4))]
             total[pl.ds(first * 8, len(sums) * 8), :] = jnp.concatenate(sums, axis=0)
+        for value in parts:
+            result = value
         write(before, result)
         earlier[...] = current
         keep(*begun)
@@ -226,13 +228,14 @@
     step = min(STEP, nodes)
     vmem = pl.BlockSpec(memory_space=pltpu.VMEM)
     smem = pl.BlockSpec(memory_space=pltpu.SMEM)
-    far = pl.BlockSpec(memory_space=pltpu.HBM)
+    far = pl.BlockSpec(memory_space=pl.ANY)
+    hbm = pl.BlockSpec(memory_space=pltpu.HBM)
     out_shape = [jax.ShapeDtypeStruct((features, nodes), BF16)] * count
     operands = [places, by_step(aux, step), *arrays, scales, *params]
     specs = [smem, far] + [far] * (len(arrays) + 1 + len(params))
     scratch, table_step = [], 0
     if segments is None:
-        operands, specs = operands + [table], specs + [far]
+        operands, specs = operands + [table], specs + [hbm]
     else:
         operands, specs = operands + [w_parent, *coarse], specs + [vmem] + [far] * len(coarse)
         table_step = min(2048, segments[0][2])
@@ -246,7 +249,7 @@
         functools.partial(update_kernel, sources, step, start, segments, table_step),
         out_shape=out_shape,
         in_specs=specs,
-        out_specs=[vmem] * count + [far] * (len(out_shape) - count),
+        out_specs=[vmem] * count + [hbm] * (len(out_shape) - count),
         scratch_shapes=scratch
         + [
             pltpu.VMEM(table.shape, F32),
@@ -266,6 +269,40 @@
         compiler_params=pltpu.CompilerParams(vmem_limit_bytes=40 << 20),
         cost_estimate=pl.CostEstimate(flops=nodes * 700000, bytes_accessed=nodes * 2048, transcendentals=nodes),
     )(*operands)
+
+
+def place_kernel(start, places, kept, first, second, *refs):
+    result, sems = refs[-2:]
+    half, length = result.shape[1] // 2, kept.shape[1]
+    mine = places[4]
+    for which, (here, there) in enumerate([(kept, first), (first, second)]):
+
+        @pl.when(places[3] == which)
+        def _(here=here, there=there):
+            copies = [
+                pltpu.make_async_copy(
+                    piece, result.at[:, pl.ds(pl.multiple_of(column + start, 128), length)], sems.at[at]
+                )
+                for at, (piece, column) in enumerate([(here, mine), (there, half - mine)])
+            ]
+            for copy in copies:
+                copy.start()
+            for copy in copies:
+                copy.wait()
+
+
+def place(start, places, kept, first, second, shape, result=None):
+    far = pl.BlockSpec(memory_space=pl.ANY)
+    given = [] if result is None else [result]
+    return pl.pallas_call(
+        functools.partial(place_kernel, start),
+        out_shape=shape,
+        in_specs=[pl.BlockSpec(memory_space=pltpu.SMEM)] + [far] * (3 + len(given)),
+        out_specs=pl.BlockSpec(memory_space=pltpu.HBM),
+        scratch_shapes=[pltpu.SemaphoreType.DMA((2,))],
+        input_output_aliases={4: 0} if given else {},
+        cost_estimate=pl.CostEstimate(flops=0, bytes_accessed=4 * kept.size, transcendentals=0),
+    )(places, kept, first, second, *given)
 
 
 def after(value, *others):
@@ -385,7 +422,6 @@
 
     making = dict(segments=segments, w_parent=w_parent, coarse=coarse)
     sources = [((0, None),), ((1, 0), (2, None))]
-    result = jnp.zeros_like(fine_latent)
     moved = []
     for c, (start, length) in enumerate(shares(half)):
         out, kept, *made = run(
@@ -393,11 +429,9 @@
         )
         table = made[0] if made else table
         moved.append((start, kept, send(out, from_first), send(kept, to_second)))
+    result, shape = None, jax.ShapeDtypeStruct(fine_latent.shape, BF16)
     for start, kept, first, second in moved:
-        result = lax.dynamic_update_slice_in_dim(result, jnp.where(matched, kept, first), mine + start, 1)
-        result = lax.dynamic_update_slice_in_dim(
-            result, jnp.where(matched, first, second), half - mine + start, 1
-        )
+        result = place(start, places, kept, first, second, shape, result)
     return result
 
 

time: 183 us -> 293 us (1.60)
  Pallas kernels: 65.1 us -> 195 us
  waiting for transfers between devices: 65.9 us -> 58 us
  local copies, waits for them, and re-layouts: 12.7 us -> 7.8 us
  other arithmetic: 8.1 us -> 3.77 us
    pallas_call x0 -> x2, Pallas kernels: none -> 131 us  [place(): pl.pallas_call(functools.partial(place_kernel, start), out_shape=shape, i...]
    ppermute x2, waiting for transfers between devices: 8.8 us -> 0.01 us  [halo(): return lax.ppermute(value, ('dom', 'feat'), perm)]
    unnamed x33 -> x41, local copies, waits for them, and re-layouts: 6.01 us -> 2.52 us
  transfers between devices with their start and end apart: 16 -> 16, of which waited for: 5 -> 6; matrix products, arithmetic and copies ran while one was open for 8% -> 3% of each run, Pallas kernels for 36% -> 45%
where the time goes in v1:
time: 293 us; the launch traced here: 291 us
  Pallas kernels  195 us (67%)
  waiting for transfers between devices  58 us (20%)
  starting transfers between devices  25.2 us (9%)
  local copies, waits for them, and re-layouts  7.8 us (3%)
  other arithmetic  3.77 us (1%)
    pallas_call x2, Pallas kernels, place(): pl.pallas_call(functools.partial(place_kernel, start), out_shape=shape, i...  131 us
    pallas_call x2, Pallas kernels, update(): pl.pallas_call(functools.partial(update_kernel, sources, step, start, seg...  64.4 us
    ppermute x14, waiting for transfers between devices, send(): return lax.ppermute(value, ('dom', 'feat'), perm)  58 us
    ppermute x14, starting transfers between devices, send(): return lax.ppermute(value, ('dom', 'feat'), perm)  17.8 us
    ppermute x2, starting transfers between devices, halo(): return lax.ppermute(value, ('dom', 'feat'), perm)  7.42 us
  transfers between devices with their start and end apart: 16, of which 6 were waited for; matrix products, arithmetic and copies ran while one was open for 3% of the time, Pallas kernels for 45%

profile of v1, /device:TPU:1, one launch (start us, length us, event | category | flops | bytes accessed | tf_op | source)
XLA Modules:
  0.0 291.3 jit_solution(11486765824769828340)
XLA Ops:
  0.0 2.1 collective-permute-start.1
  2.2 4.1 %collective-permute-start.7 = (bf16[128,8192]{1,0:T(8,128)(2,1)}, bf16[128,8192]{1,0:T(8,128)(2,1)S(1)}, u32[]{:S(2)}, u32[]{:S(2)}) collective-permute-start(bf16[128,8192]{1,0:T(8,128)(2,1)} %refs_12_.1), channel_id=1, source_target_pairs={{2,4},{6,8},{10,12},{14,16},{18,20},{22,24},{26,28},{5,3},{9,7},{1... | collective-permute-start | bytes 6291464 | tf_op jit(solution)/shard_map/ppermute | solution.py:381
  6.9 1.0 multiply_add_fusion
  8.0 1.1 fusion
  9.2 1.3 collective-permute-start
  10.6 0.1 copy.22
  10.7 0.1 copy.23
  10.8 0.1 stack.23.places
  10.9 0.1 broadcast_select_fusion.7
  11.0 0.9 constant_dynamic-slice_fusion.1
  12.0 0.0 copy-start.12
  12.0 0.0 copy-start.13
  12.0 0.0 copy-start.1
  12.0 0.0 copy-start.10
  12.0 4.0 %constant_dynamic-slice_fusion.2 = (bf16[128,4096]{1,0:T(8,128)(2,1)S(1)}, bf16[128,4096]{1,0:T(8,128)(2,1)S(1)}, bf16[128,4096]{1,0:T(8,128)(2,1)}, bf16[128,4096]{1,0:T(8,128)(2,1)}) fusion(bf16[128,16384]{1,0:T(8,128)(2,1)} %refs_1_.3, s32[]{:T(128)S(6)} %select_n.141, s32[]{:T(128)S(6)} %select_n.164, s32[]{:T(128)S(6)} %select_n.145, s32[]{:T(128)S(6)} %select_n.144), kind=kLoop, calls=%fused_computation.30 | loop fusion | bytes 8388624 | tf_op jit(solution)/shard_map/dynamic_slice | solution.py:318
  16.1 0.1 broadcast_select_fusion.3
  16.2 0.0 copy-start.4
  16.2 0.0 copy-start.5
  16.2 31.6 %collective-permute-done.1.refs_16_ = bf16[128,8192]{1,0:T(8,128)(2,1)} collective-permute-done((bf16[128,8192]{1,0:T(8,128)(2,1)}, bf16[128,8192]{1,0:T(8,128)(2,1)}, u32[]{:S(2)}, u32[]{:S(2)}) %collective-permute-start.1) | collective-permute-done | bytes 2097184 | tf_op jit(solution)/shard_map/ppermute | solution.py:370
  47.8 1.2 collective-permute-start.6
  49.1 3.3 %collective-permute-start.10 = (bf16[128,8192]{1,0:T(8,128)(2,1)}, bf16[128,8192]{1,0:T(8,128)(2,1)S(1)}, u32[]{:S(2)}, u32[]{:S(2)}) collective-permute-start(bf16[128,8192]{1,0:T(8,128)(2,1)} %collective-permute-done.1.refs_16_), channel_id=1, source_target_pairs={{2,4},{6,8},{10,12},{14,16},{18,20},{22,24},{26,28},{5,3},{9,7},{1... | collective-permute-start | bytes 6291464 | tf_op jit(solution)/shard_map/ppermute | solution.py:381
  52.4 0.0 collective-permute-done
  52.4 1.3 fusion.2
  53.7 0.0 collective-permute-start.4
  53.7 1.9 collective-permute-start.5
  55.7 0.0 collective-permute-start.2
  55.7 9.7 %collective-permute-done.4.refs_0_ = bf16[128,4096]{1,0:T(8,128)(2,1)S(1)} collective-permute-done((bf16[128,4096]{1,0:T(8,128)(2,1)S(1)}, bf16[128,4096]{1,0:T(8,128)(2,1)S(1)}, u32[]{:S(2)}, u32[]{:S(2)}) %collective-permute-start.4) | collective-permute-done | bytes 1048608 | tf_op jit(solution)/shard_map/ppermute | solution.py:370
  65.5 1.9 collective-permute-start.3
  67.4 9.3 %collective-permute-done.5.refs_2_ = bf16[128,4096]{1,0:T(8,128)(2,1)S(1)} collective-permute-done((bf16[128,4096]{1,0:T(8,128)(2,1)S(1)}, bf16[128,4096]{1,0:T(8,128)(2,1)S(1)}, u32[]{:S(2)}, u32[]{:S(2)}) %collective-permute-start.5) | collective-permute-done | bytes 1048608 | tf_op jit(solution)/shard_map/ppermute | solution.py:370
  76.7 1.3 collective-permute-start.8
  78.0 0.0 collective-permute-done.10.refs_18_
  78.0 1.3 collective-permute-start.11
  79.5 1.5 collective-permute-done.9.refs_17_
  81.1 2.8 collective-permute-done.8.refs_15_
  83.9 3.0 %collective-permute-done.11.refs_19_ = bf16[128,8192]{1,0:T(8,128)(2,1)S(1)} collective-permute-done((bf16[128,8192]{1,0:T(8,128)(2,1)S(1)}, bf16[128,8192]{1,0:T(8,128)(2,1)S(1)}, u32[]{:S(2)}, u32[]{:S(2)}) %collective-permute-start.11) | collective-permute-done | bytes 2097184 | tf_op jit(solution)/shard_map/ppermute | solution.py:370
  86.9 0.1 broadcast_in_dim.10.refs_9_
  87.0 1.2 copy-done.9
  88.2 0.1 broadcast_in_dim.11.refs_10_
  88.3 0.0 copy-start
  88.3 34.0 %shard_map.145 = (bf16[128,4096]{1,0:T(8,128)(2,1)S(1)}, bf16[128,4096]{1,0:T(8,128)(2,1)S(1)}, f32[49168,128]{1,0:T(8,128)}) custom-call(s32[5]{0:T(128)S(1)} %stack.23.places, s32[40960]{0:T(1024)S(1)} %pad_add_fusion.aux, bf16[128,4096]{1,0:T(8,128)(2,1)S(1)} %collective-permute-done.4.refs_0_, bf16[128,16384]{1,0:T(8,128)(2,1)} %refs_1_.3, ...), custom_call_target="tpu_custom_call" | custom-call | flops 2867200000 | bytes 8388608 | tf_op jit(solution)/shard_map/pallas_call | solution.py:248
  122.3 0.3 collective-permute-start.14
  122.6 4.4 %collective-permute-start.15 = (bf16[128,4096]{1,0:T(8,128)(2,1)S(1)}, bf16[128,4096]{1,0:T(8,128)(2,1)}, u32[]{:S(2)}, u32[]{:S(2)}) collective-permute-start(bf16[128,4096]{1,0:T(8,128)(2,1)S(1)} %get-tuple-element.23.kept), channel_id=1, source_target_pairs={{1,2},{2,1},{5,6},{6,5},{9,10},{10,9},{13,14},{14,13},{17,18},{18,... | collective-permute-start | bytes 3145736 | tf_op jit(solution)/shard_map/ppermute | solution.py:370
  127.1 30.4 %shard_map.146 = (bf16[128,4096]{1,0:T(8,128)(2,1)S(1)}, bf16[128,4096]{1,0:T(8,128)(2,1)S(1)}) custom-call(s32[5]{0:T(128)S(1)} %stack.23.places, s32[40960]{0:T(1024)S(1)} %pad_add_fusion.aux, bf16[128,4096]{1,0:T(8,128)(2,1)S(1)} %collective-permute-done.2.refs_0_, bf16[128,16384]{1,0:T(8,128)(2,1)S(1)} %copy-done, ...), custom_call_target="tpu_custom_call" | custom-call | flops 2867200000 | bytes 8388608 | tf_op jit(solution)/shard_map/pallas_call | solution.py:248
  157.5 0.0 collective-permute-start.12
  157.5 1.9 collective-permute-start.13
  159.5 1.0 copy-done.11
  160.4 65.3 %shard_map.147.refs_0_ = bf16[128,16384]{1,0:T(8,128)(2,1)} custom-call(s32[5]{0:T(128)} %copy-done.6, bf16[128,4096]{1,0:T(8,128)(2,1)} %copy-done.3, bf16[128,4096]{1,0:T(8,128)(2,1)} %copy-done.11, bf16[128,4096]{1,0:T(8,128)(2,1)} %collective-permute-done.15.second), custom_call_target="tpu_custom_call" | custom-call | bytes 2097152 | tf_op jit(solution)/shard_map/pallas_call | solution.py:297
  225.8 65.3 %shard_map.148 = bf16[128,16384]{1,0:T(8,128)(2,1)} custom-call(s32[5]{0:T(128)} %copy-done.6, bf16[128,4096]{1,0:T(8,128)(2,1)} %copy-done.2, bf16[128,4096]{1,0:T(8,128)(2,1)} %collective-permute-done.12.first, bf16[128,4096]{1,0:T(8,128)(2,1)} %collective-permute-done.13.second, bf16[128,16384]{1,0:T(8,128)(2,1)} %shard_map.147.refs_0_), custom_call_target="tpu_custom_call", output_to_operand_aliasing={{}: (4, {})} | custom-call | bytes 2097152 | tf_op jit(solution)/shard_map/pallas_call | solution.py:297
  (55 shorter events, 0.4 us)
Async XLA Ops:
  0.0 10.5 %copy-start.14 = (bf16[256,256]{1,0:T(8,128)(2,1)S(1)}, bf16[256,256]{1,0:T(8,128)(2,1)}, u32[]{:S(2)}) copy-start(bf16[256,256]{1,0:T(8,128)(2,1)} %param.25) | copy-start | bytes 393220
  0.0 10.9 %copy-start.15 = (f32[256]{0:T(256)S(1)}, f32[256]{0:T(256)}, u32[]{:S(2)}) copy-start(f32[256]{0:T(256)} %param.29) | copy-start | bytes 3076
  0.0 10.9 %copy-start.16 = (f32[256]{0:T(256)S(1)}, f32[256]{0:T(256)}, u32[]{:S(2)}) copy-start(f32[256]{0:T(256)} %param.28) | copy-start | bytes 3076
  0.0 11.0 %copy-start.17 = (f32[256]{0:T(256)S(1)}, f32[256]{0:T(256)}, u32[]{:S(2)}) copy-start(f32[256]{0:T(256)} %param.27) | copy-start | bytes 3076
  0.0 11.0 %copy-start.18 = (f32[256]{0:T(256)S(1)}, f32[256]{0:T(256)}, u32[]{:S(2)}) copy-start(f32[256]{0:T(256)} %param.26) | copy-start | bytes 3076
  0.0 47.8 %collective-permute-start.1 = (bf16[128,8192]{1,0:T(8,128)(2,1)}, bf16[128,8192]{1,0:T(8,128)(2,1)}, u32[]{:S(2)}, u32[]{:S(2)}) collective-permute-start(bf16[128,8192]{1,0:T(8,128)(2,1)} %refs_12_.1), channel_id=1, source_target_pairs={{0,1},{1,0},{2,3},{3,2},{4,5},{5,4},{6,7},{7,6},{8,9},{9,8},{10,11... | collective-permute-start | bytes 6291464 | tf_op jit(solution)/shard_map/ppermute | solution.py:370
  2.2 53.5 %collective-permute-start.7 = (bf16[128,8192]{1,0:T(8,128)(2,1)}, bf16[128,8192]{1,0:T(8,128)(2,1)S(1)}, u32[]{:S(2)}, u32[]{:S(2)}) collective-permute-start(bf16[128,8192]{1,0:T(8,128)(2,1)} %refs_12_.1), channel_id=1, source_target_pairs={{2,4},{6,8},{10,12},{14,16},{18,20},{22,24},{26,28},{5,3},{9,7},{1... | collective-permute-start | bytes 6291464 | tf_op jit(solution)/shard_map/ppermute | solution.py:381
  9.2 43.3 %collective-permute-start = (f32[9,8192]{1,0:T(8,128)S(1)}, f32[9,8192]{1,0:T(8,128)}, u32[]{:S(2)}, u32[]{:S(2)}) collective-permute-start(f32[9,8192]{1,0:T(8,128)S(1)} %fusion), channel_id=1, source_target_pairs={{0,2},{3,1},{4,6},{7,5},{8,10},{11,9},{12,14},{15,13},{16,18},{19,... | collective-permute-start | bytes 884744 | tf_op jit(solution)/shard_map/ppermute | solution.py:370
  10.9 116.1 %copy-start.6 = (s32[5]{0:T(128)}, s32[5]{0:T(128)S(1)}, u32[]{:S(2)}) copy-start(s32[5]{0:T(128)S(1)} %stack.23.places) | copy-start | bytes 64
  12.0 4.1 %copy-start.12 = (bf16[256,256]{1,0:T(8,128)(2,1)S(1)}, bf16[256,256]{1,0:T(8,128)(2,1)}, u32[]{:S(2)}) copy-start(bf16[256,256]{1,0:T(8,128)(2,1)} %param.23) | copy-start | bytes 393220
  12.0 4.1 %copy-start.13 = (bf16[256,256]{1,0:T(8,128)(2,1)S(1)}, bf16[256,256]{1,0:T(8,128)(2,1)}, u32[]{:S(2)}) copy-start(bf16[256,256]{1,0:T(8,128)(2,1)} %param.20) | copy-start | bytes 393220
  12.0 35.8 %copy-start.1 = (bf16[128,8192]{1,0:T(8,128)(2,1)S(1)}, bf16[128,8192]{1,0:T(8,128)(2,1)}, u32[]{:S(2)}) copy-start(bf16[128,8192]{1,0:T(8,128)(2,1)} %refs_12_.1) | copy-start | bytes 6291460
  12.0 40.4 %copy-start.10 = (f32[4,16384]{1,0:T(4,128)S(1)}, f32[4,16384]{1,0:T(4,128)}, u32[]{:S(2)}) copy-start(f32[4,16384]{1,0:T(4,128)} %param.18) | copy-start | bytes 786436
  16.2 72.1 %copy-start.4 = (bf16[256,256]{1,0:T(8,128)(2,1)S(1)}, bf16[256,256]{1,0:T(8,128)(2,1)}, u32[]{:S(2)}) copy-start(bf16[256,256]{1,0:T(8,128)(2,1)} %refs_5_.3) | copy-start | bytes 393220
  16.2 72.1 %copy-start.5 = (bf16[256,256]{1,0:T(8,128)(2,1)S(1)}, bf16[256,256]{1,0:T(8,128)(2,1)}, u32[]{:S(2)}) copy-start(bf16[256,256]{1,0:T(8,128)(2,1)} %refs_6_.3) | copy-start | bytes 393220
  47.8 28.9 %collective-permute-start.6 = (bf16[128,8192]{1,0:T(8,128)(2,1)S(1)}, bf16[128,8192]{1,0:T(8,128)(2,1)S(1)}, u32[]{:S(2)}, u32[]{:S(2)}) collective-permute-start(bf16[128,8192]{1,0:T(8,128)(2,1)S(1)} %copy-done.1), channel_id=1, source_target_pairs={{0,2},{1,3},{2,0},{3,1},{4,6},{5,7},{6,4},{7,5},{8,10},{9,11},{10,... | collective-permute-start | bytes 6291464 | tf_op jit(solution)/shard_map/ppermute | solution.py:370
  49.1 28.9 %collective-permute-start.10 = (bf16[128,8192]{1,0:T(8,128)(2,1)}, bf16[128,8192]{1,0:T(8,128)(2,1)S(1)}, u32[]{:S(2)}, u32[]{:S(2)}) collective-permute-start(bf16[128,8192]{1,0:T(8,128)(2,1)} %collective-permute-done.1.refs_16_), channel_id=1, source_target_pairs={{2,4},{6,8},{10,12},{14,16},{18,20},{22,24},{26,28},{5,3},{9,7},{1... | collective-permute-start | bytes 6291464 | tf_op jit(solution)/shard_map/ppermute | solution.py:381
  53.7 11.8 %collective-permute-start.4 = (bf16[128,4096]{1,0:T(8,128)(2,1)S(1)}, bf16[128,4096]{1,0:T(8,128)(2,1)S(1)}, u32[]{:S(2)}, u32[]{:S(2)}) collective-permute-start(bf16[128,4096]{1,0:T(8,128)(2,1)S(1)} %get-tuple-element.17), channel_id=1, source_target_pairs={{0,2},{3,1},{1,0},{2,3},{4,6},{7,5},{5,4},{6,7},{8,10},{11,9},{9,8... | collective-permute-start | bytes 3145736 | tf_op jit(solution)/shard_map/ppermute | solution.py:370
  53.7 23.0 %collective-permute-start.5 = (bf16[128,4096]{1,0:T(8,128)(2,1)S(1)}, bf16[128,4096]{1,0:T(8,128)(2,1)S(1)}, u32[]{:S(2)}, u32[]{:S(2)}) collective-permute-start(bf16[128,4096]{1,0:T(8,128)(2,1)S(1)} %get-tuple-element.18), channel_id=1, source_target_pairs={{1,2},{2,1},{5,6},{6,5},{9,10},{10,9},{13,14},{14,13},{17,18},{18,... | collective-permute-start | bytes 3145736 | tf_op jit(solution)/shard_map/ppermute | solution.py:370
  55.7 71.3 %collective-permute-start.2 = (bf16[128,4096]{1,0:T(8,128)(2,1)}, bf16[128,4096]{1,0:T(8,128)(2,1)S(1)}, u32[]{:S(2)}, u32[]{:S(2)}) collective-permute-start(bf16[128,4096]{1,0:T(8,128)(2,1)} %get-tuple-element.15), channel_id=1, source_target_pairs={{0,2},{3,1},{1,0},{2,3},{4,6},{7,5},{5,4},{6,7},{8,10},{11,9},{9,8... | collective-permute-start | bytes 3145736 | tf_op jit(solution)/shard_map/ppermute | solution.py:370
  65.5 61.6 %collective-permute-start.3 = (bf16[128,4096]{1,0:T(8,128)(2,1)}, bf16[128,4096]{1,0:T(8,128)(2,1)S(1)}, u32[]{:S(2)}, u32[]{:S(2)}) collective-permute-start(bf16[128,4096]{1,0:T(8,128)(2,1)} %get-tuple-element.16), channel_id=1, source_target_pairs={{1,2},{2,1},{5,6},{6,5},{9,10},{10,9},{13,14},{14,13},{17,18},{18,... | collective-permute-start | bytes 3145736 | tf_op jit(solution)/shard_map/ppermute | solution.py:370
  76.7 4.4 %collective-permute-start.9 = (bf16[128,8192]{1,0:T(8,128)(2,1)}, bf16[128,8192]{1,0:T(8,128)(2,1)S(1)}, u32[]{:S(2)}, u32[]{:S(2)}) collective-permute-start(bf16[128,8192]{1,0:T(8,128)(2,1)} %collective-permute-done.1.refs_16_), channel_id=1, source_target_pairs={{0,2},{1,3},{2,0},{3,1},{4,6},{5,7},{6,4},{7,5},{8,10},{9,11},{10,... | collective-permute-start | bytes 6291464 | tf_op jit(solution)/shard_map/ppermute | solution.py:370
  76.7 7.2 %collective-permute-start.8 = (bf16[128,8192]{1,0:T(8,128)(2,1)S(1)}, bf16[128,8192]{1,0:T(8,128)(2,1)S(1)}, u32[]{:S(2)}, u32[]{:S(2)}) collective-permute-start(bf16[128,8192]{1,0:T(8,128)(2,1)S(1)} %collective-permute-done.7.refs_14_), channel_id=1, source_target_pairs={{0,2},{3,1},{4,6},{7,5},{8,10},{11,9},{12,14},{15,13},{16,18},{19,... | collective-permute-start | bytes 6291464 | tf_op jit(solution)/shard_map/ppermute | solution.py:370
  78.0 10.2 %copy-start.7 = (bf16[128,8192]{1,0:T(8,128)(2,1)}, bf16[128,8192]{1,0:T(8,128)(2,1)S(1)}, u32[]{:S(2)}) copy-start(bf16[128,8192]{1,0:T(8,128)(2,1)S(1)} %collective-permute-done.10.refs_18_) | copy-start | bytes 6291460
  78.0 8.8 %collective-permute-start.11 = (bf16[128,8192]{1,0:T(8,128)(2,1)S(1)}, bf16[128,8192]{1,0:T(8,128)(2,1)S(1)}, u32[]{:S(2)}, u32[]{:S(2)}) collective-permute-start(bf16[128,8192]{1,0:T(8,128)(2,1)S(1)} %collective-permute-done.10.refs_18_), channel_id=1, source_target_pairs={{0,2},{3,1},{4,6},{7,5},{8,10},{11,9},{12,14},{15,13},{16,18},{19,... | collective-permute-start | bytes 6291464 | tf_op jit(solution)/shard_map/ppermute | solution.py:370
  81.1 5.9 %copy-start.8 = (bf16[128,8192]{1,0:T(8,128)(2,1)}, bf16[128,8192]{1,0:T(8,128)(2,1)S(1)}, u32[]{:S(2)}) copy-start(bf16[128,8192]{1,0:T(8,128)(2,1)S(1)} %collective-permute-done.9.refs_17_) | copy-start | bytes 6291460
  86.9 1.3 copy-start.9
  88.3 38.8 %copy-start = (bf16[128,16384]{1,0:T(8,128)(2,1)S(1)}, bf16[128,16384]{1,0:T(8,128)(2,1)}, u32[]{:S(2)}) copy-start(bf16[128,16384]{1,0:T(8,128)(2,1)} %refs_1_.3) | copy-start | bytes 12582916
  122.3 35.2 %copy-start.3 = (bf16[128,4096]{1,0:T(8,128)(2,1)}, bf16[128,4096]{1,0:T(8,128)(2,1)S(1)}, u32[]{:S(2)}) copy-start(bf16[128,4096]{1,0:T(8,128)(2,1)S(1)} %get-tuple-element.23.kept) | copy-start | bytes 3145732
  122.3 37.1 %collective-permute-start.14 = (bf16[128,4096]{1,0:T(8,128)(2,1)S(1)}, bf16[128,4096]{1,0:T(8,128)(2,1)S(1)}, u32[]{:S(2)}, u32[]{:S(2)}) collective-permute-start(bf16[128,4096]{1,0:T(8,128)(2,1)S(1)} %get-tuple-element.24), channel_id=1, source_target_pairs={{2,0},{1,3},{0,1},{3,2},{6,4},{5,7},{4,5},{7,6},{10,8},{9,11},{8,9... | collective-permute-start | bytes 3145736 | tf_op jit(solution)/shard_map/ppermute | solution.py:370
  122.6 37.8 %collective-permute-start.15 = (bf16[128,4096]{1,0:T(8,128)(2,1)S(1)}, bf16[128,4096]{1,0:T(8,128)(2,1)}, u32[]{:S(2)}, u32[]{:S(2)}) collective-permute-start(bf16[128,4096]{1,0:T(8,128)(2,1)S(1)} %get-tuple-element.23.kept), channel_id=1, source_target_pairs={{1,2},{2,1},{5,6},{6,5},{9,10},{10,9},{13,14},{14,13},{17,18},{18,... | collective-permute-start | bytes 3145736 | tf_op jit(solution)/shard_map/ppermute | solution.py:370
  157.5 68.3 %copy-start.2 = (bf16[128,4096]{1,0:T(8,128)(2,1)}, bf16[128,4096]{1,0:T(8,128)(2,1)S(1)}, u32[]{:S(2)}) copy-start(bf16[128,4096]{1,0:T(8,128)(2,1)S(1)} %get-tuple-element.21.kept) | copy-start | bytes 3145732
  157.5 68.3 %collective-permute-start.12 = (bf16[128,4096]{1,0:T(8,128)(2,1)S(1)}, bf16[128,4096]{1,0:T(8,128)(2,1)}, u32[]{:S(2)}, u32[]{:S(2)}) collective-permute-start(bf16[128,4096]{1,0:T(8,128)(2,1)S(1)} %get-tuple-element.22), channel_id=1, source_target_pairs={{2,0},{1,3},{0,1},{3,2},{6,4},{5,7},{4,5},{7,6},{10,8},{9,11},{8,9... | collective-permute-start | bytes 3145736 | tf_op jit(solution)/shard_map/ppermute | solution.py:370
  157.5 68.3 %collective-permute-start.13 = (bf16[128,4096]{1,0:T(8,128)(2,1)S(1)}, bf16[128,4096]{1,0:T(8,128)(2,1)}, u32[]{:S(2)}, u32[]{:S(2)}) collective-permute-start(bf16[128,4096]{1,0:T(8,128)(2,1)S(1)} %get-tuple-element.21.kept), channel_id=1, source_target_pairs={{1,2},{2,1},{5,6},{6,5},{9,10},{10,9},{13,14},{14,13},{17,18},{18,... | collective-permute-start | bytes 3145736 | tf_op jit(solution)/shard_map/ppermute | solution.py:370
  159.4 1.0 copy-start.11

commit v2 on v0

--- a/solution.py
+++ b/solution.py
@@ -79,11 +79,11 @@
     count = len(sources)
     given = 1 + max(at for source in sources for at, _ in source)
     arrays, refs = refs[:given], refs[given:]
-    given, refs = refs[:8], refs[8:]
-    held_here, refs = refs[-8:], refs[:-8]
-    scales, w_latent, w_edge, w_agg, w_out_t, bias, gain, shift = held_here
-    table, latents, fine, total, earlier, later, scale_rows, slots, live, sems, given_sems = refs[-11:]
-    refs = refs[:-11]
+    given, refs = refs[:10], refs[10:]
+    held_here, refs = refs[-10:], refs[:-10]
+    scales, w_fine, w_node, w_edge, w_agg, w_out_t, edge_bias, node_bias, gain, shift = held_here
+    table, latents, fine, total, scale_rows, slots, live, sems, given_sems = refs[-9:]
+    refs = refs[:-9]
     fetches = [
         pltpu.make_async_copy(far if at else far.at[:, pl.ds(start, near.shape[1])], near, given_sems.at[at])
         for at, (far, near) in enumerate(zip(given, held_here))
@@ -134,14 +134,12 @@
 
     def begin(i):
         columns = pl.ds(pl.multiple_of(i * step, step), step)
-        first = dot(latents[:, columns], w_latent[...], 0, 0) + bias[...]
+        first = dot(latents[:, columns], w_fine[...], 0, 0) + edge_bias[...]
         return first, scales[:, pl.ds(pl.multiple_of(i * step, step), step)].T
 
     def keep(first, scale_columns):
-        width = first.shape[1] // 2
         fine[pl.ds(0, step, stride=2), :] = first[:, :128]
-        fine[pl.ds(1, step, stride=2), :] = first[:, 128:width]
-        later[...] = first[:, width:]
+        fine[pl.ds(1, step, stride=2), :] = first[:, 128:]
         scale_rows[pl.ds(0, step, stride=2), :] = scale_columns
         scale_rows[pl.ds(1, step, stride=2), :] = scale_columns
 
@@ -158,33 +156,27 @@
             acc = hidden if acc is None else acc + hidden
         return acc
 
-    def widened(ref):
-        return jnp.concatenate([ref[...]] * (step // 128), axis=1)
-
-    def finish(i, summed, own_part):
+    def finish(i, summed):
         at = pl.multiple_of(i * step, step)
+        own_part = dot(latents[:, pl.ds(at, step)], w_node[...], 0, 0)
         aggregate = dot(summed.astype(BF16), w_edge[...], 1, 0).astype(BF16)
         yield
-        node_hidden = jnp.maximum(own_part + dot(aggregate, w_agg[...], 1, 0), 0.0).astype(BF16)
+        node_hidden = dot(aggregate, w_agg[...], 1, 0) + own_part + node_bias[...]
+        node_hidden = jnp.maximum(node_hidden, 0.0).astype(BF16)
         yield
         output = dot(w_out_t[...], node_hidden, 1, 1)
-        yield
-        centered = output - jnp.mean(output, axis=0, keepdims=True)
-        spread = jnp.mean(centered * centered, axis=0, keepdims=True)
-        yield
-        normed = centered * lax.rsqrt(spread + 1e-05) * widened(gain) + widened(shift)
-        column = start + at + lax.broadcasted_iota(jnp.int32, (1, step), 1)
-        moved = jnp.where(column < live[0], normed, 0.0)
-        yield (latents[:, pl.ds(at, step)].astype(F32) + moved).astype(BF16)
-
-    def last(parts):
-        for value in parts:
-            pass
-        return value
-
-    def write(i, result):
-        for r in range(count):
-            outs[r][:, pl.ds(pl.multiple_of(i * step, step), step)] = result[r * features : (r + 1) * features]
+        for lane in range(0, step, 128):
+            yield
+            columns = pl.ds(pl.multiple_of(at + lane, 128), 128)
+            here = output[:, lane : lane + 128]
+            centered = here - jnp.mean(here, axis=0, keepdims=True)
+            spread = jnp.mean(centered * centered, axis=0, keepdims=True)
+            normed = centered * lax.rsqrt(spread + 1e-05) * gain[...] + shift[...]
+            column = start + at + lane + lax.broadcasted_iota(jnp.int32, (1, 128), 1)
+            moved = jnp.where(column < live[0], normed, 0.0)
+            result = (latents[:, columns].astype(F32) + moved).astype(BF16)
+            for r in range(count):
+                outs[r][:, columns] = result[r * features : (r + 1) * features]
 
     def gathered():
         return jnp.concatenate([total[pl.ds(0, step, stride=2), :], total[pl.ds(1, step, stride=2), :]], axis=1)
@@ -193,22 +185,21 @@
     keep(*begin(0))
 
     def one_step(i, carry):
-        before, after = jnp.maximum(i - 1, 0), jnp.minimum(i + 1, steps - 1)
-        summed, own_part, current = gathered(), earlier[...], later[...]
-        parts = finish(before, summed, own_part)
+        parts = finish(jnp.maximum(i - 1, 0), gathered())
+        begun = begin(jnp.minimum(i + 1, steps - 1))
         base = pl.multiple_of(i * (parents * step), parents * step)
-        begun = begin(after)
         for first in range(0, step // 4, GROUPS):
-            result = next(parts, None) if first < 4 * GROUPS else last(parts)
+            next(parts, None)
             sums = [group(base, g) for g in range(first, min(first + GROUPS, step // 4))]
             total[pl.ds(first * 8, len(sums) * 8), :] = jnp.concatenate(sums, axis=0)
-        write(before, result)
-        earlier[...] = current
+        for _ in parts:
+            pass
         keep(*begun)
         return carry
 
     lax.fori_loop(0, steps, one_step, 0)
-    write(steps - 1, last(finish(steps - 1, gathered(), earlier[...])))
+    for _ in finish(steps - 1, gathered()):
+        pass
     if segments is not None:
         move.wait()
 
@@ -227,9 +218,10 @@
     vmem = pl.BlockSpec(memory_space=pltpu.VMEM)
     smem = pl.BlockSpec(memory_space=pltpu.SMEM)
     far = pl.BlockSpec(memory_space=pltpu.HBM)
+    anywhere = pl.BlockSpec(memory_space=pl.ANY)
     out_shape = [jax.ShapeDtypeStruct((features, nodes), BF16)] * count
     operands = [places, by_step(aux, step), *arrays, scales, *params]
-    specs = [smem, far] + [far] * (len(arrays) + 1 + len(params))
+    specs = [smem, far] + [anywhere] * len(arrays) + [far] * (1 + len(params))
     scratch, table_step = [], 0
     if segments is None:
         operands, specs = operands + [table], specs + [far]
@@ -253,8 +245,6 @@
             pltpu.VMEM((count * features, nodes), BF16),
             pltpu.VMEM((2 * step, 128), F32),
             pltpu.VMEM((2 * step, 128), F32),
-            pltpu.VMEM((step, 256), F32),
-            pltpu.VMEM((step, 256), F32),
             pltpu.VMEM((2 * step, 8), F32),
             pltpu.SMEM((parents * nodes,), jnp.int32),
             pltpu.SMEM((1024,), jnp.int32),
@@ -432,11 +422,13 @@
         return jnp.concatenate(parts, axis=axis)
 
     params = (
-        jnp.concatenate([ordered(w_fine, 0), ordered(w_node_fine, 0)], axis=1),
+        ordered(w_fine, 0),
+        ordered(w_node_fine, 0),
         w_edge_out,
         w_node_agg,
         ordered(w_node_out, 1).T,
-        jnp.concatenate([edge_bias, node_bias])[None],
+        edge_bias[None],
+        node_bias[None],
         jnp.broadcast_to(ordered(norm_gain, 0)[:, None], (norm_gain.shape[0], 128)),
         jnp.broadcast_to(ordered(norm_bias, 0)[:, None], (norm_bias.shape[0], 128)),
     )

time: 183 us -> 184 us (level)
    unnamed x33 -> x37, local copies, waits for them, and re-layouts: 6.01 us -> 6.03 us
where the time goes in v2:
time: 184 us; the launch traced here: 181 us
  Pallas kernels  65.6 us (36%)
  waiting for transfers between devices  65.5 us (36%)
  starting transfers between devices  27.6 us (15%)
  local copies, waits for them, and re-layouts  12.6 us (7%)
  other arithmetic  8.66 us (5%)
    pallas_call x2, Pallas kernels, update(): pl.pallas_call(functools.partial(update_kernel, sources, step, start, seg...  65.6 us
    ppermute x14, waiting for transfers between devices, send(): return lax.ppermute(value, ('dom', 'feat'), perm)  56.7 us
    ppermute x14, starting transfers between devices, send(): return lax.ppermute(value, ('dom', 'feat'), perm)  18.9 us
    ppermute x2, waiting for transfers between devices, halo(): return lax.ppermute(value, ('dom', 'feat'), perm)  8.79 us
    ppermute x2, starting transfers between devices, halo(): return lax.ppermute(value, ('dom', 'feat'), perm)  8.65 us
    unnamed x37, local copies, waits for them, and re-layouts  6.03 us
    dynamic_slice x1, local copies, waits for them, and re-layouts, cut(): return lax.dynamic_slice_in_dim(array, at, size, 1)  4.06 us
  transfers between devices with their start and end apart: 16, of which 5 were waited for; matrix products, arithmetic and copies ran while one was open for 8% of the time, Pallas kernels for 36%

profile of v2, /device:TPU:1, one launch (start us, length us, event | category | flops | bytes accessed | tf_op | source)
XLA Modules:
  0.0 181.3 jit_solution(10546393849657618049)
XLA Ops:
  0.0 2.1 %collective-permute-start.1 = (bf16[128,8192]{1,0:T(8,128)(2,1)}, bf16[128,8192]{1,0:T(8,128)(2,1)}, u32[]{:S(2)}, u32[]{:S(2)}) collective-permute-start(bf16[128,8192]{1,0:T(8,128)(2,1)} %refs_14_.1), channel_id=1, source_target_pairs={{0,1},{1,0},{2,3},{3,2},{4,5},{5,4},{6,7},{7,6},{8,9},{9,8},{10,11... | collective-permute-start | bytes 6291464 | tf_op jit(solution)/shard_map/ppermute | solution.py:323
  2.1 4.1 %collective-permute-start.5 = (bf16[128,8192]{1,0:T(8,128)(2,1)}, bf16[128,8192]{1,0:T(8,128)(2,1)S(1)}, u32[]{:S(2)}, u32[]{:S(2)}) collective-permute-start(bf16[128,8192]{1,0:T(8,128)(2,1)} %refs_14_.1), channel_id=1, source_target_pairs={{2,4},{6,8},{10,12},{14,16},{18,20},{22,24},{26,28},{5,3},{9,7},{1... | collective-permute-start | bytes 6291464 | tf_op jit(solution)/shard_map/ppermute | solution.py:334
  6.9 1.0 multiply_add_fusion
  8.0 0.8 copy-done.8
  8.7 1.9 %fusion = f32[9,8192]{1,0:T(8,128)} fusion(s32[]{:T(128)S(6)} %select_n.168, f32[5,16384]{1,0:T(8,128)S(1)} %pad_convert_fusion, f32[4,16384]{1,0:T(4,128)} %param.18), kind=kLoop, calls=%fused_computation.8 | loop fusion | flops 73728 | bytes 884740 | tf_op jit(solution)/shard_map/concatenate | solution.py:371
  10.6 1.3 collective-permute-start
  12.0 0.9 constant_dynamic-slice_fusion.5
  12.9 0.1 copy.21
  13.0 0.1 copy.22
  13.2 0.1 stack.23.places
  13.2 0.8 broadcast_select_fusion.7
  14.1 0.9 constant_dynamic-slice_fusion.3
  15.0 0.1 broadcast_select_fusion.3
  15.2 0.0 copy-start.1
  15.2 4.1 %constant_dynamic-slice_fusion = (bf16[128,4096]{1,0:T(8,128)(2,1)}, bf16[128,4096]{1,0:T(8,128)(2,1)}, bf16[128,4096]{1,0:T(8,128)(2,1)S(1)}, bf16[128,4096]{1,0:T(8,128)(2,1)S(1)}) fusion(bf16[128,16384]{1,0:T(8,128)(2,1)} %refs_1_.3, s32[]{:T(128)S(6)} %select_n.193, s32[]{:T(128)S(6)} %select_n.192, s32[]{:T(128)S(6)} %select_n.168, s32[]{:T(128)S(6)} %select_n.171), kind=kLoop, calls=%fused_computation.33 | loop fusion | bytes 8388624 | tf_op jit(solution)/shard_map/dynamic_slice | solution.py:271
  19.2 0.0 copy-start.7
  19.3 28.4 %collective-permute-done.1.refs_18_ = bf16[128,8192]{1,0:T(8,128)(2,1)} collective-permute-done((bf16[128,8192]{1,0:T(8,128)(2,1)}, bf16[128,8192]{1,0:T(8,128)(2,1)}, u32[]{:S(2)}, u32[]{:S(2)}) %collective-permute-start.1) | collective-permute-done | bytes 2097184 | tf_op jit(solution)/shard_map/ppermute | solution.py:323
  47.7 4.6 %collective-permute-start.8 = (bf16[128,8192]{1,0:T(8,128)(2,1)}, bf16[128,8192]{1,0:T(8,128)(2,1)S(1)}, u32[]{:S(2)}, u32[]{:S(2)}) collective-permute-start(bf16[128,8192]{1,0:T(8,128)(2,1)} %collective-permute-done.1.refs_18_), channel_id=1, source_target_pairs={{2,4},{6,8},{10,12},{14,16},{18,20},{22,24},{26,28},{5,3},{9,7},{1... | collective-permute-start | bytes 6291464 | tf_op jit(solution)/shard_map/ppermute | solution.py:334
  52.4 1.3 fusion.2
  53.6 0.0 collective-permute-start.2
  53.7 1.9 %collective-permute-start.3 = (bf16[128,4096]{1,0:T(8,128)(2,1)S(1)}, bf16[128,4096]{1,0:T(8,128)(2,1)S(1)}, u32[]{:S(2)}, u32[]{:S(2)}) collective-permute-start(bf16[128,4096]{1,0:T(8,128)(2,1)S(1)} %get-tuple-element.16), channel_id=1, source_target_pairs={{1,2},{2,1},{5,6},{6,5},{9,10},{10,9},{13,14},{14,13},{17,18},{18,... | collective-permute-start | bytes 3145736 | tf_op jit(solution)/shard_map/ppermute | solution.py:323
  55.6 0.1 collective-permute-start.4
  55.7 0.5 collective-permute-start.7
  56.2 9.2 %collective-permute-done.2.refs_0_ = bf16[128,4096]{1,0:T(8,128)(2,1)S(1)} collective-permute-done((bf16[128,4096]{1,0:T(8,128)(2,1)S(1)}, bf16[128,4096]{1,0:T(8,128)(2,1)S(1)}, u32[]{:S(2)}, u32[]{:S(2)}) %collective-permute-start.2) | collective-permute-done | bytes 1048608 | tf_op jit(solution)/shard_map/ppermute | solution.py:323
  65.4 1.3 collective-permute-start.6
  66.7 8.8 %collective-permute-done.8.refs_20_ = bf16[128,8192]{1,0:T(8,128)(2,1)S(1)} collective-permute-done((bf16[128,8192]{1,0:T(8,128)(2,1)}, bf16[128,8192]{1,0:T(8,128)(2,1)S(1)}, u32[]{:S(2)}, u32[]{:S(2)}) %collective-permute-start.8) | collective-permute-done | bytes 2097184 | tf_op jit(solution)/shard_map/ppermute | solution.py:334
  75.5 1.3 collective-permute-start.9
  76.9 0.1 copy.23
  77.0 1.7 collective-permute-start.12
  78.7 3.1 %collective-permute-start.13 = (bf16[128,4096]{1,0:T(8,128)(2,1)}, bf16[128,4096]{1,0:T(8,128)(2,1)}, u32[]{:S(2)}, u32[]{:S(2)}) collective-permute-start(bf16[128,4096]{1,0:T(8,128)(2,1)} %get-tuple-element.21), channel_id=1, source_target_pairs={{1,2},{2,1},{5,6},{6,5},{9,10},{10,9},{13,14},{14,13},{17,18},{18,... | collective-permute-start | bytes 3145736 | tf_op jit(solution)/shard_map/ppermute | solution.py:323
  81.9 0.1 broadcast_in_dim.32.refs_11_
  82.0 0.1 broadcast_in_dim.33.refs_12_
  82.1 1.1 copy-done.12
  83.2 0.7 copy-done.13
  83.9 34.9 %shard_map.145 = (bf16[128,4096]{1,0:T(8,128)(2,1)}, bf16[128,4096]{1,0:T(8,128)(2,1)S(1)}, f32[49168,128]{1,0:T(8,128)}) custom-call(s32[5]{0:T(128)S(1)} %stack.23.places, s32[40960]{0:T(1024)S(1)} %pad_add_fusion.aux, bf16[128,4096]{1,0:T(8,128)(2,1)S(1)} %collective-permute-done.2.refs_0_, bf16[128,16384]{1,0:T(8,128)(2,1)} %refs_1_.3, ...), custom_call_target="tpu_custom_call" | custom-call | flops 2867200000 | bytes 8388608 | tf_op jit(solution)/shard_map/pallas_call | solution.py:237
  118.7 1.0 copy-done.2
  119.7 2.5 %collective-permute-start.11 = (bf16[128,4096]{1,0:T(8,128)(2,1)}, bf16[128,4096]{1,0:T(8,128)(2,1)S(1)}, u32[]{:S(2)}, u32[]{:S(2)}) collective-permute-start(bf16[128,4096]{1,0:T(8,128)(2,1)} %copy-done.2), channel_id=1, source_target_pairs={{1,2},{2,1},{5,6},{6,5},{9,10},{10,9},{13,14},{14,13},{17,18},{18,... | collective-permute-start | bytes 3145736 | tf_op jit(solution)/shard_map/ppermute | solution.py:323
  122.2 2.2 %copy-done = bf16[128,16384]{1,0:T(8,128)(2,1)S(1)} copy-done((bf16[128,16384]{1,0:T(8,128)(2,1)S(1)}, bf16[128,16384]{1,0:T(8,128)(2,1)}, u32[]{:S(2)}) %copy-start) | copy-done | bytes 4194328
  124.4 30.7 %shard_map.146 = (bf16[128,4096]{1,0:T(8,128)(2,1)S(1)}, bf16[128,4096]{1,0:T(8,128)(2,1)S(1)}) custom-call(s32[5]{0:T(128)S(1)} %stack.23.places, s32[40960]{0:T(1024)S(1)} %pad_add_fusion.aux, bf16[128,4096]{1,0:T(8,128)(2,1)} %collective-permute-done.12.refs_0_, bf16[128,16384]{1,0:T(8,128)(2,1)S(1)} %copy-done, ...), custom_call_target="tpu_custom_call" | custom-call | flops 2867200000 | bytes 8388608 | tf_op jit(solution)/shard_map/pallas_call | solution.py:237
  155.1 0.0 collective-permute-start.14
  155.2 3.2 %collective-permute-start.15 = (bf16[128,4096]{1,0:T(8,128)(2,1)S(1)}, bf16[128,4096]{1,0:T(8,128)(2,1)S(1)}, u32[]{:S(2)}, u32[]{:S(2)}) collective-permute-start(bf16[128,4096]{1,0:T(8,128)(2,1)S(1)} %get-tuple-element.23), channel_id=1, source_target_pairs={{1,2},{2,1},{5,6},{6,5},{9,10},{10,9},{13,14},{14,13},{17,18},{18,... | collective-permute-start | bytes 3145736 | tf_op jit(solution)/shard_map/ppermute | solution.py:323
  158.4 0.4 broadcast_in_dim.12
  158.8 1.5 select_dynamic-update-slice_fusion.3
  160.4 0.3 select_dynamic-update-slice_fusion.2
  160.7 16.6 %collective-permute-done.14 = bf16[128,4096]{1,0:T(8,128)(2,1)S(1)} collective-permute-done((bf16[128,4096]{1,0:T(8,128)(2,1)S(1)}, bf16[128,4096]{1,0:T(8,128)(2,1)S(1)}, u32[]{:S(2)}, u32[]{:S(2)}) %collective-permute-start.14) | collective-permute-done | bytes 1048608 | tf_op jit(solution)/shard_map/ppermute | solution.py:323
  177.4 0.3 select_dynamic-update-slice_fusion.1
  177.7 2.4 %collective-permute-done.15 = bf16[128,4096]{1,0:T(8,128)(2,1)S(1)} collective-permute-done((bf16[128,4096]{1,0:T(8,128)(2,1)S(1)}, bf16[128,4096]{1,0:T(8,128)(2,1)S(1)}, u32[]{:S(2)}, u32[]{:S(2)}) %collective-permute-start.15) | collective-permute-done | bytes 1048608 | tf_op jit(solution)/shard_map/ppermute | solution.py:323
  180.1 1.2 select_dynamic-update-slice_fusion
  (54 shorter events, 0.4 us)
Async XLA Ops:
  0.0 15.0 %copy-start.16 = (bf16[256,256]{1,0:T(8,128)(2,1)S(1)}, bf16[256,256]{1,0:T(8,128)(2,1)}, u32[]{:S(2)}) copy-start(bf16[256,256]{1,0:T(8,128)(2,1)} %param.20) | copy-start | bytes 393220
  0.0 15.0 %copy-start.15 = (bf16[256,256]{1,0:T(8,128)(2,1)S(1)}, bf16[256,256]{1,0:T(8,128)(2,1)}, u32[]{:S(2)}) copy-start(bf16[256,256]{1,0:T(8,128)(2,1)} %param.23) | copy-start | bytes 393220
  0.0 47.7 %collective-permute-start.1 = (bf16[128,8192]{1,0:T(8,128)(2,1)}, bf16[128,8192]{1,0:T(8,128)(2,1)}, u32[]{:S(2)}, u32[]{:S(2)}) collective-permute-start(bf16[128,8192]{1,0:T(8,128)(2,1)} %refs_14_.1), channel_id=1, source_target_pairs={{0,1},{1,0},{2,3},{3,2},{4,5},{5,4},{6,7},{7,6},{8,9},{9,8},{10,11... | collective-permute-start | bytes 6291464 | tf_op jit(solution)/shard_map/ppermute | solution.py:323
  2.1 53.6 %collective-permute-start.5 = (bf16[128,8192]{1,0:T(8,128)(2,1)}, bf16[128,8192]{1,0:T(8,128)(2,1)S(1)}, u32[]{:S(2)}, u32[]{:S(2)}) collective-permute-start(bf16[128,8192]{1,0:T(8,128)(2,1)} %refs_14_.1), channel_id=1, source_target_pairs={{2,4},{6,8},{10,12},{14,16},{18,20},{22,24},{26,28},{5,3},{9,7},{1... | collective-permute-start | bytes 6291464 | tf_op jit(solution)/shard_map/ppermute | solution.py:334
  8.0 0.8 copy-start.8
  10.6 41.7 %collective-permute-start = (f32[9,8192]{1,0:T(8,128)}, f32[9,8192]{1,0:T(8,128)}, u32[]{:S(2)}, u32[]{:S(2)}) collective-permute-start(f32[9,8192]{1,0:T(8,128)} %fusion), channel_id=1, source_target_pairs={{0,2},{3,1},{4,6},{7,5},{8,10},{11,9},{12,14},{15,13},{16,18},{19,... | collective-permute-start | bytes 884744 | tf_op jit(solution)/shard_map/ppermute | solution.py:323
  15.1 37.2 %copy-start.9 = (f32[5,16384]{1,0:T(8,128)S(1)}, f32[5,16384]{1,0:T(8,128)}, u32[]{:S(2)}) copy-start(f32[5,16384]{1,0:T(8,128)} %copy-done.8) | copy-start | bytes 983044
  15.1 37.2 %copy-start.14 = (f32[4,16384]{1,0:T(4,128)S(1)}, f32[4,16384]{1,0:T(4,128)}, u32[]{:S(2)}) copy-start(f32[4,16384]{1,0:T(4,128)} %param.18) | copy-start | bytes 786436
  15.2 40.5 %copy-start.1 = (bf16[128,8192]{1,0:T(8,128)(2,1)S(1)}, bf16[128,8192]{1,0:T(8,128)(2,1)}, u32[]{:S(2)}) copy-start(bf16[128,8192]{1,0:T(8,128)(2,1)} %refs_14_.1) | copy-start | bytes 6291460
  19.2 64.6 %copy-start.4 = (bf16[256,256]{1,0:T(8,128)(2,1)S(1)}, bf16[256,256]{1,0:T(8,128)(2,1)}, u32[]{:S(2)}) copy-start(bf16[256,256]{1,0:T(8,128)(2,1)} %refs_6_.3) | copy-start | bytes 393220
  19.2 64.6 %copy-start.5 = (bf16[256,256]{1,0:T(8,128)(2,1)S(1)}, bf16[256,256]{1,0:T(8,128)(2,1)}, u32[]{:S(2)}) copy-start(bf16[256,256]{1,0:T(8,128)(2,1)} %refs_7_.3) | copy-start | bytes 393220
  19.2 64.6 %copy-start.6 = (f32[256]{0:T(256)S(1)}, f32[256]{0:T(256)}, u32[]{:S(2)}) copy-start(f32[256]{0:T(256)} %param.26) | copy-start | bytes 3076
  19.2 64.6 %copy-start.7 = (f32[256]{0:T(256)S(1)}, f32[256]{0:T(256)}, u32[]{:S(2)}) copy-start(f32[256]{0:T(256)} %param.27) | copy-start | bytes 3076
  47.7 27.7 %collective-permute-start.8 = (bf16[128,8192]{1,0:T(8,128)(2,1)}, bf16[128,8192]{1,0:T(8,128)(2,1)S(1)}, u32[]{:S(2)}, u32[]{:S(2)}) collective-permute-start(bf16[128,8192]{1,0:T(8,128)(2,1)} %collective-permute-done.1.refs_18_), channel_id=1, source_target_pairs={{2,4},{6,8},{10,12},{14,16},{18,20},{22,24},{26,28},{5,3},{9,7},{1... | collective-permute-start | bytes 6291464 | tf_op jit(solution)/shard_map/ppermute | solution.py:334
  53.6 11.8 %collective-permute-start.2 = (bf16[128,4096]{1,0:T(8,128)(2,1)S(1)}, bf16[128,4096]{1,0:T(8,128)(2,1)S(1)}, u32[]{:S(2)}, u32[]{:S(2)}) collective-permute-start(bf16[128,4096]{1,0:T(8,128)(2,1)S(1)} %get-tuple-element.15), channel_id=1, source_target_pairs={{0,2},{3,1},{1,0},{2,3},{4,6},{7,5},{5,4},{6,7},{8,10},{11,9},{9,8... | collective-permute-start | bytes 3145736 | tf_op jit(solution)/shard_map/ppermute | solution.py:323
  53.7 23.3 %collective-permute-start.3 = (bf16[128,4096]{1,0:T(8,128)(2,1)S(1)}, bf16[128,4096]{1,0:T(8,128)(2,1)S(1)}, u32[]{:S(2)}, u32[]{:S(2)}) collective-permute-start(bf16[128,4096]{1,0:T(8,128)(2,1)S(1)} %get-tuple-element.16), channel_id=1, source_target_pairs={{1,2},{2,1},{5,6},{6,5},{9,10},{10,9},{13,14},{14,13},{17,18},{18,... | collective-permute-start | bytes 3145736 | tf_op jit(solution)/shard_map/ppermute | solution.py:323
  55.6 23.1 %collective-permute-start.4 = (bf16[128,8192]{1,0:T(8,128)(2,1)S(1)}, bf16[128,8192]{1,0:T(8,128)(2,1)S(1)}, u32[]{:S(2)}, u32[]{:S(2)}) collective-permute-start(bf16[128,8192]{1,0:T(8,128)(2,1)S(1)} %copy-done.1), channel_id=1, source_target_pairs={{0,2},{1,3},{2,0},{3,1},{4,6},{5,7},{6,4},{7,5},{8,10},{9,11},{10,... | collective-permute-start | bytes 6291464 | tf_op jit(solution)/shard_map/ppermute | solution.py:323
  55.7 26.1 %collective-permute-start.7 = (bf16[128,8192]{1,0:T(8,128)(2,1)}, bf16[128,8192]{1,0:T(8,128)(2,1)S(1)}, u32[]{:S(2)}, u32[]{:S(2)}) collective-permute-start(bf16[128,8192]{1,0:T(8,128)(2,1)} %collective-permute-done.1.refs_18_), channel_id=1, source_target_pairs={{0,2},{1,3},{2,0},{3,1},{4,6},{5,7},{6,4},{7,5},{8,10},{9,11},{10,... | collective-permute-start | bytes 6291464 | tf_op jit(solution)/shard_map/ppermute | solution.py:323
  65.4 16.5 %collective-permute-start.6 = (bf16[128,8192]{1,0:T(8,128)(2,1)S(1)}, bf16[128,8192]{1,0:T(8,128)(2,1)S(1)}, u32[]{:S(2)}, u32[]{:S(2)}) collective-permute-start(bf16[128,8192]{1,0:T(8,128)(2,1)S(1)} %collective-permute-done.5.refs_16_), channel_id=1, source_target_pairs={{0,2},{3,1},{4,6},{7,5},{8,10},{11,9},{12,14},{15,13},{16,18},{19,... | collective-permute-start | bytes 6291464 | tf_op jit(solution)/shard_map/ppermute | solution.py:323
  75.5 6.6 %copy-start.11 = (bf16[128,8192]{1,0:T(8,128)(2,1)}, bf16[128,8192]{1,0:T(8,128)(2,1)S(1)}, u32[]{:S(2)}) copy-start(bf16[128,8192]{1,0:T(8,128)(2,1)S(1)} %collective-permute-done.8.refs_20_) | copy-start | bytes 6291460
  75.5 6.4 %collective-permute-start.9 = (bf16[128,8192]{1,0:T(8,128)(2,1)S(1)}, bf16[128,8192]{1,0:T(8,128)(2,1)S(1)}, u32[]{:S(2)}, u32[]{:S(2)}) collective-permute-start(bf16[128,8192]{1,0:T(8,128)(2,1)S(1)} %collective-permute-done.8.refs_20_), channel_id=1, source_target_pairs={{0,2},{3,1},{4,6},{7,5},{8,10},{11,9},{12,14},{15,13},{16,18},{19,... | collective-permute-start | bytes 6291464 | tf_op jit(solution)/shard_map/ppermute | solution.py:323
  77.0 45.2 %collective-permute-start.12 = (bf16[128,4096]{1,0:T(8,128)(2,1)}, bf16[128,4096]{1,0:T(8,128)(2,1)}, u32[]{:S(2)}, u32[]{:S(2)}) collective-permute-start(bf16[128,4096]{1,0:T(8,128)(2,1)} %get-tuple-element.20), channel_id=1, source_target_pairs={{0,2},{3,1},{1,0},{2,3},{4,6},{7,5},{5,4},{6,7},{8,10},{11,9},{9,8... | collective-permute-start | bytes 3145736 | tf_op jit(solution)/shard_map/ppermute | solution.py:323
  78.7 43.5 %collective-permute-start.13 = (bf16[128,4096]{1,0:T(8,128)(2,1)}, bf16[128,4096]{1,0:T(8,128)(2,1)}, u32[]{:S(2)}, u32[]{:S(2)}) collective-permute-start(bf16[128,4096]{1,0:T(8,128)(2,1)} %get-tuple-element.21), channel_id=1, source_target_pairs={{1,2},{2,1},{5,6},{6,5},{9,10},{10,9},{13,14},{14,13},{17,18},{18,... | collective-permute-start | bytes 3145736 | tf_op jit(solution)/shard_map/ppermute | solution.py:323
  81.8 1.3 copy-start.12
  81.9 2.0 %copy-start.13 = (bf16[128,8192]{1,0:T(8,128)(2,1)}, bf16[128,8192]{1,0:T(8,128)(2,1)S(1)}, u32[]{:S(2)}) copy-start(bf16[128,8192]{1,0:T(8,128)(2,1)S(1)} %collective-permute-done.9.refs_21_) | copy-start | bytes 6291460
  118.7 1.0 copy-start.2
  119.7 38.7 %collective-permute-start.10 = (bf16[128,4096]{1,0:T(8,128)(2,1)}, bf16[128,4096]{1,0:T(8,128)(2,1)}, u32[]{:S(2)}, u32[]{:S(2)}) collective-permute-start(bf16[128,4096]{1,0:T(8,128)(2,1)} %get-tuple-element.19), channel_id=1, source_target_pairs={{2,0},{1,3},{0,1},{3,2},{6,4},{5,7},{4,5},{7,6},{10,8},{9,11},{8,9... | collective-permute-start | bytes 3145736 | tf_op jit(solution)/shard_map/ppermute | solution.py:323
  119.7 40.7 %collective-permute-start.11 = (bf16[128,4096]{1,0:T(8,128)(2,1)}, bf16[128,4096]{1,0:T(8,128)(2,1)S(1)}, u32[]{:S(2)}, u32[]{:S(2)}) collective-permute-start(bf16[128,4096]{1,0:T(8,128)(2,1)} %copy-done.2), channel_id=1, source_target_pairs={{1,2},{2,1},{5,6},{6,5},{9,10},{10,9},{13,14},{14,13},{17,18},{18,... | collective-permute-start | bytes 3145736 | tf_op jit(solution)/shard_map/ppermute | solution.py:323
  122.2 2.2 %copy-start = (bf16[128,16384]{1,0:T(8,128)(2,1)S(1)}, bf16[128,16384]{1,0:T(8,128)(2,1)}, u32[]{:S(2)}) copy-start(bf16[128,16384]{1,0:T(8,128)(2,1)} %refs_1_.3) | copy-start | bytes 12582916
  155.1 3.7 %copy-start.3 = (bf16[128,4096]{1,0:T(8,128)(2,1)S(1)}, bf16[128,4096]{1,0:T(8,128)(2,1)}, u32[]{:S(2)}) copy-start(bf16[128,4096]{1,0:T(8,128)(2,1)} %copy-done.2) | copy-start | bytes 3145732
  155.1 22.2 %collective-permute-start.14 = (bf16[128,4096]{1,0:T(8,128)(2,1)S(1)}, bf16[128,4096]{1,0:T(8,128)(2,1)S(1)}, u32[]{:S(2)}, u32[]{:S(2)}) collective-permute-start(bf16[128,4096]{1,0:T(8,128)(2,1)S(1)} %get-tuple-element.24), channel_id=1, source_target_pairs={{2,0},{1,3},{0,1},{3,2},{6,4},{5,7},{4,5},{7,6},{10,8},{9,11},{8,9... | collective-permute-start | bytes 3145736 | tf_op jit(solution)/shard_map/ppermute | solution.py:323
  155.2 24.9 %collective-permute-start.15 = (bf16[128,4096]{1,0:T(8,128)(2,1)S(1)}, bf16[128,4096]{1,0:T(8,128)(2,1)S(1)}, u32[]{:S(2)}, u32[]{:S(2)}) collective-permute-start(bf16[128,4096]{1,0:T(8,128)(2,1)S(1)} %get-tuple-element.23), channel_id=1, source_target_pairs={{1,2},{2,1},{5,6},{6,5},{9,10},{10,9},{13,14},{14,13},{17,18},{18,... | collective-permute-start | bytes 3145736 | tf_op jit(solution)/shard_map/ppermute | solution.py:323
  177.7 2.4 %copy-start.10 = (bf16[128,16384]{1,0:T(8,128)(2,1)}, bf16[128,16384]{1,0:T(8,128)(2,1)S(1)}, u32[]{:S(2)}) copy-start(bf16[128,16384]{1,0:T(8,128)(2,1)S(1)} %select_dynamic-update-slice_fusion.1) | copy-start | bytes 12582916

commit v3 on v0

--- a/solution.py
+++ b/solution.py
@@ -150,12 +150,16 @@
         scale = scale_rows[pl.ds(g * 8, 8), :]
         acc = None
         for k in range(parents):
-            rows = None
+            low = high = None
             for j in range(4):
-                loaded = table[pl.ds(slots[at + (k * step + g * 4 + j)], 8), :]
-                rows = loaded if rows is None else jnp.where(owns[j], loaded, rows)
-            hidden = jnp.maximum(part + rows, 0.0) * scale[:, k : k + 1]
-            acc = hidden if acc is None else acc + hidden
+                word = slots[at + (k * step + g * 4 + j)]
+                loaded = table[pl.ds(word & 0xFFFF, 8), :]
+                low = loaded if low is None else jnp.where(owns[j], loaded, low)
+                loaded = table[pl.ds(lax.shift_right_logical(word, 16), 8), :]
+                high = loaded if high is None else jnp.where(owns[j], loaded, high)
+            for way, rows in ((2 * k, low), (2 * k + 1, high)):
+                hidden = jnp.maximum(part + rows, 0.0) * scale[:, way : way + 1]
+                acc = hidden if acc is None else acc + hidden
         return acc
 
     def widened(ref):
@@ -222,6 +226,7 @@
     start, nodes, aux, arrays, sources, scales, params, places, table=None, segments=None, w_parent=None, coarse=()
 ):
     count, features = len(sources), arrays[0].shape[0]
+    aux = jnp.concatenate([aux[0:-1:2] | (aux[1:-1:2] << 16), aux[-1:]])
     parents = aux.shape[0] - 1
     step = min(STEP, nodes)
     vmem = pl.BlockSpec(memory_space=pltpu.VMEM)

time: 183 us -> 185 us (1.011)
  waiting for transfers between devices: 65.9 us -> 63 us
  starting transfers between devices: 27.6 us -> 30.1 us
    ppermute x2, starting transfers between devices: 8.65 us -> 11.1 us  [halo(): return lax.ppermute(value, ('dom', 'feat'), perm)]
    unnamed x33 -> x35, local copies, waits for them, and re-layouts: 6.01 us -> 5.24 us
  transfers between devices with their start and end apart: 16 -> 16, of which waited for: 5 -> 6; matrix products, arithmetic and copies ran while one was open for 8% -> 9% of each run, Pallas kernels for 36% -> 36%
where the time goes in v3:
time: 185 us; the launch traced here: 182 us
  Pallas kernels  65.8 us (36%)
  waiting for transfers between devices  63 us (34%)
  starting transfers between devices  30.1 us (16%)
  local copies, waits for them, and re-layouts  14.4 us (8%)
  other arithmetic  7.97 us (4%)
    pallas_call x2, Pallas kernels, update(): pl.pallas_call(functools.partial(update_kernel, sources, step, start, seg...  65.8 us
    ppermute x14, waiting for transfers between devices, send(): return lax.ppermute(value, ('dom', 'feat'), perm)  55.6 us
    ppermute x14, starting transfers between devices, send(): return lax.ppermute(value, ('dom', 'feat'), perm)  19 us
    ppermute x2, starting transfers between devices, halo(): return lax.ppermute(value, ('dom', 'feat'), perm)  11.1 us
    ppermute x2, waiting for transfers between devices, halo(): return lax.ppermute(value, ('dom', 'feat'), perm)  7.39 us
    unnamed x35, local copies, waits for them, and re-layouts  5.24 us
    dynamic_slice x1, local copies, waits for them, and re-layouts, cut(): return lax.dynamic_slice_in_dim(array, at, size, 1)  4.45 us
  transfers between devices with their start and end apart: 16, of which 6 were waited for; matrix products, arithmetic and copies ran while one was open for 9% of the time, Pallas kernels for 36%

profile of v3, /device:TPU:1, one launch (start us, length us, event | category | flops | bytes accessed | tf_op | source)
XLA Modules:
  0.0 182.5 jit_solution(10368787365337924509)
XLA Ops:
  0.0 2.1 %collective-permute-start.1 = (bf16[128,8192]{1,0:T(8,128)(2,1)}, bf16[128,8192]{1,0:T(8,128)(2,1)}, u32[]{:S(2)}, u32[]{:S(2)}) collective-permute-start(bf16[128,8192]{1,0:T(8,128)(2,1)} %refs_12_.1), channel_id=1, source_target_pairs={{0,1},{1,0},{2,3},{3,2},{4,5},{5,4},{6,7},{7,6},{8,9},{9,8},{10,11... | collective-permute-start | bytes 6291464 | tf_op jit(solution)/shard_map/ppermute | solution.py:338
  2.2 5.3 %collective-permute-start.5 = (bf16[128,8192]{1,0:T(8,128)(2,1)}, bf16[128,8192]{1,0:T(8,128)(2,1)}, u32[]{:S(2)}, u32[]{:S(2)}) collective-permute-start(bf16[128,8192]{1,0:T(8,128)(2,1)} %refs_12_.1), channel_id=1, source_target_pairs={{2,4},{6,8},{10,12},{14,16},{18,20},{22,24},{26,28},{5,3},{9,7},{1... | collective-permute-start | bytes 6291464 | tf_op jit(solution)/shard_map/ppermute | solution.py:349
  8.2 1.0 multiply_add_fusion
  9.3 1.9 %fusion = f32[9,8192]{1,0:T(8,128)} fusion(s32[]{:T(128)S(6)} %select_n.168, f32[5,16384]{1,0:T(8,128)S(1)} %pad_convert_fusion, f32[4,16384]{1,0:T(4,128)} %param.18), kind=kLoop, calls=%fused_computation.8 | loop fusion | flops 73728 | bytes 884740 | tf_op jit(solution)/shard_map/concatenate | solution.py:386
  11.2 1.3 collective-permute-start
  12.5 0.9 constant_dynamic-slice_fusion.5
  13.4 0.1 copy.21
  13.5 0.1 copy.22
  13.7 0.9 constant_dynamic-slice_fusion.3
  14.6 0.1 broadcast_select_fusion.7
  14.8 4.4 %constant_dynamic-slice_fusion = (bf16[128,4096]{1,0:T(8,128)(2,1)}, bf16[128,4096]{1,0:T(8,128)(2,1)}, bf16[128,4096]{1,0:T(8,128)(2,1)}, bf16[128,4096]{1,0:T(8,128)(2,1)}) fusion(bf16[128,16384]{1,0:T(8,128)(2,1)} %refs_1_.3, s32[]{:T(128)S(6)} %select_n.193, s32[]{:T(128)S(6)} %select_n.192, s32[]{:T(128)S(6)} %select_n.168, s32[]{:T(128)S(6)} %select_n.171), kind=kLoop, calls=%fused_computation.33 | loop fusion | bytes 8388624 | tf_op jit(solution)/shard_map/dynamic_slice | solution.py:286
  19.3 0.1 stack.23.places
  19.4 0.1 broadcast_select_fusion.3
  19.5 1.3 fusion.2
  20.8 27.1 %collective-permute-done.1.refs_16_ = bf16[128,8192]{1,0:T(8,128)(2,1)} collective-permute-done((bf16[128,8192]{1,0:T(8,128)(2,1)}, bf16[128,8192]{1,0:T(8,128)(2,1)}, u32[]{:S(2)}, u32[]{:S(2)}) %collective-permute-start.1) | collective-permute-done | bytes 2097184 | tf_op jit(solution)/shard_map/ppermute | solution.py:338
  47.8 5.8 %collective-permute-start.8 = (bf16[128,8192]{1,0:T(8,128)(2,1)}, bf16[128,8192]{1,0:T(8,128)(2,1)}, u32[]{:S(2)}, u32[]{:S(2)}) collective-permute-start(bf16[128,8192]{1,0:T(8,128)(2,1)} %collective-permute-done.1.refs_16_), channel_id=1, source_target_pairs={{2,4},{6,8},{10,12},{14,16},{18,20},{22,24},{26,28},{5,3},{9,7},{1... | collective-permute-start | bytes 6291464 | tf_op jit(solution)/shard_map/ppermute | solution.py:349
  53.6 0.6 slice.22
  54.2 0.6 slice.23
  54.8 0.0 collective-permute-start.2
  54.9 1.9 %collective-permute-start.3 = (bf16[128,4096]{1,0:T(8,128)(2,1)}, bf16[128,4096]{1,0:T(8,128)(2,1)S(1)}, u32[]{:S(2)}, u32[]{:S(2)}) collective-permute-start(bf16[128,4096]{1,0:T(8,128)(2,1)} %get-tuple-element.16), channel_id=1, source_target_pairs={{1,2},{2,1},{5,6},{6,5},{9,10},{10,9},{13,14},{14,13},{17,18},{18,... | collective-permute-start | bytes 3145736 | tf_op jit(solution)/shard_map/ppermute | solution.py:338
  56.8 0.1 collective-permute-start.4
  56.9 0.5 collective-permute-start.7
  57.4 9.5 %collective-permute-done.2.refs_0_ = bf16[128,4096]{1,0:T(8,128)(2,1)S(1)} collective-permute-done((bf16[128,4096]{1,0:T(8,128)(2,1)}, bf16[128,4096]{1,0:T(8,128)(2,1)S(1)}, u32[]{:S(2)}, u32[]{:S(2)}) %collective-permute-start.2) | collective-permute-done | bytes 1048608 | tf_op jit(solution)/shard_map/ppermute | solution.py:338
  66.9 1.3 collective-permute-start.6
  68.2 7.4 %collective-permute-done.8.refs_18_ = bf16[128,8192]{1,0:T(8,128)(2,1)} collective-permute-done((bf16[128,8192]{1,0:T(8,128)(2,1)}, bf16[128,8192]{1,0:T(8,128)(2,1)}, u32[]{:S(2)}, u32[]{:S(2)}) %collective-permute-start.8) | collective-permute-done | bytes 2097184 | tf_op jit(solution)/shard_map/ppermute | solution.py:349
  75.6 1.3 collective-permute-start.9
  76.9 1.1 slice.29
  78.1 0.1 collective-permute-done.3.refs_2_
  78.1 1.7 collective-permute-start.12
  79.8 3.1 %collective-permute-start.13 = (bf16[128,4096]{1,0:T(8,128)(2,1)}, bf16[128,4096]{1,0:T(8,128)(2,1)}, u32[]{:S(2)}, u32[]{:S(2)}) collective-permute-start(bf16[128,4096]{1,0:T(8,128)(2,1)} %get-tuple-element.21), channel_id=1, source_target_pairs={{1,2},{2,1},{5,6},{6,5},{9,10},{10,9},{13,14},{14,13},{17,18},{18,... | collective-permute-start | bytes 3145736 | tf_op jit(solution)/shard_map/ppermute | solution.py:338
  82.9 0.1 broadcast_in_dim.13.refs_9_
  83.0 0.1 broadcast_in_dim.14.refs_10_
  83.1 1.1 copy-done.7
  84.2 0.7 copy-done.8
  84.9 34.7 %shard_map.145 = (bf16[128,4096]{1,0:T(8,128)(2,1)}, bf16[128,4096]{1,0:T(8,128)(2,1)S(1)}, f32[49168,128]{1,0:T(8,128)}) custom-call(s32[5]{0:T(128)S(1)} %stack.23.places, s32[24576]{0:T(1024)S(1)} %pad_add_fusion.aux, bf16[128,4096]{1,0:T(8,128)(2,1)S(1)} %collective-permute-done.2.refs_0_, bf16[128,16384]{1,0:T(8,128)(2,1)} %refs_1_.3, ...), custom_call_target="tpu_custom_call" | custom-call | flops 2867200000 | bytes 8388608 | tf_op jit(solution)/shard_map/pallas_call | solution.py:250
  119.7 1.0 copy-done.2
  120.6 2.4 %collective-permute-start.11 = (bf16[128,4096]{1,0:T(8,128)(2,1)}, bf16[128,4096]{1,0:T(8,128)(2,1)S(1)}, u32[]{:S(2)}, u32[]{:S(2)}) collective-permute-start(bf16[128,4096]{1,0:T(8,128)(2,1)} %copy-done.2), channel_id=1, source_target_pairs={{1,2},{2,1},{5,6},{6,5},{9,10},{10,9},{13,14},{14,13},{17,18},{18,... | collective-permute-start | bytes 3145736 | tf_op jit(solution)/shard_map/ppermute | solution.py:338
  123.1 2.2 %copy-done = bf16[128,16384]{1,0:T(8,128)(2,1)S(1)} copy-done((bf16[128,16384]{1,0:T(8,128)(2,1)S(1)}, bf16[128,16384]{1,0:T(8,128)(2,1)}, u32[]{:S(2)}) %copy-start) | copy-done | bytes 4194328
  125.3 31.0 %shard_map.146 = (bf16[128,4096]{1,0:T(8,128)(2,1)S(1)}, bf16[128,4096]{1,0:T(8,128)(2,1)S(1)}) custom-call(s32[5]{0:T(128)S(1)} %stack.23.places, s32[24576]{0:T(1024)S(1)} %pad_add_fusion.aux, bf16[128,4096]{1,0:T(8,128)(2,1)} %collective-permute-done.12.refs_0_, bf16[128,16384]{1,0:T(8,128)(2,1)S(1)} %copy-done, ...), custom_call_target="tpu_custom_call" | custom-call | flops 2867200000 | bytes 8388608 | tf_op jit(solution)/shard_map/pallas_call | solution.py:250
  156.4 0.0 collective-permute-start.14
  156.4 3.3 %collective-permute-start.15 = (bf16[128,4096]{1,0:T(8,128)(2,1)S(1)}, bf16[128,4096]{1,0:T(8,128)(2,1)S(1)}, u32[]{:S(2)}, u32[]{:S(2)}) collective-permute-start(bf16[128,4096]{1,0:T(8,128)(2,1)S(1)} %get-tuple-element.23), channel_id=1, source_target_pairs={{1,2},{2,1},{5,6},{6,5},{9,10},{10,9},{13,14},{14,13},{17,18},{18,... | collective-permute-start | bytes 3145736 | tf_op jit(solution)/shard_map/ppermute | solution.py:338
  159.7 0.4 broadcast_in_dim.10
  160.1 1.5 select_dynamic-update-slice_fusion.3
  161.6 0.3 select_dynamic-update-slice_fusion.2
  162.0 16.6 %collective-permute-done.14 = bf16[128,4096]{1,0:T(8,128)(2,1)S(1)} collective-permute-done((bf16[128,4096]{1,0:T(8,128)(2,1)S(1)}, bf16[128,4096]{1,0:T(8,128)(2,1)S(1)}, u32[]{:S(2)}, u32[]{:S(2)}) %collective-permute-start.14) | collective-permute-done | bytes 1048608 | tf_op jit(solution)/shard_map/ppermute | solution.py:338
  178.6 0.3 select_dynamic-update-slice_fusion.1
  178.9 2.4 %collective-permute-done.15 = bf16[128,4096]{1,0:T(8,128)(2,1)S(1)} collective-permute-done((bf16[128,4096]{1,0:T(8,128)(2,1)S(1)}, bf16[128,4096]{1,0:T(8,128)(2,1)S(1)}, u32[]{:S(2)}, u32[]{:S(2)}) %collective-permute-start.15) | collective-permute-done | bytes 1048608 | tf_op jit(solution)/shard_map/ppermute | solution.py:338
  181.3 1.2 select_dynamic-update-slice_fusion
  (55 shorter events, 0.4 us)
Async XLA Ops:
  0.0 14.6 %copy-start.13 = (f32[256]{0:T(256)S(1)}, f32[256]{0:T(256)}, u32[]{:S(2)}) copy-start(f32[256]{0:T(256)} %param.28) | copy-start | bytes 3076
  0.0 14.6 %copy-start.12 = (f32[256]{0:T(256)S(1)}, f32[256]{0:T(256)}, u32[]{:S(2)}) copy-start(f32[256]{0:T(256)} %param.29) | copy-start | bytes 3076
  0.0 14.7 %copy-start.15 = (f32[256]{0:T(256)S(1)}, f32[256]{0:T(256)}, u32[]{:S(2)}) copy-start(f32[256]{0:T(256)} %param.26) | copy-start | bytes 3076
  0.0 14.7 %copy-start.14 = (f32[256]{0:T(256)S(1)}, f32[256]{0:T(256)}, u32[]{:S(2)}) copy-start(f32[256]{0:T(256)} %param.27) | copy-start | bytes 3076
  0.0 47.8 %collective-permute-start.1 = (bf16[128,8192]{1,0:T(8,128)(2,1)}, bf16[128,8192]{1,0:T(8,128)(2,1)}, u32[]{:S(2)}, u32[]{:S(2)}) collective-permute-start(bf16[128,8192]{1,0:T(8,128)(2,1)} %refs_12_.1), channel_id=1, source_target_pairs={{0,1},{1,0},{2,3},{3,2},{4,5},{5,4},{6,7},{7,6},{8,9},{9,8},{10,11... | collective-permute-start | bytes 6291464 | tf_op jit(solution)/shard_map/ppermute | solution.py:338
  2.2 54.7 %collective-permute-start.5 = (bf16[128,8192]{1,0:T(8,128)(2,1)}, bf16[128,8192]{1,0:T(8,128)(2,1)}, u32[]{:S(2)}, u32[]{:S(2)}) collective-permute-start(bf16[128,8192]{1,0:T(8,128)(2,1)} %refs_12_.1), channel_id=1, source_target_pairs={{2,4},{6,8},{10,12},{14,16},{18,20},{22,24},{26,28},{5,3},{9,7},{1... | collective-permute-start | bytes 6291464 | tf_op jit(solution)/shard_map/ppermute | solution.py:349
  11.2 8.3 %collective-permute-start = (f32[9,8192]{1,0:T(8,128)}, f32[9,8192]{1,0:T(8,128)}, u32[]{:S(2)}, u32[]{:S(2)}) collective-permute-start(f32[9,8192]{1,0:T(8,128)} %fusion), channel_id=1, source_target_pairs={{0,2},{3,1},{4,6},{7,5},{8,10},{11,9},{12,14},{15,13},{16,18},{19,... | collective-permute-start | bytes 884744 | tf_op jit(solution)/shard_map/ppermute | solution.py:338
  14.8 4.6 %copy-start.10 = (bf16[256,256]{1,0:T(8,128)(2,1)S(1)}, bf16[256,256]{1,0:T(8,128)(2,1)}, u32[]{:S(2)}) copy-start(bf16[256,256]{1,0:T(8,128)(2,1)} %param.23) | copy-start | bytes 393220
  14.8 4.6 %copy-start.11 = (bf16[256,256]{1,0:T(8,128)(2,1)S(1)}, bf16[256,256]{1,0:T(8,128)(2,1)}, u32[]{:S(2)}) copy-start(bf16[256,256]{1,0:T(8,128)(2,1)} %param.20) | copy-start | bytes 393220
  14.8 42.0 %copy-start.1 = (bf16[128,8192]{1,0:T(8,128)(2,1)S(1)}, bf16[128,8192]{1,0:T(8,128)(2,1)}, u32[]{:S(2)}) copy-start(bf16[128,8192]{1,0:T(8,128)(2,1)} %refs_12_.1) | copy-start | bytes 6291460
  19.3 65.6 %copy-start.4 = (bf16[256,256]{1,0:T(8,128)(2,1)S(1)}, bf16[256,256]{1,0:T(8,128)(2,1)}, u32[]{:S(2)}) copy-start(bf16[256,256]{1,0:T(8,128)(2,1)} %refs_5_.3) | copy-start | bytes 393220
  19.3 65.6 %copy-start.5 = (bf16[256,256]{1,0:T(8,128)(2,1)S(1)}, bf16[256,256]{1,0:T(8,128)(2,1)}, u32[]{:S(2)}) copy-start(bf16[256,256]{1,0:T(8,128)(2,1)} %refs_6_.3) | copy-start | bytes 393220
  20.8 32.8 %copy-start.9 = (f32[9,8192]{1,0:T(8,128)}, f32[9,8192]{1,0:T(8,128)S(1)}, u32[]{:S(2)}) copy-start(f32[9,8192]{1,0:T(8,128)S(1)} %fusion.2) | copy-start | bytes 884740
  47.8 27.7 %collective-permute-start.8 = (bf16[128,8192]{1,0:T(8,128)(2,1)}, bf16[128,8192]{1,0:T(8,128)(2,1)}, u32[]{:S(2)}, u32[]{:S(2)}) collective-permute-start(bf16[128,8192]{1,0:T(8,128)(2,1)} %collective-permute-done.1.refs_16_), channel_id=1, source_target_pairs={{2,4},{6,8},{10,12},{14,16},{18,20},{22,24},{26,28},{5,3},{9,7},{1... | collective-permute-start | bytes 6291464 | tf_op jit(solution)/shard_map/ppermute | solution.py:349
  54.8 12.1 %collective-permute-start.2 = (bf16[128,4096]{1,0:T(8,128)(2,1)}, bf16[128,4096]{1,0:T(8,128)(2,1)S(1)}, u32[]{:S(2)}, u32[]{:S(2)}) collective-permute-start(bf16[128,4096]{1,0:T(8,128)(2,1)} %get-tuple-element.15), channel_id=1, source_target_pairs={{0,2},{3,1},{1,0},{2,3},{4,6},{7,5},{5,4},{6,7},{8,10},{11,9},{9,8... | collective-permute-start | bytes 3145736 | tf_op jit(solution)/shard_map/ppermute | solution.py:338
  54.9 23.2 %collective-permute-start.3 = (bf16[128,4096]{1,0:T(8,128)(2,1)}, bf16[128,4096]{1,0:T(8,128)(2,1)S(1)}, u32[]{:S(2)}, u32[]{:S(2)}) collective-permute-start(bf16[128,4096]{1,0:T(8,128)(2,1)} %get-tuple-element.16), channel_id=1, source_target_pairs={{1,2},{2,1},{5,6},{6,5},{9,10},{10,9},{13,14},{14,13},{17,18},{18,... | collective-permute-start | bytes 3145736 | tf_op jit(solution)/shard_map/ppermute | solution.py:338
  56.8 23.0 %collective-permute-start.4 = (bf16[128,8192]{1,0:T(8,128)(2,1)S(1)}, bf16[128,8192]{1,0:T(8,128)(2,1)S(1)}, u32[]{:S(2)}, u32[]{:S(2)}) collective-permute-start(bf16[128,8192]{1,0:T(8,128)(2,1)S(1)} %copy-done.1), channel_id=1, source_target_pairs={{0,2},{1,3},{2,0},{3,1},{4,6},{5,7},{6,4},{7,5},{8,10},{9,11},{10,... | collective-permute-start | bytes 6291464 | tf_op jit(solution)/shard_map/ppermute | solution.py:338
  56.9 26.0 %collective-permute-start.7 = (bf16[128,8192]{1,0:T(8,128)(2,1)}, bf16[128,8192]{1,0:T(8,128)(2,1)S(1)}, u32[]{:S(2)}, u32[]{:S(2)}) collective-permute-start(bf16[128,8192]{1,0:T(8,128)(2,1)} %collective-permute-done.1.refs_16_), channel_id=1, source_target_pairs={{0,2},{1,3},{2,0},{3,1},{4,6},{5,7},{6,4},{7,5},{8,10},{9,11},{10,... | collective-permute-start | bytes 6291464 | tf_op jit(solution)/shard_map/ppermute | solution.py:338
  66.9 16.0 %collective-permute-start.6 = (bf16[128,8192]{1,0:T(8,128)(2,1)}, bf16[128,8192]{1,0:T(8,128)(2,1)S(1)}, u32[]{:S(2)}, u32[]{:S(2)}) collective-permute-start(bf16[128,8192]{1,0:T(8,128)(2,1)} %collective-permute-done.5.refs_14_), channel_id=1, source_target_pairs={{0,2},{3,1},{4,6},{7,5},{8,10},{11,9},{12,14},{15,13},{16,18},{19,... | collective-permute-start | bytes 6291464 | tf_op jit(solution)/shard_map/ppermute | solution.py:338
  75.6 7.4 %collective-permute-start.9 = (bf16[128,8192]{1,0:T(8,128)(2,1)}, bf16[128,8192]{1,0:T(8,128)(2,1)S(1)}, u32[]{:S(2)}, u32[]{:S(2)}) collective-permute-start(bf16[128,8192]{1,0:T(8,128)(2,1)} %collective-permute-done.8.refs_18_), channel_id=1, source_target_pairs={{0,2},{3,1},{4,6},{7,5},{8,10},{11,9},{12,14},{15,13},{16,18},{19,... | collective-permute-start | bytes 6291464 | tf_op jit(solution)/shard_map/ppermute | solution.py:338
  78.1 45.0 %collective-permute-start.12 = (bf16[128,4096]{1,0:T(8,128)(2,1)}, bf16[128,4096]{1,0:T(8,128)(2,1)}, u32[]{:S(2)}, u32[]{:S(2)}) collective-permute-start(bf16[128,4096]{1,0:T(8,128)(2,1)} %get-tuple-element.20), channel_id=1, source_target_pairs={{0,2},{3,1},{1,0},{2,3},{4,6},{7,5},{5,4},{6,7},{8,10},{11,9},{9,8... | collective-permute-start | bytes 3145736 | tf_op jit(solution)/shard_map/ppermute | solution.py:338
  79.8 43.3 %collective-permute-start.13 = (bf16[128,4096]{1,0:T(8,128)(2,1)}, bf16[128,4096]{1,0:T(8,128)(2,1)}, u32[]{:S(2)}, u32[]{:S(2)}) collective-permute-start(bf16[128,4096]{1,0:T(8,128)(2,1)} %get-tuple-element.21), channel_id=1, source_target_pairs={{1,2},{2,1},{5,6},{6,5},{9,10},{10,9},{13,14},{14,13},{17,18},{18,... | collective-permute-start | bytes 3145736 | tf_op jit(solution)/shard_map/ppermute | solution.py:338
  82.9 1.3 copy-start.7
  82.9 2.0 %copy-start.8 = (bf16[128,8192]{1,0:T(8,128)(2,1)}, bf16[128,8192]{1,0:T(8,128)(2,1)S(1)}, u32[]{:S(2)}) copy-start(bf16[128,8192]{1,0:T(8,128)(2,1)S(1)} %collective-permute-done.9.refs_19_) | copy-start | bytes 6291460
  119.7 1.0 copy-start.2
  120.6 39.0 %collective-permute-start.10 = (bf16[128,4096]{1,0:T(8,128)(2,1)}, bf16[128,4096]{1,0:T(8,128)(2,1)}, u32[]{:S(2)}, u32[]{:S(2)}) collective-permute-start(bf16[128,4096]{1,0:T(8,128)(2,1)} %get-tuple-element.19), channel_id=1, source_target_pairs={{2,0},{1,3},{0,1},{3,2},{6,4},{5,7},{4,5},{7,6},{10,8},{9,11},{8,9... | collective-permute-start | bytes 3145736 | tf_op jit(solution)/shard_map/ppermute | solution.py:338
  120.6 41.0 %collective-permute-start.11 = (bf16[128,4096]{1,0:T(8,128)(2,1)}, bf16[128,4096]{1,0:T(8,128)(2,1)S(1)}, u32[]{:S(2)}, u32[]{:S(2)}) collective-permute-start(bf16[128,4096]{1,0:T(8,128)(2,1)} %copy-done.2), channel_id=1, source_target_pairs={{1,2},{2,1},{5,6},{6,5},{9,10},{10,9},{13,14},{14,13},{17,18},{18,... | collective-permute-start | bytes 3145736 | tf_op jit(solution)/shard_map/ppermute | solution.py:338
  123.1 2.2 %copy-start = (bf16[128,16384]{1,0:T(8,128)(2,1)S(1)}, bf16[128,16384]{1,0:T(8,128)(2,1)}, u32[]{:S(2)}) copy-start(bf16[128,16384]{1,0:T(8,128)(2,1)} %refs_1_.3) | copy-start | bytes 12582916
  156.3 3.7 %copy-start.3 = (bf16[128,4096]{1,0:T(8,128)(2,1)S(1)}, bf16[128,4096]{1,0:T(8,128)(2,1)}, u32[]{:S(2)}) copy-start(bf16[128,4096]{1,0:T(8,128)(2,1)} %copy-done.2) | copy-start | bytes 3145732
  156.4 22.2 %collective-permute-start.14 = (bf16[128,4096]{1,0:T(8,128)(2,1)S(1)}, bf16[128,4096]{1,0:T(8,128)(2,1)S(1)}, u32[]{:S(2)}, u32[]{:S(2)}) collective-permute-start(bf16[128,4096]{1,0:T(8,128)(2,1)S(1)} %get-tuple-element.24), channel_id=1, source_target_pairs={{2,0},{1,3},{0,1},{3,2},{6,4},{5,7},{4,5},{7,6},{10,8},{9,11},{8,9... | collective-permute-start | bytes 3145736 | tf_op jit(solution)/shard_map/ppermute | solution.py:338
  156.4 24.9 %collective-permute-start.15 = (bf16[128,4096]{1,0:T(8,128)(2,1)S(1)}, bf16[128,4096]{1,0:T(8,128)(2,1)S(1)}, u32[]{:S(2)}, u32[]{:S(2)}) collective-permute-start(bf16[128,4096]{1,0:T(8,128)(2,1)S(1)} %get-tuple-element.23), channel_id=1, source_target_pairs={{1,2},{2,1},{5,6},{6,5},{9,10},{10,9},{13,14},{14,13},{17,18},{18,... | collective-permute-start | bytes 3145736 | tf_op jit(solution)/shard_map/ppermute | solution.py:338
  178.9 2.4 %copy-start.6 = (bf16[128,16384]{1,0:T(8,128)(2,1)}, bf16[128,16384]{1,0:T(8,128)(2,1)S(1)}, u32[]{:S(2)}) copy-start(bf16[128,16384]{1,0:T(8,128)(2,1)S(1)} %select_dynamic-update-slice_fusion.1) | copy-start | bytes 12582916

commit v4 on v0

--- a/solution.py
+++ b/solution.py
@@ -82,8 +82,8 @@
     given, refs = refs[:8], refs[8:]
     held_here, refs = refs[-8:], refs[:-8]
     scales, w_latent, w_edge, w_agg, w_out_t, bias, gain, shift = held_here
-    table, latents, fine, total, earlier, later, scale_rows, slots, live, sems, given_sems = refs[-11:]
-    refs = refs[:-11]
+    table, latents, fine, total, earlier, later, scale_rows, slots, live, sems, given_sems, *buffers = refs[-13:]
+    refs = refs[:-13]
     fetches = [
         pltpu.make_async_copy(far if at else far.at[:, pl.ds(start, near.shape[1])], near, given_sems.at[at])
         for at, (far, near) in enumerate(zip(given, held_here))
@@ -129,8 +129,7 @@
         bring(p, 0).wait()
     if segments is None:
         move.wait()
-    sublane = lax.broadcasted_iota(jnp.int32, (8, 128), 0)
-    owns = [sublane >= 2 * j for j in range(4)]
+    origin = places[0] // 8
 
     def begin(i):
         columns = pl.ds(pl.multiple_of(i * step, step), step)
@@ -145,18 +144,25 @@
         scale_rows[pl.ds(0, step, stride=2), :] = scale_columns
         scale_rows[pl.ds(1, step, stride=2), :] = scale_columns
 
-    def group(at, g):
-        part = fine[pl.ds(g * 8, 8), :]
-        scale = scale_rows[pl.ds(g * 8, 8), :]
-        acc = None
-        for k in range(parents):
-            rows = None
-            for j in range(4):
-                loaded = table[pl.ds(slots[at + (k * step + g * 4 + j)], 8), :]
-                rows = loaded if rows is None else jnp.where(owns[j], loaded, rows)
-            hidden = jnp.maximum(part + rows, 0.0) * scale[:, k : k + 1]
-            acc = hidden if acc is None else acc + hidden
-        return acc
+    def fetch_rows(at, groups, buffer):
+        for here, g in enumerate(groups):
+            for k in range(parents):
+                for j in range(4):
+                    to = origin + ((k * GROUPS + here) * 8 + 2 * j)
+                    buffer[pl.ds(to, 2), :] = table[pl.ds(slots[at + (k * step + g * 4 + j)], 2), :]
+
+    def sum_rows(groups, buffer):
+        sums = []
+        for here, g in enumerate(groups):
+            part = fine[pl.ds(g * 8, 8), :]
+            scale = scale_rows[pl.ds(g * 8, 8), :]
+            acc = None
+            for k in range(parents):
+                rows = buffer[pl.ds((k * GROUPS + here) * 8, 8), :]
+                hidden = jnp.maximum(part + rows, 0.0) * scale[:, k : k + 1]
+                acc = hidden if acc is None else acc + hidden
+            sums.append(acc)
+        total[pl.ds(groups[0] * 8, len(sums) * 8), :] = jnp.concatenate(sums, axis=0)
 
     def widened(ref):
         return jnp.concatenate([ref[...]] * (step // 128), axis=1)
@@ -198,10 +204,11 @@
         parts = finish(before, summed, own_part)
         base = pl.multiple_of(i * (parents * step), parents * step)
         begun = begin(after)
-        for first in range(0, step // 4, GROUPS):
+        for at, first in enumerate(range(0, step // 4, GROUPS)):
             result = next(parts, None) if first < 4 * GROUPS else last(parts)
-            sums = [group(base, g) for g in range(first, min(first + GROUPS, step // 4))]
-            total[pl.ds(first * 8, len(sums) * 8), :] = jnp.concatenate(sums, axis=0)
+            groups = range(first, min(first + GROUPS, step // 4))
+            fetch_rows(base, groups, buffers[at % 2])
+            sum_rows(groups, buffers[at % 2])
         write(before, result)
         earlier[...] = current
         keep(*begun)
@@ -260,6 +267,8 @@
             pltpu.SMEM((1024,), jnp.int32),
             pltpu.SemaphoreType.DMA((parents + 2 + count,)),
             pltpu.SemaphoreType.DMA((1 + len(params),)),
+            pltpu.VMEM((parents * GROUPS * 8, 128), F32),
+            pltpu.VMEM((parents * GROUPS * 8, 128), F32),
             pltpu.VMEM((scales.shape[0], nodes), F32),
         ]
         + [pltpu.VMEM(param.shape, param.dtype) for param in params],
@@ -446,7 +455,7 @@
         return update(start, nodes, aux, arrays, sources, scales, params, places, **table)
 
     count = parents.shape[1]
-    slots = 2 * parents + (PAD - 2 * (jnp.arange(count, dtype=jnp.int32) % 4))
+    slots = 2 * parents + PAD
     aux = jnp.concatenate([slots, jnp.broadcast_to(live_rows[:, None], (1, count))])
     plan = paired if pairing else plain
     return plan(fine_latent, coarse_latent, aux, interp_weights, ordered(w_parent, 0, 0), run)

time: 183 us -> 184 us (level)
  no operation moved by 1% of the time
where the time goes in v4:
time: 184 us; the launch traced here: 182 us
  Pallas kernels  66.4 us (36%)
  waiting for transfers between devices  65.9 us (36%)
  starting transfers between devices  27.6 us (15%)
  local copies, waits for them, and re-layouts  12.7 us (7%)
  other arithmetic  8.06 us (4%)
    pallas_call x2, Pallas kernels, update(): pl.pallas_call(functools.partial(update_kernel, sources, step, start, seg...  66.4 us
    ppermute x14, waiting for transfers between devices, send(): return lax.ppermute(value, ('dom', 'feat'), perm)  57.1 us
    ppermute x14, starting transfers between devices, send(): return lax.ppermute(value, ('dom', 'feat'), perm)  18.9 us
    ppermute x2, waiting for transfers between devices, halo(): return lax.ppermute(value, ('dom', 'feat'), perm)  8.8 us
    ppermute x2, starting transfers between devices, halo(): return lax.ppermute(value, ('dom', 'feat'), perm)  8.65 us
    unnamed x33, local copies, waits for them, and re-layouts  6.01 us
    dynamic_slice x1, local copies, waits for them, and re-layouts, cut(): return lax.dynamic_slice_in_dim(array, at, size, 1)  4.16 us
  transfers between devices with their start and end apart: 16, of which 5 were waited for; matrix products, arithmetic and copies ran while one was open for 8% of the time, Pallas kernels for 36%

profile of v4, /device:TPU:1, one launch (start us, length us, event | category | flops | bytes accessed | tf_op | source)
XLA Modules:
  0.0 182.0 jit_solution(3239145724599944104)
XLA Ops:
  0.0 2.1 %collective-permute-start.1 = (bf16[128,8192]{1,0:T(8,128)(2,1)}, bf16[128,8192]{1,0:T(8,128)(2,1)}, u32[]{:S(2)}, u32[]{:S(2)}) collective-permute-start(bf16[128,8192]{1,0:T(8,128)(2,1)} %refs_12_.1), channel_id=1, source_target_pairs={{0,1},{1,0},{2,3},{3,2},{4,5},{5,4},{6,7},{7,6},{8,9},{9,8},{10,11... | collective-permute-start | bytes 6291464 | tf_op jit(solution)/shard_map/ppermute | solution.py:342
  2.1 4.1 %collective-permute-start.5 = (bf16[128,8192]{1,0:T(8,128)(2,1)}, bf16[128,8192]{1,0:T(8,128)(2,1)S(1)}, u32[]{:S(2)}, u32[]{:S(2)}) collective-permute-start(bf16[128,8192]{1,0:T(8,128)(2,1)} %refs_12_.1), channel_id=1, source_target_pairs={{2,4},{6,8},{10,12},{14,16},{18,20},{22,24},{26,28},{5,3},{9,7},{1... | collective-permute-start | bytes 6291464 | tf_op jit(solution)/shard_map/ppermute | solution.py:353
  6.2 1.0 multiply_add_fusion
  7.9 0.8 copy-done.6
  8.7 1.9 %fusion = f32[9,8192]{1,0:T(8,128)} fusion(s32[]{:T(128)S(6)} %select_n.157, f32[5,16384]{1,0:T(8,128)S(1)} %pad_convert_fusion, f32[4,16384]{1,0:T(4,128)} %param.18), kind=kLoop, calls=%fused_computation.8 | loop fusion | flops 73728 | bytes 884740 | tf_op jit(solution)/shard_map/concatenate | solution.py:390
  10.6 1.3 collective-permute-start
  11.9 0.9 constant_dynamic-slice_fusion.5
  12.8 0.1 copy.21
  13.0 0.1 copy.22
  13.1 0.1 stack.23.places
  13.2 0.8 broadcast_select_fusion.7
  14.0 0.7 pad_maximum_fusion.1
  14.7 0.9 constant_dynamic-slice_fusion.3
  15.7 0.0 copy-start.13
  15.7 4.2 %constant_dynamic-slice_fusion = (bf16[128,4096]{1,0:T(8,128)(2,1)}, bf16[128,4096]{1,0:T(8,128)(2,1)}, bf16[128,4096]{1,0:T(8,128)(2,1)S(1)}, bf16[128,4096]{1,0:T(8,128)(2,1)S(1)}) fusion(bf16[128,16384]{1,0:T(8,128)(2,1)} %refs_1_.3, s32[]{:T(128)S(6)} %select_n.182, s32[]{:T(128)S(6)} %select_n.181, s32[]{:T(128)S(6)} %select_n.157, s32[]{:T(128)S(6)} %select_n.160), kind=kLoop, calls=%fused_computation.25 | loop fusion | bytes 8388624 | tf_op jit(solution)/shard_map/dynamic_slice | solution.py:290
  19.9 0.1 broadcast_select_fusion.3
  20.0 27.7 %collective-permute-done.1.refs_16_ = bf16[128,8192]{1,0:T(8,128)(2,1)} collective-permute-done((bf16[128,8192]{1,0:T(8,128)(2,1)}, bf16[128,8192]{1,0:T(8,128)(2,1)}, u32[]{:S(2)}, u32[]{:S(2)}) %collective-permute-start.1) | collective-permute-done | bytes 2097184 | tf_op jit(solution)/shard_map/ppermute | solution.py:342
  47.7 4.6 %collective-permute-start.8 = (bf16[128,8192]{1,0:T(8,128)(2,1)}, bf16[128,8192]{1,0:T(8,128)(2,1)S(1)}, u32[]{:S(2)}, u32[]{:S(2)}) collective-permute-start(bf16[128,8192]{1,0:T(8,128)(2,1)} %collective-permute-done.1.refs_16_), channel_id=1, source_target_pairs={{2,4},{6,8},{10,12},{14,16},{18,20},{22,24},{26,28},{5,3},{9,7},{1... | collective-permute-start | bytes 6291464 | tf_op jit(solution)/shard_map/ppermute | solution.py:353
  52.4 1.3 fusion.2
  53.6 0.0 collective-permute-start.2
  53.7 1.9 %collective-permute-start.3 = (bf16[128,4096]{1,0:T(8,128)(2,1)S(1)}, bf16[128,4096]{1,0:T(8,128)(2,1)S(1)}, u32[]{:S(2)}, u32[]{:S(2)}) collective-permute-start(bf16[128,4096]{1,0:T(8,128)(2,1)S(1)} %get-tuple-element.16), channel_id=1, source_target_pairs={{1,2},{2,1},{5,6},{6,5},{9,10},{10,9},{13,14},{14,13},{17,18},{18,... | collective-permute-start | bytes 3145736 | tf_op jit(solution)/shard_map/ppermute | solution.py:342
  55.6 0.1 collective-permute-start.4
  55.7 0.5 collective-permute-start.7
  56.2 9.2 %collective-permute-done.2.refs_0_ = bf16[128,4096]{1,0:T(8,128)(2,1)S(1)} collective-permute-done((bf16[128,4096]{1,0:T(8,128)(2,1)S(1)}, bf16[128,4096]{1,0:T(8,128)(2,1)S(1)}, u32[]{:S(2)}, u32[]{:S(2)}) %collective-permute-start.2) | collective-permute-done | bytes 1048608 | tf_op jit(solution)/shard_map/ppermute | solution.py:342
  65.4 1.3 collective-permute-start.6
  66.7 8.8 %collective-permute-done.8.refs_18_ = bf16[128,8192]{1,0:T(8,128)(2,1)S(1)} collective-permute-done((bf16[128,8192]{1,0:T(8,128)(2,1)}, bf16[128,8192]{1,0:T(8,128)(2,1)S(1)}, u32[]{:S(2)}, u32[]{:S(2)}) %collective-permute-start.8) | collective-permute-done | bytes 2097184 | tf_op jit(solution)/shard_map/ppermute | solution.py:353
  75.5 1.3 collective-permute-start.9
  76.9 0.1 copy.23
  77.0 1.7 collective-permute-start.12
  78.7 3.1 %collective-permute-start.13 = (bf16[128,4096]{1,0:T(8,128)(2,1)}, bf16[128,4096]{1,0:T(8,128)(2,1)}, u32[]{:S(2)}, u32[]{:S(2)}) collective-permute-start(bf16[128,4096]{1,0:T(8,128)(2,1)} %get-tuple-element.21), channel_id=1, source_target_pairs={{1,2},{2,1},{5,6},{6,5},{9,10},{10,9},{13,14},{14,13},{17,18},{18,... | collective-permute-start | bytes 3145736 | tf_op jit(solution)/shard_map/ppermute | solution.py:342
  81.9 0.1 broadcast_in_dim.13.refs_9_
  82.0 0.1 broadcast_in_dim.28.refs_10_
  82.1 1.1 copy-done.10
  83.2 0.7 copy-done.11
  83.8 35.1 %shard_map.145 = (bf16[128,4096]{1,0:T(8,128)(2,1)}, bf16[128,4096]{1,0:T(8,128)(2,1)S(1)}, f32[49168,128]{1,0:T(8,128)}) custom-call(s32[5]{0:T(128)S(1)} %stack.23.places, s32[40960]{0:T(1024)S(1)} %pad_add_fusion.aux, bf16[128,4096]{1,0:T(8,128)(2,1)S(1)} %collective-permute-done.2.refs_0_, bf16[128,16384]{1,0:T(8,128)(2,1)} %refs_1_.3, ...), custom_call_target="tpu_custom_call" | custom-call | flops 2867200000 | bytes 8388608 | tf_op jit(solution)/shard_map/pallas_call | solution.py:252
  118.9 1.0 copy-done.2
  119.9 2.4 %collective-permute-start.11 = (bf16[128,4096]{1,0:T(8,128)(2,1)}, bf16[128,4096]{1,0:T(8,128)(2,1)S(1)}, u32[]{:S(2)}, u32[]{:S(2)}) collective-permute-start(bf16[128,4096]{1,0:T(8,128)(2,1)} %copy-done.2), channel_id=1, source_target_pairs={{1,2},{2,1},{5,6},{6,5},{9,10},{10,9},{13,14},{14,13},{17,18},{18,... | collective-permute-start | bytes 3145736 | tf_op jit(solution)/shard_map/ppermute | solution.py:342
  122.3 2.2 %copy-done = bf16[128,16384]{1,0:T(8,128)(2,1)S(1)} copy-done((bf16[128,16384]{1,0:T(8,128)(2,1)S(1)}, bf16[128,16384]{1,0:T(8,128)(2,1)}, u32[]{:S(2)}) %copy-start) | copy-done | bytes 4194328
  124.5 31.3 %shard_map.146 = (bf16[128,4096]{1,0:T(8,128)(2,1)S(1)}, bf16[128,4096]{1,0:T(8,128)(2,1)S(1)}) custom-call(s32[5]{0:T(128)S(1)} %stack.23.places, s32[40960]{0:T(1024)S(1)} %pad_add_fusion.aux, bf16[128,4096]{1,0:T(8,128)(2,1)} %collective-permute-done.12.refs_0_, bf16[128,16384]{1,0:T(8,128)(2,1)S(1)} %copy-done, ...), custom_call_target="tpu_custom_call" | custom-call | flops 2867200000 | bytes 8388608 | tf_op jit(solution)/shard_map/pallas_call | solution.py:252
  155.8 0.0 collective-permute-start.14
  155.9 3.3 %collective-permute-start.15 = (bf16[128,4096]{1,0:T(8,128)(2,1)S(1)}, bf16[128,4096]{1,0:T(8,128)(2,1)S(1)}, u32[]{:S(2)}, u32[]{:S(2)}) collective-permute-start(bf16[128,4096]{1,0:T(8,128)(2,1)S(1)} %get-tuple-element.23), channel_id=1, source_target_pairs={{1,2},{2,1},{5,6},{6,5},{9,10},{10,9},{13,14},{14,13},{17,18},{18,... | collective-permute-start | bytes 3145736 | tf_op jit(solution)/shard_map/ppermute | solution.py:342
  159.2 0.4 broadcast_in_dim.10
  159.6 0.3 select_dynamic-update-slice_fusion.3
  159.9 0.3 select_dynamic-update-slice_fusion.2
  160.2 17.8 %collective-permute-done.14 = bf16[128,4096]{1,0:T(8,128)(2,1)S(1)} collective-permute-done((bf16[128,4096]{1,0:T(8,128)(2,1)S(1)}, bf16[128,4096]{1,0:T(8,128)(2,1)S(1)}, u32[]{:S(2)}, u32[]{:S(2)}) %collective-permute-start.14) | collective-permute-done | bytes 1048608 | tf_op jit(solution)/shard_map/ppermute | solution.py:342
  178.1 0.3 select_dynamic-update-slice_fusion.1
  178.4 2.4 %collective-permute-done.15 = bf16[128,4096]{1,0:T(8,128)(2,1)S(1)} collective-permute-done((bf16[128,4096]{1,0:T(8,128)(2,1)S(1)}, bf16[128,4096]{1,0:T(8,128)(2,1)S(1)}, u32[]{:S(2)}, u32[]{:S(2)}) %collective-permute-start.15) | collective-permute-done | bytes 1048608 | tf_op jit(solution)/shard_map/ppermute | solution.py:342
  180.8 1.2 select_dynamic-update-slice_fusion
  (49 shorter events, 0.4 us)
Async XLA Ops:
  0.0 47.7 %collective-permute-start.1 = (bf16[128,8192]{1,0:T(8,128)(2,1)}, bf16[128,8192]{1,0:T(8,128)(2,1)}, u32[]{:S(2)}, u32[]{:S(2)}) collective-permute-start(bf16[128,8192]{1,0:T(8,128)(2,1)} %refs_12_.1), channel_id=1, source_target_pairs={{0,1},{1,0},{2,3},{3,2},{4,5},{5,4},{6,7},{7,6},{8,9},{9,8},{10,11... | collective-permute-start | bytes 6291464 | tf_op jit(solution)/shard_map/ppermute | solution.py:342
  2.1 53.6 %collective-permute-start.5 = (bf16[128,8192]{1,0:T(8,128)(2,1)}, bf16[128,8192]{1,0:T(8,128)(2,1)S(1)}, u32[]{:S(2)}, u32[]{:S(2)}) collective-permute-start(bf16[128,8192]{1,0:T(8,128)(2,1)} %refs_12_.1), channel_id=1, source_target_pairs={{2,4},{6,8},{10,12},{14,16},{18,20},{22,24},{26,28},{5,3},{9,7},{1... | collective-permute-start | bytes 6291464 | tf_op jit(solution)/shard_map/ppermute | solution.py:353
  7.9 0.8 copy-start.6
  10.6 41.7 %collective-permute-start = (f32[9,8192]{1,0:T(8,128)}, f32[9,8192]{1,0:T(8,128)}, u32[]{:S(2)}, u32[]{:S(2)}) collective-permute-start(f32[9,8192]{1,0:T(8,128)} %fusion), channel_id=1, source_target_pairs={{0,2},{3,1},{4,6},{7,5},{8,10},{11,9},{12,14},{15,13},{16,18},{19,... | collective-permute-start | bytes 884744 | tf_op jit(solution)/shard_map/ppermute | solution.py:342
  15.7 4.2 %copy-start.13 = (bf16[256,256]{1,0:T(8,128)(2,1)S(1)}, bf16[256,256]{1,0:T(8,128)(2,1)}, u32[]{:S(2)}) copy-start(bf16[256,256]{1,0:T(8,128)(2,1)} %param.23) | copy-start | bytes 393220
  15.7 4.2 %copy-start.14 = (bf16[256,256]{1,0:T(8,128)(2,1)S(1)}, bf16[256,256]{1,0:T(8,128)(2,1)}, u32[]{:S(2)}) copy-start(bf16[256,256]{1,0:T(8,128)(2,1)} %param.20) | copy-start | bytes 393220
  15.7 36.6 %copy-start.7 = (f32[5,16384]{1,0:T(8,128)S(1)}, f32[5,16384]{1,0:T(8,128)}, u32[]{:S(2)}) copy-start(f32[5,16384]{1,0:T(8,128)} %copy-done.6) | copy-start | bytes 983044
  15.7 36.6 %copy-start.12 = (f32[4,16384]{1,0:T(4,128)S(1)}, f32[4,16384]{1,0:T(4,128)}, u32[]{:S(2)}) copy-start(f32[4,16384]{1,0:T(4,128)} %param.18) | copy-start | bytes 786436
  15.7 39.9 %copy-start.1 = (bf16[128,8192]{1,0:T(8,128)(2,1)S(1)}, bf16[128,8192]{1,0:T(8,128)(2,1)}, u32[]{:S(2)}) copy-start(bf16[128,8192]{1,0:T(8,128)(2,1)} %refs_12_.1) | copy-start | bytes 6291460
  19.9 63.9 %copy-start.4 = (bf16[256,256]{1,0:T(8,128)(2,1)S(1)}, bf16[256,256]{1,0:T(8,128)(2,1)}, u32[]{:S(2)}) copy-start(bf16[256,256]{1,0:T(8,128)(2,1)} %refs_5_.3) | copy-start | bytes 393220
  19.9 63.9 %copy-start.5 = (bf16[256,256]{1,0:T(8,128)(2,1)S(1)}, bf16[256,256]{1,0:T(8,128)(2,1)}, u32[]{:S(2)}) copy-start(bf16[256,256]{1,0:T(8,128)(2,1)} %refs_6_.3) | copy-start | bytes 393220
  47.7 27.7 %collective-permute-start.8 = (bf16[128,8192]{1,0:T(8,128)(2,1)}, bf16[128,8192]{1,0:T(8,128)(2,1)S(1)}, u32[]{:S(2)}, u32[]{:S(2)}) collective-permute-start(bf16[128,8192]{1,0:T(8,128)(2,1)} %collective-permute-done.1.refs_16_), channel_id=1, source_target_pairs={{2,4},{6,8},{10,12},{14,16},{18,20},{22,24},{26,28},{5,3},{9,7},{1... | collective-permute-start | bytes 6291464 | tf_op jit(solution)/shard_map/ppermute | solution.py:353
  53.6 11.8 %collective-permute-start.2 = (bf16[128,4096]{1,0:T(8,128)(2,1)S(1)}, bf16[128,4096]{1,0:T(8,128)(2,1)S(1)}, u32[]{:S(2)}, u32[]{:S(2)}) collective-permute-start(bf16[128,4096]{1,0:T(8,128)(2,1)S(1)} %get-tuple-element.15), channel_id=1, source_target_pairs={{0,2},{3,1},{1,0},{2,3},{4,6},{7,5},{5,4},{6,7},{8,10},{11,9},{9,8... | collective-permute-start | bytes 3145736 | tf_op jit(solution)/shard_map/ppermute | solution.py:342
  53.7 23.3 %collective-permute-start.3 = (bf16[128,4096]{1,0:T(8,128)(2,1)S(1)}, bf16[128,4096]{1,0:T(8,128)(2,1)S(1)}, u32[]{:S(2)}, u32[]{:S(2)}) collective-permute-start(bf16[128,4096]{1,0:T(8,128)(2,1)S(1)} %get-tuple-element.16), channel_id=1, source_target_pairs={{1,2},{2,1},{5,6},{6,5},{9,10},{10,9},{13,14},{14,13},{17,18},{18,... | collective-permute-start | bytes 3145736 | tf_op jit(solution)/shard_map/ppermute | solution.py:342
  55.6 23.1 %collective-permute-start.4 = (bf16[128,8192]{1,0:T(8,128)(2,1)S(1)}, bf16[128,8192]{1,0:T(8,128)(2,1)S(1)}, u32[]{:S(2)}, u32[]{:S(2)}) collective-permute-start(bf16[128,8192]{1,0:T(8,128)(2,1)S(1)} %copy-done.1), channel_id=1, source_target_pairs={{0,2},{1,3},{2,0},{3,1},{4,6},{5,7},{6,4},{7,5},{8,10},{9,11},{10,... | collective-permute-start | bytes 6291464 | tf_op jit(solution)/shard_map/ppermute | solution.py:342
  55.7 26.1 %collective-permute-start.7 = (bf16[128,8192]{1,0:T(8,128)(2,1)}, bf16[128,8192]{1,0:T(8,128)(2,1)S(1)}, u32[]{:S(2)}, u32[]{:S(2)}) collective-permute-start(bf16[128,8192]{1,0:T(8,128)(2,1)} %collective-permute-done.1.refs_16_), channel_id=1, source_target_pairs={{0,2},{1,3},{2,0},{3,1},{4,6},{5,7},{6,4},{7,5},{8,10},{9,11},{10,... | collective-permute-start | bytes 6291464 | tf_op jit(solution)/shard_map/ppermute | solution.py:342
  65.4 16.5 %collective-permute-start.6 = (bf16[128,8192]{1,0:T(8,128)(2,1)S(1)}, bf16[128,8192]{1,0:T(8,128)(2,1)S(1)}, u32[]{:S(2)}, u32[]{:S(2)}) collective-permute-start(bf16[128,8192]{1,0:T(8,128)(2,1)S(1)} %collective-permute-done.5.refs_14_), channel_id=1, source_target_pairs={{0,2},{3,1},{4,6},{7,5},{8,10},{11,9},{12,14},{15,13},{16,18},{19,... | collective-permute-start | bytes 6291464 | tf_op jit(solution)/shard_map/ppermute | solution.py:342
  75.5 6.6 %copy-start.9 = (bf16[128,8192]{1,0:T(8,128)(2,1)}, bf16[128,8192]{1,0:T(8,128)(2,1)S(1)}, u32[]{:S(2)}) copy-start(bf16[128,8192]{1,0:T(8,128)(2,1)S(1)} %collective-permute-done.8.refs_18_) | copy-start | bytes 6291460
  75.5 6.4 %collective-permute-start.9 = (bf16[128,8192]{1,0:T(8,128)(2,1)S(1)}, bf16[128,8192]{1,0:T(8,128)(2,1)S(1)}, u32[]{:S(2)}, u32[]{:S(2)}) collective-permute-start(bf16[128,8192]{1,0:T(8,128)(2,1)S(1)} %collective-permute-done.8.refs_18_), channel_id=1, source_target_pairs={{0,2},{3,1},{4,6},{7,5},{8,10},{11,9},{12,14},{15,13},{16,18},{19,... | collective-permute-start | bytes 6291464 | tf_op jit(solution)/shard_map/ppermute | solution.py:342
  77.0 45.3 %collective-permute-start.12 = (bf16[128,4096]{1,0:T(8,128)(2,1)}, bf16[128,4096]{1,0:T(8,128)(2,1)}, u32[]{:S(2)}, u32[]{:S(2)}) collective-permute-start(bf16[128,4096]{1,0:T(8,128)(2,1)} %get-tuple-element.20), channel_id=1, source_target_pairs={{0,2},{3,1},{1,0},{2,3},{4,6},{7,5},{5,4},{6,7},{8,10},{11,9},{9,8... | collective-permute-start | bytes 3145736 | tf_op jit(solution)/shard_map/ppermute | solution.py:342
  78.7 43.6 %collective-permute-start.13 = (bf16[128,4096]{1,0:T(8,128)(2,1)}, bf16[128,4096]{1,0:T(8,128)(2,1)}, u32[]{:S(2)}, u32[]{:S(2)}) collective-permute-start(bf16[128,4096]{1,0:T(8,128)(2,1)} %get-tuple-element.21), channel_id=1, source_target_pairs={{1,2},{2,1},{5,6},{6,5},{9,10},{10,9},{13,14},{14,13},{17,18},{18,... | collective-permute-start | bytes 3145736 | tf_op jit(solution)/shard_map/ppermute | solution.py:342
  81.8 1.3 copy-start.10
  81.9 2.0 %copy-start.11 = (bf16[128,8192]{1,0:T(8,128)(2,1)}, bf16[128,8192]{1,0:T(8,128)(2,1)S(1)}, u32[]{:S(2)}) copy-start(bf16[128,8192]{1,0:T(8,128)(2,1)S(1)} %collective-permute-done.9.refs_19_) | copy-start | bytes 6291460
  118.9 1.0 copy-start.2
  119.9 39.3 %collective-permute-start.10 = (bf16[128,4096]{1,0:T(8,128)(2,1)}, bf16[128,4096]{1,0:T(8,128)(2,1)S(1)}, u32[]{:S(2)}, u32[]{:S(2)}) collective-permute-start(bf16[128,4096]{1,0:T(8,128)(2,1)} %get-tuple-element.19), channel_id=1, source_target_pairs={{2,0},{1,3},{0,1},{3,2},{6,4},{5,7},{4,5},{7,6},{10,8},{9,11},{8,9... | collective-permute-start | bytes 3145736 | tf_op jit(solution)/shard_map/ppermute | solution.py:342
  119.9 40.0 %collective-permute-start.11 = (bf16[128,4096]{1,0:T(8,128)(2,1)}, bf16[128,4096]{1,0:T(8,128)(2,1)S(1)}, u32[]{:S(2)}, u32[]{:S(2)}) collective-permute-start(bf16[128,4096]{1,0:T(8,128)(2,1)} %copy-done.2), channel_id=1, source_target_pairs={{1,2},{2,1},{5,6},{6,5},{9,10},{10,9},{13,14},{14,13},{17,18},{18,... | collective-permute-start | bytes 3145736 | tf_op jit(solution)/shard_map/ppermute | solution.py:342
  122.3 2.2 %copy-start = (bf16[128,16384]{1,0:T(8,128)(2,1)S(1)}, bf16[128,16384]{1,0:T(8,128)(2,1)}, u32[]{:S(2)}) copy-start(bf16[128,16384]{1,0:T(8,128)(2,1)} %refs_1_.3) | copy-start | bytes 12582916
  155.8 3.8 %copy-start.3 = (bf16[128,4096]{1,0:T(8,128)(2,1)S(1)}, bf16[128,4096]{1,0:T(8,128)(2,1)}, u32[]{:S(2)}) copy-start(bf16[128,4096]{1,0:T(8,128)(2,1)} %copy-done.2) | copy-start | bytes 3145732
  155.8 22.2 %collective-permute-start.14 = (bf16[128,4096]{1,0:T(8,128)(2,1)S(1)}, bf16[128,4096]{1,0:T(8,128)(2,1)S(1)}, u32[]{:S(2)}, u32[]{:S(2)}) collective-permute-start(bf16[128,4096]{1,0:T(8,128)(2,1)S(1)} %get-tuple-element.24), channel_id=1, source_target_pairs={{2,0},{1,3},{0,1},{3,2},{6,4},{5,7},{4,5},{7,6},{10,8},{9,11},{8,9... | collective-permute-start | bytes 3145736 | tf_op jit(solution)/shard_map/ppermute | solution.py:342
  155.9 24.9 %collective-permute-start.15 = (bf16[128,4096]{1,0:T(8,128)(2,1)S(1)}, bf16[128,4096]{1,0:T(8,128)(2,1)S(1)}, u32[]{:S(2)}, u32[]{:S(2)}) collective-permute-start(bf16[128,4096]{1,0:T(8,128)(2,1)S(1)} %get-tuple-element.23), channel_id=1, source_target_pairs={{1,2},{2,1},{5,6},{6,5},{9,10},{10,9},{13,14},{14,13},{17,18},{18,... | collective-permute-start | bytes 3145736 | tf_op jit(solution)/shard_map/ppermute | solution.py:342
  178.4 2.4 %copy-start.8 = (bf16[128,16384]{1,0:T(8,128)(2,1)}, bf16[128,16384]{1,0:T(8,128)(2,1)S(1)}, u32[]{:S(2)}) copy-start(bf16[128,16384]{1,0:T(8,128)(2,1)S(1)} %select_dynamic-update-slice_fusion.1) | copy-start | bytes 12582916

commit v5 on v0

--- a/solution.py
+++ b/solution.py
@@ -263,7 +263,7 @@
             pltpu.VMEM((scales.shape[0], nodes), F32),
         ]
         + [pltpu.VMEM(param.shape, param.dtype) for param in params],
-        compiler_params=pltpu.CompilerParams(vmem_limit_bytes=40 << 20),
+        compiler_params=pltpu.CompilerParams(vmem_limit_bytes=40 << 20, fuse_transposed_lhs_in_matmul=True),
         cost_estimate=pl.CostEstimate(flops=nodes * 700000, bytes_accessed=nodes * 2048, transcendentals=nodes),
     )(*operands)
 

time: 183 us -> 184 us (level)
  no operation moved by 1% of the time
where the time goes in v5:
time: 184 us; the launch traced here: 182 us
  Pallas kernels  66.2 us (36%)
  waiting for transfers between devices  66 us (36%)
  starting transfers between devices  27.6 us (15%)
  local copies, waits for them, and re-layouts  12.7 us (7%)
  other arithmetic  8.1 us (4%)
    pallas_call x2, Pallas kernels, update(): pl.pallas_call(functools.partial(update_kernel, sources, step, start, seg...  66.2 us
    ppermute x14, waiting for transfers between devices, send(): return lax.ppermute(value, ('dom', 'feat'), perm)  57.2 us
    ppermute x14, starting transfers between devices, send(): return lax.ppermute(value, ('dom', 'feat'), perm)  18.9 us
    ppermute x2, waiting for transfers between devices, halo(): return lax.ppermute(value, ('dom', 'feat'), perm)  8.8 us
    ppermute x2, starting transfers between devices, halo(): return lax.ppermute(value, ('dom', 'feat'), perm)  8.65 us
    unnamed x33, local copies, waits for them, and re-layouts  6.01 us
    dynamic_slice x1, local copies, waits for them, and re-layouts, cut(): return lax.dynamic_slice_in_dim(array, at, size, 1)  4.16 us
  transfers between devices with their start and end apart: 16, of which 5 were waited for; matrix products, arithmetic and copies ran while one was open for 8% of the time, Pallas kernels for 36%

profile of v5, /device:TPU:1, one launch (start us, length us, event | category | flops | bytes accessed | tf_op | source)
XLA Modules:
  0.0 181.9 jit_solution(3799743221816933131)
XLA Ops:
  0.0 2.1 %collective-permute-start.1 = (bf16[128,8192]{1,0:T(8,128)(2,1)}, bf16[128,8192]{1,0:T(8,128)(2,1)}, u32[]{:S(2)}, u32[]{:S(2)}) collective-permute-start(bf16[128,8192]{1,0:T(8,128)(2,1)} %refs_12_.1), channel_id=1, source_target_pairs={{0,1},{1,0},{2,3},{3,2},{4,5},{5,4},{6,7},{7,6},{8,9},{9,8},{10,11... | collective-permute-start | bytes 6291464 | tf_op jit(solution)/shard_map/ppermute | solution.py:333
  2.1 4.1 %collective-permute-start.5 = (bf16[128,8192]{1,0:T(8,128)(2,1)}, bf16[128,8192]{1,0:T(8,128)(2,1)S(1)}, u32[]{:S(2)}, u32[]{:S(2)}) collective-permute-start(bf16[128,8192]{1,0:T(8,128)(2,1)} %refs_12_.1), channel_id=1, source_target_pairs={{2,4},{6,8},{10,12},{14,16},{18,20},{22,24},{26,28},{5,3},{9,7},{1... | collective-permute-start | bytes 6291464 | tf_op jit(solution)/shard_map/ppermute | solution.py:344
  6.9 1.0 multiply_add_fusion
  8.0 0.8 copy-done.6
  8.7 1.9 %fusion = f32[9,8192]{1,0:T(8,128)} fusion(s32[]{:T(128)S(6)} %select_n.168, f32[5,16384]{1,0:T(8,128)S(1)} %pad_convert_fusion, f32[4,16384]{1,0:T(4,128)} %param.18), kind=kLoop, calls=%fused_computation.8 | loop fusion | flops 73728 | bytes 884740 | tf_op jit(solution)/shard_map/concatenate | solution.py:381
  10.6 1.3 collective-permute-start
  12.0 0.9 constant_dynamic-slice_fusion.5
  12.9 0.1 copy.21
  13.0 0.1 copy.22
  13.1 0.1 stack.23.places
  13.2 0.8 broadcast_select_fusion.7
  14.1 0.7 pad_maximum_fusion.1
  14.8 0.9 constant_dynamic-slice_fusion.3
  15.7 0.0 copy-start.13
  15.8 4.2 %constant_dynamic-slice_fusion = (bf16[128,4096]{1,0:T(8,128)(2,1)}, bf16[128,4096]{1,0:T(8,128)(2,1)}, bf16[128,4096]{1,0:T(8,128)(2,1)S(1)}, bf16[128,4096]{1,0:T(8,128)(2,1)S(1)}) fusion(bf16[128,16384]{1,0:T(8,128)(2,1)} %refs_1_.3, s32[]{:T(128)S(6)} %select_n.193, s32[]{:T(128)S(6)} %select_n.192, s32[]{:T(128)S(6)} %select_n.168, s32[]{:T(128)S(6)} %select_n.171), kind=kLoop, calls=%fused_computation.32 | loop fusion | bytes 8388624 | tf_op jit(solution)/shard_map/dynamic_slice | solution.py:281
  20.0 0.1 broadcast_select_fusion.3
  20.1 27.7 %collective-permute-done.1.refs_16_ = bf16[128,8192]{1,0:T(8,128)(2,1)} collective-permute-done((bf16[128,8192]{1,0:T(8,128)(2,1)}, bf16[128,8192]{1,0:T(8,128)(2,1)}, u32[]{:S(2)}, u32[]{:S(2)}) %collective-permute-start.1) | collective-permute-done | bytes 2097184 | tf_op jit(solution)/shard_map/ppermute | solution.py:333
  47.7 4.6 %collective-permute-start.8 = (bf16[128,8192]{1,0:T(8,128)(2,1)}, bf16[128,8192]{1,0:T(8,128)(2,1)S(1)}, u32[]{:S(2)}, u32[]{:S(2)}) collective-permute-start(bf16[128,8192]{1,0:T(8,128)(2,1)} %collective-permute-done.1.refs_16_), channel_id=1, source_target_pairs={{2,4},{6,8},{10,12},{14,16},{18,20},{22,24},{26,28},{5,3},{9,7},{1... | collective-permute-start | bytes 6291464 | tf_op jit(solution)/shard_map/ppermute | solution.py:344
  52.4 1.3 fusion.2
  53.6 0.0 collective-permute-start.2
  53.7 1.9 %collective-permute-start.3 = (bf16[128,4096]{1,0:T(8,128)(2,1)S(1)}, bf16[128,4096]{1,0:T(8,128)(2,1)S(1)}, u32[]{:S(2)}, u32[]{:S(2)}) collective-permute-start(bf16[128,4096]{1,0:T(8,128)(2,1)S(1)} %get-tuple-element.16), channel_id=1, source_target_pairs={{1,2},{2,1},{5,6},{6,5},{9,10},{10,9},{13,14},{14,13},{17,18},{18,... | collective-permute-start | bytes 3145736 | tf_op jit(solution)/shard_map/ppermute | solution.py:333
  55.6 0.1 collective-permute-start.4
  55.7 0.5 collective-permute-start.7
  56.2 9.2 %collective-permute-done.2.refs_0_ = bf16[128,4096]{1,0:T(8,128)(2,1)S(1)} collective-permute-done((bf16[128,4096]{1,0:T(8,128)(2,1)S(1)}, bf16[128,4096]{1,0:T(8,128)(2,1)S(1)}, u32[]{:S(2)}, u32[]{:S(2)}) %collective-permute-start.2) | collective-permute-done | bytes 1048608 | tf_op jit(solution)/shard_map/ppermute | solution.py:333
  65.4 1.3 collective-permute-start.6
  66.7 8.8 %collective-permute-done.8.refs_18_ = bf16[128,8192]{1,0:T(8,128)(2,1)S(1)} collective-permute-done((bf16[128,8192]{1,0:T(8,128)(2,1)}, bf16[128,8192]{1,0:T(8,128)(2,1)S(1)}, u32[]{:S(2)}, u32[]{:S(2)}) %collective-permute-start.8) | collective-permute-done | bytes 2097184 | tf_op jit(solution)/shard_map/ppermute | solution.py:344
  75.5 1.3 collective-permute-start.9
  76.9 0.1 copy.23
  77.0 1.7 collective-permute-start.12
  78.7 3.1 %collective-permute-start.13 = (bf16[128,4096]{1,0:T(8,128)(2,1)}, bf16[128,4096]{1,0:T(8,128)(2,1)}, u32[]{:S(2)}, u32[]{:S(2)}) collective-permute-start(bf16[128,4096]{1,0:T(8,128)(2,1)} %get-tuple-element.21), channel_id=1, source_target_pairs={{1,2},{2,1},{5,6},{6,5},{9,10},{10,9},{13,14},{14,13},{17,18},{18,... | collective-permute-start | bytes 3145736 | tf_op jit(solution)/shard_map/ppermute | solution.py:333
  81.9 0.1 broadcast_in_dim.13.refs_9_
  82.0 0.1 broadcast_in_dim.14.refs_10_
  82.1 1.1 copy-done.10
  83.2 0.7 copy-done.11
  83.8 35.5 %shard_map.145 = (bf16[128,4096]{1,0:T(8,128)(2,1)}, bf16[128,4096]{1,0:T(8,128)(2,1)S(1)}, f32[49168,128]{1,0:T(8,128)}) custom-call(s32[5]{0:T(128)S(1)} %stack.23.places, s32[40960]{0:T(1024)S(1)} %pad_add_fusion.aux, bf16[128,4096]{1,0:T(8,128)(2,1)S(1)} %collective-permute-done.2.refs_0_, bf16[128,16384]{1,0:T(8,128)(2,1)} %refs_1_.3, ...), custom_call_target="tpu_custom_call" | custom-call | flops 2867200000 | bytes 8388608 | tf_op jit(solution)/shard_map/pallas_call | solution.py:245
  119.4 1.0 copy-done.2
  120.3 2.5 %collective-permute-start.11 = (bf16[128,4096]{1,0:T(8,128)(2,1)}, bf16[128,4096]{1,0:T(8,128)(2,1)S(1)}, u32[]{:S(2)}, u32[]{:S(2)}) collective-permute-start(bf16[128,4096]{1,0:T(8,128)(2,1)} %copy-done.2), channel_id=1, source_target_pairs={{1,2},{2,1},{5,6},{6,5},{9,10},{10,9},{13,14},{14,13},{17,18},{18,... | collective-permute-start | bytes 3145736 | tf_op jit(solution)/shard_map/ppermute | solution.py:333
  122.8 2.2 %copy-done = bf16[128,16384]{1,0:T(8,128)(2,1)S(1)} copy-done((bf16[128,16384]{1,0:T(8,128)(2,1)S(1)}, bf16[128,16384]{1,0:T(8,128)(2,1)}, u32[]{:S(2)}) %copy-start) | copy-done | bytes 4194328
  125.0 30.7 %shard_map.146 = (bf16[128,4096]{1,0:T(8,128)(2,1)S(1)}, bf16[128,4096]{1,0:T(8,128)(2,1)S(1)}) custom-call(s32[5]{0:T(128)S(1)} %stack.23.places, s32[40960]{0:T(1024)S(1)} %pad_add_fusion.aux, bf16[128,4096]{1,0:T(8,128)(2,1)} %collective-permute-done.12.refs_0_, bf16[128,16384]{1,0:T(8,128)(2,1)S(1)} %copy-done, ...), custom_call_target="tpu_custom_call" | custom-call | flops 2867200000 | bytes 8388608 | tf_op jit(solution)/shard_map/pallas_call | solution.py:245
  155.8 0.0 collective-permute-start.14
  155.8 3.2 %collective-permute-start.15 = (bf16[128,4096]{1,0:T(8,128)(2,1)S(1)}, bf16[128,4096]{1,0:T(8,128)(2,1)S(1)}, u32[]{:S(2)}, u32[]{:S(2)}) collective-permute-start(bf16[128,4096]{1,0:T(8,128)(2,1)S(1)} %get-tuple-element.23), channel_id=1, source_target_pairs={{1,2},{2,1},{5,6},{6,5},{9,10},{10,9},{13,14},{14,13},{17,18},{18,... | collective-permute-start | bytes 3145736 | tf_op jit(solution)/shard_map/ppermute | solution.py:333
  159.0 0.4 broadcast_in_dim.10
  159.4 0.3 select_dynamic-update-slice_fusion.3
  159.7 0.3 select_dynamic-update-slice_fusion.2
  160.1 17.9 %collective-permute-done.14 = bf16[128,4096]{1,0:T(8,128)(2,1)S(1)} collective-permute-done((bf16[128,4096]{1,0:T(8,128)(2,1)S(1)}, bf16[128,4096]{1,0:T(8,128)(2,1)S(1)}, u32[]{:S(2)}, u32[]{:S(2)}) %collective-permute-start.14) | collective-permute-done | bytes 1048608 | tf_op jit(solution)/shard_map/ppermute | solution.py:333
  178.0 0.3 select_dynamic-update-slice_fusion.1
  178.3 2.4 %collective-permute-done.15 = bf16[128,4096]{1,0:T(8,128)(2,1)S(1)} collective-permute-done((bf16[128,4096]{1,0:T(8,128)(2,1)S(1)}, bf16[128,4096]{1,0:T(8,128)(2,1)S(1)}, u32[]{:S(2)}, u32[]{:S(2)}) %collective-permute-start.15) | collective-permute-done | bytes 1048608 | tf_op jit(solution)/shard_map/ppermute | solution.py:333
  180.7 1.2 select_dynamic-update-slice_fusion
  (50 shorter events, 0.4 us)
Async XLA Ops:
  0.0 47.7 %collective-permute-start.1 = (bf16[128,8192]{1,0:T(8,128)(2,1)}, bf16[128,8192]{1,0:T(8,128)(2,1)}, u32[]{:S(2)}, u32[]{:S(2)}) collective-permute-start(bf16[128,8192]{1,0:T(8,128)(2,1)} %refs_12_.1), channel_id=1, source_target_pairs={{0,1},{1,0},{2,3},{3,2},{4,5},{5,4},{6,7},{7,6},{8,9},{9,8},{10,11... | collective-permute-start | bytes 6291464 | tf_op jit(solution)/shard_map/ppermute | solution.py:333
  2.1 53.6 %collective-permute-start.5 = (bf16[128,8192]{1,0:T(8,128)(2,1)}, bf16[128,8192]{1,0:T(8,128)(2,1)S(1)}, u32[]{:S(2)}, u32[]{:S(2)}) collective-permute-start(bf16[128,8192]{1,0:T(8,128)(2,1)} %refs_12_.1), channel_id=1, source_target_pairs={{2,4},{6,8},{10,12},{14,16},{18,20},{22,24},{26,28},{5,3},{9,7},{1... | collective-permute-start | bytes 6291464 | tf_op jit(solution)/shard_map/ppermute | solution.py:344
  7.9 0.8 copy-start.6
  10.6 41.7 %collective-permute-start = (f32[9,8192]{1,0:T(8,128)}, f32[9,8192]{1,0:T(8,128)}, u32[]{:S(2)}, u32[]{:S(2)}) collective-permute-start(f32[9,8192]{1,0:T(8,128)} %fusion), channel_id=1, source_target_pairs={{0,2},{3,1},{4,6},{7,5},{8,10},{11,9},{12,14},{15,13},{16,18},{19,... | collective-permute-start | bytes 884744 | tf_op jit(solution)/shard_map/ppermute | solution.py:333
  15.7 4.2 %copy-start.13 = (bf16[256,256]{1,0:T(8,128)(2,1)S(1)}, bf16[256,256]{1,0:T(8,128)(2,1)}, u32[]{:S(2)}) copy-start(bf16[256,256]{1,0:T(8,128)(2,1)} %param.23) | copy-start | bytes 393220
  15.7 4.2 %copy-start.14 = (bf16[256,256]{1,0:T(8,128)(2,1)S(1)}, bf16[256,256]{1,0:T(8,128)(2,1)}, u32[]{:S(2)}) copy-start(bf16[256,256]{1,0:T(8,128)(2,1)} %param.20) | copy-start | bytes 393220
  15.8 36.6 %copy-start.7 = (f32[5,16384]{1,0:T(8,128)S(1)}, f32[5,16384]{1,0:T(8,128)}, u32[]{:S(2)}) copy-start(f32[5,16384]{1,0:T(8,128)} %copy-done.6) | copy-start | bytes 983044
  15.8 36.6 %copy-start.12 = (f32[4,16384]{1,0:T(4,128)S(1)}, f32[4,16384]{1,0:T(4,128)}, u32[]{:S(2)}) copy-start(f32[4,16384]{1,0:T(4,128)} %param.18) | copy-start | bytes 786436
  15.8 39.8 %copy-start.1 = (bf16[128,8192]{1,0:T(8,128)(2,1)S(1)}, bf16[128,8192]{1,0:T(8,128)(2,1)}, u32[]{:S(2)}) copy-start(bf16[128,8192]{1,0:T(8,128)(2,1)} %refs_12_.1) | copy-start | bytes 6291460
  19.9 63.9 %copy-start.4 = (bf16[256,256]{1,0:T(8,128)(2,1)S(1)}, bf16[256,256]{1,0:T(8,128)(2,1)}, u32[]{:S(2)}) copy-start(bf16[256,256]{1,0:T(8,128)(2,1)} %refs_5_.3) | copy-start | bytes 393220
  19.9 63.9 %copy-start.5 = (bf16[256,256]{1,0:T(8,128)(2,1)S(1)}, bf16[256,256]{1,0:T(8,128)(2,1)}, u32[]{:S(2)}) copy-start(bf16[256,256]{1,0:T(8,128)(2,1)} %refs_6_.3) | copy-start | bytes 393220
  47.7 27.7 %collective-permute-start.8 = (bf16[128,8192]{1,0:T(8,128)(2,1)}, bf16[128,8192]{1,0:T(8,128)(2,1)S(1)}, u32[]{:S(2)}, u32[]{:S(2)}) collective-permute-start(bf16[128,8192]{1,0:T(8,128)(2,1)} %collective-permute-done.1.refs_16_), channel_id=1, source_target_pairs={{2,4},{6,8},{10,12},{14,16},{18,20},{22,24},{26,28},{5,3},{9,7},{1... | collective-permute-start | bytes 6291464 | tf_op jit(solution)/shard_map/ppermute | solution.py:344
  53.6 11.8 %collective-permute-start.2 = (bf16[128,4096]{1,0:T(8,128)(2,1)S(1)}, bf16[128,4096]{1,0:T(8,128)(2,1)S(1)}, u32[]{:S(2)}, u32[]{:S(2)}) collective-permute-start(bf16[128,4096]{1,0:T(8,128)(2,1)S(1)} %get-tuple-element.15), channel_id=1, source_target_pairs={{0,2},{3,1},{1,0},{2,3},{4,6},{7,5},{5,4},{6,7},{8,10},{11,9},{9,8... | collective-permute-start | bytes 3145736 | tf_op jit(solution)/shard_map/ppermute | solution.py:333
  53.7 23.3 %collective-permute-start.3 = (bf16[128,4096]{1,0:T(8,128)(2,1)S(1)}, bf16[128,4096]{1,0:T(8,128)(2,1)S(1)}, u32[]{:S(2)}, u32[]{:S(2)}) collective-permute-start(bf16[128,4096]{1,0:T(8,128)(2,1)S(1)} %get-tuple-element.16), channel_id=1, source_target_pairs={{1,2},{2,1},{5,6},{6,5},{9,10},{10,9},{13,14},{14,13},{17,18},{18,... | collective-permute-start | bytes 3145736 | tf_op jit(solution)/shard_map/ppermute | solution.py:333
  55.6 23.1 %collective-permute-start.4 = (bf16[128,8192]{1,0:T(8,128)(2,1)S(1)}, bf16[128,8192]{1,0:T(8,128)(2,1)S(1)}, u32[]{:S(2)}, u32[]{:S(2)}) collective-permute-start(bf16[128,8192]{1,0:T(8,128)(2,1)S(1)} %copy-done.1), channel_id=1, source_target_pairs={{0,2},{1,3},{2,0},{3,1},{4,6},{5,7},{6,4},{7,5},{8,10},{9,11},{10,... | collective-permute-start | bytes 6291464 | tf_op jit(solution)/shard_map/ppermute | solution.py:333
  55.7 26.1 %collective-permute-start.7 = (bf16[128,8192]{1,0:T(8,128)(2,1)}, bf16[128,8192]{1,0:T(8,128)(2,1)S(1)}, u32[]{:S(2)}, u32[]{:S(2)}) collective-permute-start(bf16[128,8192]{1,0:T(8,128)(2,1)} %collective-permute-done.1.refs_16_), channel_id=1, source_target_pairs={{0,2},{1,3},{2,0},{3,1},{4,6},{5,7},{6,4},{7,5},{8,10},{9,11},{10,... | collective-permute-start | bytes 6291464 | tf_op jit(solution)/shard_map/ppermute | solution.py:333
  65.4 16.5 %collective-permute-start.6 = (bf16[128,8192]{1,0:T(8,128)(2,1)S(1)}, bf16[128,8192]{1,0:T(8,128)(2,1)S(1)}, u32[]{:S(2)}, u32[]{:S(2)}) collective-permute-start(bf16[128,8192]{1,0:T(8,128)(2,1)S(1)} %collective-permute-done.5.refs_14_), channel_id=1, source_target_pairs={{0,2},{3,1},{4,6},{7,5},{8,10},{11,9},{12,14},{15,13},{16,18},{19,... | collective-permute-start | bytes 6291464 | tf_op jit(solution)/shard_map/ppermute | solution.py:333
  75.5 6.6 %copy-start.9 = (bf16[128,8192]{1,0:T(8,128)(2,1)}, bf16[128,8192]{1,0:T(8,128)(2,1)S(1)}, u32[]{:S(2)}) copy-start(bf16[128,8192]{1,0:T(8,128)(2,1)S(1)} %collective-permute-done.8.refs_18_) | copy-start | bytes 6291460
  75.5 6.4 %collective-permute-start.9 = (bf16[128,8192]{1,0:T(8,128)(2,1)S(1)}, bf16[128,8192]{1,0:T(8,128)(2,1)S(1)}, u32[]{:S(2)}, u32[]{:S(2)}) collective-permute-start(bf16[128,8192]{1,0:T(8,128)(2,1)S(1)} %collective-permute-done.8.refs_18_), channel_id=1, source_target_pairs={{0,2},{3,1},{4,6},{7,5},{8,10},{11,9},{12,14},{15,13},{16,18},{19,... | collective-permute-start | bytes 6291464 | tf_op jit(solution)/shard_map/ppermute | solution.py:333
  77.0 45.8 %collective-permute-start.12 = (bf16[128,4096]{1,0:T(8,128)(2,1)}, bf16[128,4096]{1,0:T(8,128)(2,1)}, u32[]{:S(2)}, u32[]{:S(2)}) collective-permute-start(bf16[128,4096]{1,0:T(8,128)(2,1)} %get-tuple-element.20), channel_id=1, source_target_pairs={{0,2},{3,1},{1,0},{2,3},{4,6},{7,5},{5,4},{6,7},{8,10},{11,9},{9,8... | collective-permute-start | bytes 3145736 | tf_op jit(solution)/shard_map/ppermute | solution.py:333
  78.7 44.1 %collective-permute-start.13 = (bf16[128,4096]{1,0:T(8,128)(2,1)}, bf16[128,4096]{1,0:T(8,128)(2,1)}, u32[]{:S(2)}, u32[]{:S(2)}) collective-permute-start(bf16[128,4096]{1,0:T(8,128)(2,1)} %get-tuple-element.21), channel_id=1, source_target_pairs={{1,2},{2,1},{5,6},{6,5},{9,10},{10,9},{13,14},{14,13},{17,18},{18,... | collective-permute-start | bytes 3145736 | tf_op jit(solution)/shard_map/ppermute | solution.py:333
  81.8 1.3 copy-start.10
  81.9 2.0 %copy-start.11 = (bf16[128,8192]{1,0:T(8,128)(2,1)}, bf16[128,8192]{1,0:T(8,128)(2,1)S(1)}, u32[]{:S(2)}) copy-start(bf16[128,8192]{1,0:T(8,128)(2,1)S(1)} %collective-permute-done.9.refs_19_) | copy-start | bytes 6291460
  119.3 1.0 copy-start.2
  120.3 38.7 %collective-permute-start.10 = (bf16[128,4096]{1,0:T(8,128)(2,1)}, bf16[128,4096]{1,0:T(8,128)(2,1)S(1)}, u32[]{:S(2)}, u32[]{:S(2)}) collective-permute-start(bf16[128,4096]{1,0:T(8,128)(2,1)} %get-tuple-element.19), channel_id=1, source_target_pairs={{2,0},{1,3},{0,1},{3,2},{6,4},{5,7},{4,5},{7,6},{10,8},{9,11},{8,9... | collective-permute-start | bytes 3145736 | tf_op jit(solution)/shard_map/ppermute | solution.py:333
  120.3 39.4 %collective-permute-start.11 = (bf16[128,4096]{1,0:T(8,128)(2,1)}, bf16[128,4096]{1,0:T(8,128)(2,1)S(1)}, u32[]{:S(2)}, u32[]{:S(2)}) collective-permute-start(bf16[128,4096]{1,0:T(8,128)(2,1)} %copy-done.2), channel_id=1, source_target_pairs={{1,2},{2,1},{5,6},{6,5},{9,10},{10,9},{13,14},{14,13},{17,18},{18,... | collective-permute-start | bytes 3145736 | tf_op jit(solution)/shard_map/ppermute | solution.py:333
  122.8 2.2 %copy-start = (bf16[128,16384]{1,0:T(8,128)(2,1)S(1)}, bf16[128,16384]{1,0:T(8,128)(2,1)}, u32[]{:S(2)}) copy-start(bf16[128,16384]{1,0:T(8,128)(2,1)} %refs_1_.3) | copy-start | bytes 12582916
  155.8 3.7 %copy-start.3 = (bf16[128,4096]{1,0:T(8,128)(2,1)S(1)}, bf16[128,4096]{1,0:T(8,128)(2,1)}, u32[]{:S(2)}) copy-start(bf16[128,4096]{1,0:T(8,128)(2,1)} %copy-done.2) | copy-start | bytes 3145732
  155.8 22.2 %collective-permute-start.14 = (bf16[128,4096]{1,0:T(8,128)(2,1)S(1)}, bf16[128,4096]{1,0:T(8,128)(2,1)S(1)}, u32[]{:S(2)}, u32[]{:S(2)}) collective-permute-start(bf16[128,4096]{1,0:T(8,128)(2,1)S(1)} %get-tuple-element.24), channel_id=1, source_target_pairs={{2,0},{1,3},{0,1},{3,2},{6,4},{5,7},{4,5},{7,6},{10,8},{9,11},{8,9... | collective-permute-start | bytes 3145736 | tf_op jit(solution)/shard_map/ppermute | solution.py:333
  155.8 24.9 %collective-permute-start.15 = (bf16[128,4096]{1,0:T(8,128)(2,1)S(1)}, bf16[128,4096]{1,0:T(8,128)(2,1)S(1)}, u32[]{:S(2)}, u32[]{:S(2)}) collective-permute-start(bf16[128,4096]{1,0:T(8,128)(2,1)S(1)} %get-tuple-element.23), channel_id=1, source_target_pairs={{1,2},{2,1},{5,6},{6,5},{9,10},{10,9},{13,14},{14,13},{17,18},{18,... | collective-permute-start | bytes 3145736 | tf_op jit(solution)/shard_map/ppermute | solution.py:333
  178.3 2.4 %copy-start.8 = (bf16[128,16384]{1,0:T(8,128)(2,1)}, bf16[128,16384]{1,0:T(8,128)(2,1)S(1)}, u32[]{:S(2)}) copy-start(bf16[128,16384]{1,0:T(8,128)(2,1)S(1)} %select_dynamic-update-slice_fusion.1) | copy-start | bytes 12582916
